TPU v7x, 512 devices: a whole 4x4x16 slice. The times are simulated.
512 devices in a mesh: blk: 32 (over x_lo, z), uly: 16 (over x_hi, y, core).
Axes of the slice: x: 4 (x_hi: 2, x_lo: 2; x = x_hi * 2 + x_lo), y: 4, z: 16, core: 2. Of those that a mesh axis runs over, the one named last changes fastest.
Arguments:
- query_rows: bfloat16 [4096, 4096], P('blk', 'uly'), may hold values from -6 to 6
- key_rows: bfloat16 [4096, 4096], P('blk', 'uly'), may hold values from -6 to 6
- value_rows: bfloat16 [4096, 4096], P('blk', 'uly'), may hold values from -6 to 6
- output_rows: bfloat16 [4096, 4096], P('blk', 'uly'), may hold values from -1.5 to 1.5
- grad_output: bfloat16 [4096, 4096], P(('blk', 'uly')), may hold values from -96 to 96
- log_norm: float32 [4096, 32], P('blk', 'uly'), may hold values from 7.2 to 9.2
Outputs:
- grad_query: bfloat16 [4096, 4096], P('blk', 'uly')
- grad_key: bfloat16 [4096, 4096], P('blk', 'uly')
- grad_value: bfloat16 [4096, 4096], P('blk', 'uly')
All inputs are finite; a program needn't handle non-finite values.
Results may differ from a plain program's by a relative error of at most 0.0056.
Values may be sent and summed in bfloat16 or wider, within the bound.
No kernel may reach another device: no remote copies, remote signals or barrier semaphores. Data moves between devices by JAX's collectives and lax.ppermute only.
A program may use at most 64 MiB of HBM per device.

v0:
```python
import math

import jax
import jax.numpy as jnp
from jax import lax
from jax.sharding import PartitionSpec as P


def shifted(value, axis, steps):
    count = lax.axis_size(axis)
    pairs = [(source, (source + steps) % count) for source in range(count)]
    return lax.ppermute(value, axis, pairs)


def split_heads(rows, count):
    return rows.reshape(rows.shape[0], count, rows.shape[1] // count)


def join_heads(rows):
    return rows.reshape(rows.shape[0], rows.shape[1] * rows.shape[2])


def pair_grads(query_blk, dout_blk, lnorm_blk, delta_blk, key_blk, value_blk):
    count = lnorm_blk.shape[1]
    query_h = split_heads(query_blk, count)
    dout_h = split_heads(dout_blk, count)
    key_h = split_heads(key_blk, count)
    value_h = split_heads(value_blk, count)
    factor = 1.0 / math.sqrt(query_h.shape[2])
    scores = jnp.einsum("qhd,khd->hqk", query_h, key_h, preferred_element_type=jnp.float32) * factor
    probs = jnp.exp(scores - lnorm_blk.T[:, :, None])
    probs_low = probs.astype(jnp.bfloat16)
    dprobs = jnp.einsum("qhd,khd->hqk", dout_h, value_h, preferred_element_type=jnp.float32)
    dscore = (probs * (dprobs - delta_blk.T[:, :, None])).astype(jnp.bfloat16)
    grad_q = jnp.einsum("hqk,khd->qhd", dscore, key_h, preferred_element_type=jnp.float32) * factor
    grad_k = (
        jnp.einsum("hqk,qhd->khd", dscore, query_h, preferred_element_type=jnp.float32) * factor
    )
    grad_v = jnp.einsum("hqk,qhd->khd", probs_low, dout_h, preferred_element_type=jnp.float32)
    return (join_heads(grad_q), join_heads(grad_k), join_heads(grad_v))


def move_keys(key_blk, value_blk):
    return shifted((key_blk, value_blk), "blk", 1)


def move_key_grads(grad_k, grad_v):
    return shifted((grad_k, grad_v), "blk", 1)


def body(query_rows, key_rows, value_rows, output_rows, grad_output, log_norm):
    tokens = query_rows.shape[0]
    head_count = log_norm.shape[1]
    width = query_rows.shape[1]
    dout_x = lax.all_to_all(grad_output, "uly", split_axis=1, concat_axis=0, tiled=True)
    product = dout_x.astype(jnp.float32) * output_rows.astype(jnp.float32)
    delta_x = jnp.sum(product.reshape(tokens, head_count, width // head_count), axis=2)
    blocks = lax.axis_size("blk")
    own = pair_grads(query_rows, dout_x, log_norm, delta_x, key_rows, value_rows)
    key_now, value_now = move_keys(key_rows, value_rows)
    first = pair_grads(query_rows, dout_x, log_norm, delta_x, key_now, value_now)

    def key_step(step, carry):
        key_cur, value_cur, acc_k, acc_v, total_q = carry
        key_cur, value_cur = move_keys(key_cur, value_cur)
        acc_k, acc_v = move_key_grads(acc_k, acc_v)
        grads = pair_grads(query_rows, dout_x, log_norm, delta_x, key_cur, value_cur)
        return (key_cur, value_cur, acc_k + grads[1], acc_v + grads[2], total_q + grads[0])

    start = (key_now, value_now, first[1], first[2], own[0] + first[0])
    key_cur, value_cur, acc_k, acc_v, total_q = lax.fori_loop(2, blocks, key_step, start)
    acc_k, acc_v = move_key_grads(acc_k, acc_v)
    total_k = own[1] + acc_k
    total_v = own[2] + acc_v
    return (
        total_q.astype(jnp.bfloat16),
        total_k.astype(jnp.bfloat16),
        total_v.astype(jnp.bfloat16),
    )


def solution(mesh):
    placed = (
        P("blk", "uly"),
        P("blk", "uly"),
        P("blk", "uly"),
        P("blk", "uly"),
        P(("blk", "uly"), None),
        P("blk", "uly"),
    )
    return jax.shard_map(
        body,
        mesh=mesh,
        in_specs=placed,
        out_specs=(P("blk", "uly"), P("blk", "uly"), P("blk", "uly")),
        check_vma=False,
    )
```

profile of v0, /device:TPU:6, one launch (start us, length us, event | category | flops | bytes accessed | tf_op | source)
XLA Modules:
  0.0 550.4 jit_solution(12937468087183390363)
XLA Ops:
  0.6 7.6 %all-to-all-start = ((bf16[8,16,256]{2,0,1:T(8,128)(2,1)}), bf16[8,16,256]{2,0,1:T(8,128)(2,1)S(1)}, u32[]{:S(2)}, u32[]{:S(2)}) async-start(bf16[8,16,256]{2,0,1:T(8,128)(2,1)} %bitcast.151), calls=%async_computation | async-start | bytes 131072 | tf_op jit(solution)/shard_map/all_to_all | solution.py:55
  8.4 4.0 collective-permute-start.5
  12.5 3.8 collective-permute-start.4
  19.4 5.2 collective-permute-done.4
  25.8 511.9 %while.18 = (s32[]{:T(128)}, bf16[128,256]{0,1:T(8,128)(2,1)S(1)}, bf16[128,256]{0,1:T(8,128)(2,1)S(1)}, f32[128,256]{0,1:T(8,128)S(1)}, f32[128,256]{0,1:T(8,12...) while((s32[]{:T(128)}, bf16[128,256]{0,1:T(8,128)(2,1)S(1)}, ...), condition=%wide.region_2.0_spmd, body=%wide.region_1.0_spmd.sunk | while | flops 42303488 | bytes 4983053 | solution.py:71
  29.7 3.6 collective-permute-start.3
  33.3 4.2 collective-permute-start.2
  38.9 3.4 collective-permute-done.2
  44.5 4.1 collective-permute-start.1
  48.6 4.4 collective-permute-start.3
  52.9 4.2 collective-permute-start.2
  69.2 3.7 collective-permute-start.2
  82.7 3.6 collective-permute-start.3
  91.7 3.6 collective-permute-done.2
  101.2 3.4 collective-permute-start.2
  116.9 4.8 collective-permute-start.2
  132.4 4.9 collective-permute-start.3
  137.3 5.6 %collective-permute-start.2 = (f32[128,256]{0,1:T(8,128)S(1)}, f32[128,256]{0,1:T(8,128)S(1)}, u32[]{:S(2)}, u32[]{:S(2)}) collective-permute-start(f32[128,256]{0,1:T(8,128)S(1)} %get-tuple-element.191), channel_id=1, source_target_pairs={{0,16},{16,32},{32,48},{48,64},{64,80},{80,96},{96,112},{112,128},... | collective-permute-start | bytes 393224 | tf_op jit(solution)/shard_map/while/body/eval_jaxpr/ppermute | solution.py:12
  144.2 3.4 collective-permute-done.2
  171.5 5.6 %collective-permute-start.2 = (f32[128,256]{0,1:T(8,128)S(1)}, f32[128,256]{0,1:T(8,128)S(1)}, u32[]{:S(2)}, u32[]{:S(2)}) collective-permute-start(f32[128,256]{0,1:T(8,128)S(1)} %get-tuple-element.191), channel_id=1, source_target_pairs={{0,16},{16,32},{32,48},{48,64},{64,80},{80,96},{96,112},{112,128},... | collective-permute-start | bytes 393224 | tf_op jit(solution)/shard_map/while/body/eval_jaxpr/ppermute | solution.py:12
  188.9 3.4 collective-permute-start.2
  217.9 3.7 collective-permute-start.3
  221.7 5.6 %collective-permute-start.2 = (f32[128,256]{0,1:T(8,128)S(1)}, f32[128,256]{0,1:T(8,128)S(1)}, u32[]{:S(2)}, u32[]{:S(2)}) collective-permute-start(f32[128,256]{0,1:T(8,128)S(1)} %get-tuple-element.191), channel_id=1, source_target_pairs={{0,16},{16,32},{32,48},{48,64},{64,80},{80,96},{96,112},{112,128},... | collective-permute-start | bytes 393224 | tf_op jit(solution)/shard_map/while/body/eval_jaxpr/ppermute | solution.py:12
  230.7 3.4 collective-permute-start
  234.1 3.8 collective-permute-start.1
  240.4 3.7 collective-permute-start.2
  256.4 4.0 collective-permute-start.2
  273.1 4.4 collective-permute-start.2
  289.2 4.3 collective-permute-start.2
  305.0 4.7 collective-permute-start.2
  316.8 4.4 collective-permute-start.1
  323.8 5.3 collective-permute-start.2
  342.9 4.0 collective-permute-start.2
  358.8 4.2 collective-permute-start.2
  375.3 3.6 collective-permute-start.2
  391.1 4.0 collective-permute-start.2
  404.5 3.4 collective-permute-start.3
  407.9 5.5 collective-permute-start.2
  416.9 3.4 collective-permute-start
  423.2 3.5 collective-permute-start.3
  426.7 5.6 %collective-permute-start.2 = (f32[128,256]{0,1:T(8,128)S(1)}, f32[128,256]{0,1:T(8,128)S(1)}, u32[]{:S(2)}, u32[]{:S(2)}) collective-permute-start(f32[128,256]{0,1:T(8,128)S(1)} %get-tuple-element.191), channel_id=1, source_target_pairs={{0,16},{16,32},{32,48},{48,64},{64,80},{80,96},{96,112},{112,128},... | collective-permute-start | bytes 393224 | tf_op jit(solution)/shard_map/while/body/eval_jaxpr/ppermute | solution.py:12
  443.8 4.7 collective-permute-start.2
  460.5 5.1 collective-permute-start.2
  467.0 3.6 collective-permute-done.2
  494.3 3.8 collective-permute-start.2
  511.6 5.0 collective-permute-start.2
  528.7 3.7 collective-permute-start.2
  543.0 3.7 collective-permute-done.6
  (603 shorter events, 345.0 us)
Async XLA Ops:
  0.6 16.6 %all-to-all-start = ((bf16[8,16,256]{2,0,1:T(8,128)(2,1)}), bf16[8,16,256]{2,0,1:T(8,128)(2,1)S(1)}, u32[]{:S(2)}, u32[]{:S(2)}) async-start(bf16[8,16,256]{2,0,1:T(8,128)(2,1)} %bitcast.151), calls=%async_computation | async-start | bytes 131072 | tf_op jit(solution)/shard_map/all_to_all | solution.py:55
  8.4 16.6 %collective-permute-start.5 = (bf16[128,256]{0,1:T(8,128)(2,1)S(1)}, bf16[128,256]{0,1:T(8,128)(2,1)S(1)}, u32[]{:S(2)}, u32[]{:S(2)}) collective-permute-start(bf16[128,256]{0,1:T(8,128)(2,1)S(1)} %copy.78), channel_id=1, source_target_pairs={{0,16},{16,32},{32,48},{48,64},{64,80},{80,96},{96,112},{112,128},... | collective-permute-start | bytes 196616 | tf_op jit(solution)/shard_map/ppermute | solution.py:12
  12.5 12.2 %collective-permute-start.4 = (bf16[128,256]{0,1:T(8,128)(2,1)S(1)}, bf16[128,256]{0,1:T(8,128)(2,1)S(1)}, u32[]{:S(2)}, u32[]{:S(2)}) collective-permute-start(bf16[128,256]{0,1:T(8,128)(2,1)S(1)} %copy.77), channel_id=1, source_target_pairs={{0,16},{16,32},{32,48},{48,64},{64,80},{80,96},{96,112},{112,128},... | collective-permute-start | bytes 196616 | tf_op jit(solution)/shard_map/ppermute | solution.py:12
  25.8 11.8 %collective-permute-start = (bf16[128,256]{0,1:T(8,128)(2,1)S(1)}, bf16[128,256]{0,1:T(8,128)(2,1)S(1)}, u32[]{:S(2)}, u32[]{:S(2)}) collective-permute-start(bf16[128,256]{0,1:T(8,128)(2,1)S(1)} %get-tuple-element.189), channel_id=1, source_target_pairs={{0,16},{16,32},{32,48},{48,64},{64,80},{80,96},{96,112},{112,128},... | collective-permute-start | bytes 196616 | tf_op jit(solution)/shard_map/while/body/eval_jaxpr/ppermute | solution.py:12
  42.3 14.9 %collective-permute-start = (bf16[128,256]{0,1:T(8,128)(2,1)S(1)}, bf16[128,256]{0,1:T(8,128)(2,1)S(1)}, u32[]{:S(2)}, u32[]{:S(2)}) collective-permute-start(bf16[128,256]{0,1:T(8,128)(2,1)S(1)} %get-tuple-element.189), channel_id=1, source_target_pairs={{0,16},{16,32},{32,48},{48,64},{64,80},{80,96},{96,112},{112,128},... | collective-permute-start | bytes 196616 | tf_op jit(solution)/shard_map/while/body/eval_jaxpr/ppermute | solution.py:12
  44.5 13.0 %collective-permute-start.1 = (bf16[128,256]{0,1:T(8,128)(2,1)S(1)}, bf16[128,256]{0,1:T(8,128)(2,1)S(1)}, u32[]{:S(2)}, u32[]{:S(2)}) collective-permute-start(bf16[128,256]{0,1:T(8,128)(2,1)S(1)} %get-tuple-element.190), channel_id=1, source_target_pairs={{0,16},{16,32},{32,48},{48,64},{64,80},{80,96},{96,112},{112,128},... | collective-permute-start | bytes 196616 | tf_op jit(solution)/shard_map/while/body/eval_jaxpr/ppermute | solution.py:12
  48.6 10.2 %collective-permute-start.3 = (f32[128,256]{0,1:T(8,128)S(1)}, f32[128,256]{0,1:T(8,128)S(1)}, u32[]{:S(2)}, u32[]{:S(2)}) collective-permute-start(f32[128,256]{0,1:T(8,128)S(1)} %get-tuple-element.192), channel_id=1, source_target_pairs={{0,16},{16,32},{32,48},{48,64},{64,80},{80,96},{96,112},{112,128},... | collective-permute-start | bytes 393224 | tf_op jit(solution)/shard_map/while/body/eval_jaxpr/ppermute | solution.py:12
  62.0 11.0 %collective-permute-start = (bf16[128,256]{0,1:T(8,128)(2,1)S(1)}, bf16[128,256]{0,1:T(8,128)(2,1)S(1)}, u32[]{:S(2)}, u32[]{:S(2)}) collective-permute-start(bf16[128,256]{0,1:T(8,128)(2,1)S(1)} %get-tuple-element.189), channel_id=1, source_target_pairs={{0,16},{16,32},{32,48},{48,64},{64,80},{80,96},{96,112},{112,128},... | collective-permute-start | bytes 196616 | tf_op jit(solution)/shard_map/while/body/eval_jaxpr/ppermute | solution.py:12
  78.2 10.8 %collective-permute-start = (bf16[128,256]{0,1:T(8,128)(2,1)S(1)}, bf16[128,256]{0,1:T(8,128)(2,1)S(1)}, u32[]{:S(2)}, u32[]{:S(2)}) collective-permute-start(bf16[128,256]{0,1:T(8,128)(2,1)S(1)} %get-tuple-element.189), channel_id=1, source_target_pairs={{0,16},{16,32},{32,48},{48,64},{64,80},{80,96},{96,112},{112,128},... | collective-permute-start | bytes 196616 | tf_op jit(solution)/shard_map/while/body/eval_jaxpr/ppermute | solution.py:12
  110.2 11.5 %collective-permute-start = (bf16[128,256]{0,1:T(8,128)(2,1)S(1)}, bf16[128,256]{0,1:T(8,128)(2,1)S(1)}, u32[]{:S(2)}, u32[]{:S(2)}) collective-permute-start(bf16[128,256]{0,1:T(8,128)(2,1)S(1)} %get-tuple-element.189), channel_id=1, source_target_pairs={{0,16},{16,32},{32,48},{48,64},{64,80},{80,96},{96,112},{112,128},... | collective-permute-start | bytes 196616 | tf_op jit(solution)/shard_map/while/body/eval_jaxpr/ppermute | solution.py:12
  126.0 16.9 %collective-permute-start = (bf16[128,256]{0,1:T(8,128)(2,1)S(1)}, bf16[128,256]{0,1:T(8,128)(2,1)S(1)}, u32[]{:S(2)}, u32[]{:S(2)}) collective-permute-start(bf16[128,256]{0,1:T(8,128)(2,1)S(1)} %get-tuple-element.189), channel_id=1, source_target_pairs={{0,16},{16,32},{32,48},{48,64},{64,80},{80,96},{96,112},{112,128},... | collective-permute-start | bytes 196616 | tf_op jit(solution)/shard_map/while/body/eval_jaxpr/ppermute | solution.py:12
  129.3 13.8 %collective-permute-start.1 = (bf16[128,256]{0,1:T(8,128)(2,1)S(1)}, bf16[128,256]{0,1:T(8,128)(2,1)S(1)}, u32[]{:S(2)}, u32[]{:S(2)}) collective-permute-start(bf16[128,256]{0,1:T(8,128)(2,1)S(1)} %get-tuple-element.190), channel_id=1, source_target_pairs={{0,16},{16,32},{32,48},{48,64},{64,80},{80,96},{96,112},{112,128},... | collective-permute-start | bytes 196616 | tf_op jit(solution)/shard_map/while/body/eval_jaxpr/ppermute | solution.py:12
  132.4 11.8 %collective-permute-start.3 = (f32[128,256]{0,1:T(8,128)S(1)}, f32[128,256]{0,1:T(8,128)S(1)}, u32[]{:S(2)}, u32[]{:S(2)}) collective-permute-start(f32[128,256]{0,1:T(8,128)S(1)} %get-tuple-element.192), channel_id=1, source_target_pairs={{0,16},{16,32},{32,48},{48,64},{64,80},{80,96},{96,112},{112,128},... | collective-permute-start | bytes 393224 | tf_op jit(solution)/shard_map/while/body/eval_jaxpr/ppermute | solution.py:12
  137.3 10.3 %collective-permute-start.2 = (f32[128,256]{0,1:T(8,128)S(1)}, f32[128,256]{0,1:T(8,128)S(1)}, u32[]{:S(2)}, u32[]{:S(2)}) collective-permute-start(f32[128,256]{0,1:T(8,128)S(1)} %get-tuple-element.191), channel_id=1, source_target_pairs={{0,16},{16,32},{32,48},{48,64},{64,80},{80,96},{96,112},{112,128},... | collective-permute-start | bytes 393224 | tf_op jit(solution)/shard_map/while/body/eval_jaxpr/ppermute | solution.py:12
  147.6 10.8 %collective-permute-start = (bf16[128,256]{0,1:T(8,128)(2,1)S(1)}, bf16[128,256]{0,1:T(8,128)(2,1)S(1)}, u32[]{:S(2)}, u32[]{:S(2)}) collective-permute-start(bf16[128,256]{0,1:T(8,128)(2,1)S(1)} %get-tuple-element.189), channel_id=1, source_target_pairs={{0,16},{16,32},{32,48},{48,64},{64,80},{80,96},{96,112},{112,128},... | collective-permute-start | bytes 196616 | tf_op jit(solution)/shard_map/while/body/eval_jaxpr/ppermute | solution.py:12
  165.4 11.6 %collective-permute-start = (bf16[128,256]{0,1:T(8,128)(2,1)S(1)}, bf16[128,256]{0,1:T(8,128)(2,1)S(1)}, u32[]{:S(2)}, u32[]{:S(2)}) collective-permute-start(bf16[128,256]{0,1:T(8,128)(2,1)S(1)} %get-tuple-element.189), channel_id=1, source_target_pairs={{0,16},{16,32},{32,48},{48,64},{64,80},{80,96},{96,112},{112,128},... | collective-permute-start | bytes 196616 | tf_op jit(solution)/shard_map/while/body/eval_jaxpr/ppermute | solution.py:12
  169.3 10.3 %collective-permute-start.3 = (f32[128,256]{0,1:T(8,128)S(1)}, f32[128,256]{0,1:T(8,128)S(1)}, u32[]{:S(2)}, u32[]{:S(2)}) collective-permute-start(f32[128,256]{0,1:T(8,128)S(1)} %get-tuple-element.192), channel_id=1, source_target_pairs={{0,16},{16,32},{32,48},{48,64},{64,80},{80,96},{96,112},{112,128},... | collective-permute-start | bytes 393224 | tf_op jit(solution)/shard_map/while/body/eval_jaxpr/ppermute | solution.py:12
  171.5 10.1 %collective-permute-start.2 = (f32[128,256]{0,1:T(8,128)S(1)}, f32[128,256]{0,1:T(8,128)S(1)}, u32[]{:S(2)}, u32[]{:S(2)}) collective-permute-start(f32[128,256]{0,1:T(8,128)S(1)} %get-tuple-element.191), channel_id=1, source_target_pairs={{0,16},{16,32},{32,48},{48,64},{64,80},{80,96},{96,112},{112,128},... | collective-permute-start | bytes 393224 | tf_op jit(solution)/shard_map/while/body/eval_jaxpr/ppermute | solution.py:12
  181.6 10.7 %collective-permute-start = (bf16[128,256]{0,1:T(8,128)(2,1)S(1)}, bf16[128,256]{0,1:T(8,128)(2,1)S(1)}, u32[]{:S(2)}, u32[]{:S(2)}) collective-permute-start(bf16[128,256]{0,1:T(8,128)(2,1)S(1)} %get-tuple-element.189), channel_id=1, source_target_pairs={{0,16},{16,32},{32,48},{48,64},{64,80},{80,96},{96,112},{112,128},... | collective-permute-start | bytes 196616 | tf_op jit(solution)/shard_map/while/body/eval_jaxpr/ppermute | solution.py:12
  213.3 13.9 %collective-permute-start = (bf16[128,256]{0,1:T(8,128)(2,1)S(1)}, bf16[128,256]{0,1:T(8,128)(2,1)S(1)}, u32[]{:S(2)}, u32[]{:S(2)}) collective-permute-start(bf16[128,256]{0,1:T(8,128)(2,1)S(1)} %get-tuple-element.189), channel_id=1, source_target_pairs={{0,16},{16,32},{32,48},{48,64},{64,80},{80,96},{96,112},{112,128},... | collective-permute-start | bytes 196616 | tf_op jit(solution)/shard_map/while/body/eval_jaxpr/ppermute | solution.py:12
  215.3 12.2 %collective-permute-start.1 = (bf16[128,256]{0,1:T(8,128)(2,1)S(1)}, bf16[128,256]{0,1:T(8,128)(2,1)S(1)}, u32[]{:S(2)}, u32[]{:S(2)}) collective-permute-start(bf16[128,256]{0,1:T(8,128)(2,1)S(1)} %get-tuple-element.190), channel_id=1, source_target_pairs={{0,16},{16,32},{32,48},{48,64},{64,80},{80,96},{96,112},{112,128},... | collective-permute-start | bytes 196616 | tf_op jit(solution)/shard_map/while/body/eval_jaxpr/ppermute | solution.py:12
  217.9 10.6 %collective-permute-start.3 = (f32[128,256]{0,1:T(8,128)S(1)}, f32[128,256]{0,1:T(8,128)S(1)}, u32[]{:S(2)}, u32[]{:S(2)}) collective-permute-start(f32[128,256]{0,1:T(8,128)S(1)} %get-tuple-element.192), channel_id=1, source_target_pairs={{0,16},{16,32},{32,48},{48,64},{64,80},{80,96},{96,112},{112,128},... | collective-permute-start | bytes 393224 | tf_op jit(solution)/shard_map/while/body/eval_jaxpr/ppermute | solution.py:12
  230.7 13.4 %collective-permute-start = (bf16[128,256]{0,1:T(8,128)(2,1)S(1)}, bf16[128,256]{0,1:T(8,128)(2,1)S(1)}, u32[]{:S(2)}, u32[]{:S(2)}) collective-permute-start(bf16[128,256]{0,1:T(8,128)(2,1)S(1)} %get-tuple-element.189), channel_id=1, source_target_pairs={{0,16},{16,32},{32,48},{48,64},{64,80},{80,96},{96,112},{112,128},... | collective-permute-start | bytes 196616 | tf_op jit(solution)/shard_map/while/body/eval_jaxpr/ppermute | solution.py:12
  234.1 10.2 %collective-permute-start.1 = (bf16[128,256]{0,1:T(8,128)(2,1)S(1)}, bf16[128,256]{0,1:T(8,128)(2,1)S(1)}, u32[]{:S(2)}, u32[]{:S(2)}) collective-permute-start(bf16[128,256]{0,1:T(8,128)(2,1)S(1)} %get-tuple-element.190), channel_id=1, source_target_pairs={{0,16},{16,32},{32,48},{48,64},{64,80},{80,96},{96,112},{112,128},... | collective-permute-start | bytes 196616 | tf_op jit(solution)/shard_map/while/body/eval_jaxpr/ppermute | solution.py:12
  250.1 10.3 %collective-permute-start = (bf16[128,256]{0,1:T(8,128)(2,1)S(1)}, bf16[128,256]{0,1:T(8,128)(2,1)S(1)}, u32[]{:S(2)}, u32[]{:S(2)}) collective-permute-start(bf16[128,256]{0,1:T(8,128)(2,1)S(1)} %get-tuple-element.189), channel_id=1, source_target_pairs={{0,16},{16,32},{32,48},{48,64},{64,80},{80,96},{96,112},{112,128},... | collective-permute-start | bytes 196616 | tf_op jit(solution)/shard_map/while/body/eval_jaxpr/ppermute | solution.py:12
  265.4 12.1 %collective-permute-start = (bf16[128,256]{0,1:T(8,128)(2,1)S(1)}, bf16[128,256]{0,1:T(8,128)(2,1)S(1)}, u32[]{:S(2)}, u32[]{:S(2)}) collective-permute-start(bf16[128,256]{0,1:T(8,128)(2,1)S(1)} %get-tuple-element.189), channel_id=1, source_target_pairs={{0,16},{16,32},{32,48},{48,64},{64,80},{80,96},{96,112},{112,128},... | collective-permute-start | bytes 196616 | tf_op jit(solution)/shard_map/while/body/eval_jaxpr/ppermute | solution.py:12
  283.0 10.5 %collective-permute-start = (bf16[128,256]{0,1:T(8,128)(2,1)S(1)}, bf16[128,256]{0,1:T(8,128)(2,1)S(1)}, u32[]{:S(2)}, u32[]{:S(2)}) collective-permute-start(bf16[128,256]{0,1:T(8,128)(2,1)S(1)} %get-tuple-element.189), channel_id=1, source_target_pairs={{0,16},{16,32},{32,48},{48,64},{64,80},{80,96},{96,112},{112,128},... | collective-permute-start | bytes 196616 | tf_op jit(solution)/shard_map/while/body/eval_jaxpr/ppermute | solution.py:12
  298.8 11.0 %collective-permute-start = (bf16[128,256]{0,1:T(8,128)(2,1)S(1)}, bf16[128,256]{0,1:T(8,128)(2,1)S(1)}, u32[]{:S(2)}, u32[]{:S(2)}) collective-permute-start(bf16[128,256]{0,1:T(8,128)(2,1)S(1)} %get-tuple-element.189), channel_id=1, source_target_pairs={{0,16},{16,32},{32,48},{48,64},{64,80},{80,96},{96,112},{112,128},... | collective-permute-start | bytes 196616 | tf_op jit(solution)/shard_map/while/body/eval_jaxpr/ppermute | solution.py:12
  314.6 14.4 %collective-permute-start = (bf16[128,256]{0,1:T(8,128)(2,1)S(1)}, bf16[128,256]{0,1:T(8,128)(2,1)S(1)}, u32[]{:S(2)}, u32[]{:S(2)}) collective-permute-start(bf16[128,256]{0,1:T(8,128)(2,1)S(1)} %get-tuple-element.189), channel_id=1, source_target_pairs={{0,16},{16,32},{32,48},{48,64},{64,80},{80,96},{96,112},{112,128},... | collective-permute-start | bytes 196616 | tf_op jit(solution)/shard_map/while/body/eval_jaxpr/ppermute | solution.py:12
  316.8 12.5 %collective-permute-start.1 = (bf16[128,256]{0,1:T(8,128)(2,1)S(1)}, bf16[128,256]{0,1:T(8,128)(2,1)S(1)}, u32[]{:S(2)}, u32[]{:S(2)}) collective-permute-start(bf16[128,256]{0,1:T(8,128)(2,1)S(1)} %get-tuple-element.190), channel_id=1, source_target_pairs={{0,16},{16,32},{32,48},{48,64},{64,80},{80,96},{96,112},{112,128},... | collective-permute-start | bytes 196616 | tf_op jit(solution)/shard_map/while/body/eval_jaxpr/ppermute | solution.py:12
  333.9 13.0 %collective-permute-start = (bf16[128,256]{0,1:T(8,128)(2,1)S(1)}, bf16[128,256]{0,1:T(8,128)(2,1)S(1)}, u32[]{:S(2)}, u32[]{:S(2)}) collective-permute-start(bf16[128,256]{0,1:T(8,128)(2,1)S(1)} %get-tuple-element.189), channel_id=1, source_target_pairs={{0,16},{16,32},{32,48},{48,64},{64,80},{80,96},{96,112},{112,128},... | collective-permute-start | bytes 196616 | tf_op jit(solution)/shard_map/while/body/eval_jaxpr/ppermute | solution.py:12
  337.1 10.1 %collective-permute-start.1 = (bf16[128,256]{0,1:T(8,128)(2,1)S(1)}, bf16[128,256]{0,1:T(8,128)(2,1)S(1)}, u32[]{:S(2)}, u32[]{:S(2)}) collective-permute-start(bf16[128,256]{0,1:T(8,128)(2,1)S(1)} %get-tuple-element.190), channel_id=1, source_target_pairs={{0,16},{16,32},{32,48},{48,64},{64,80},{80,96},{96,112},{112,128},... | collective-permute-start | bytes 196616 | tf_op jit(solution)/shard_map/while/body/eval_jaxpr/ppermute | solution.py:12
  352.0 11.1 %collective-permute-start = (bf16[128,256]{0,1:T(8,128)(2,1)S(1)}, bf16[128,256]{0,1:T(8,128)(2,1)S(1)}, u32[]{:S(2)}, u32[]{:S(2)}) collective-permute-start(bf16[128,256]{0,1:T(8,128)(2,1)S(1)} %get-tuple-element.189), channel_id=1, source_target_pairs={{0,16},{16,32},{32,48},{48,64},{64,80},{80,96},{96,112},{112,128},... | collective-permute-start | bytes 196616 | tf_op jit(solution)/shard_map/while/body/eval_jaxpr/ppermute | solution.py:12
  368.0 10.9 %collective-permute-start = (bf16[128,256]{0,1:T(8,128)(2,1)S(1)}, bf16[128,256]{0,1:T(8,128)(2,1)S(1)}, u32[]{:S(2)}, u32[]{:S(2)}) collective-permute-start(bf16[128,256]{0,1:T(8,128)(2,1)S(1)} %get-tuple-element.189), channel_id=1, source_target_pairs={{0,16},{16,32},{32,48},{48,64},{64,80},{80,96},{96,112},{112,128},... | collective-permute-start | bytes 196616 | tf_op jit(solution)/shard_map/while/body/eval_jaxpr/ppermute | solution.py:12
  384.3 10.8 %collective-permute-start = (bf16[128,256]{0,1:T(8,128)(2,1)S(1)}, bf16[128,256]{0,1:T(8,128)(2,1)S(1)}, u32[]{:S(2)}, u32[]{:S(2)}) collective-permute-start(bf16[128,256]{0,1:T(8,128)(2,1)S(1)} %get-tuple-element.189), channel_id=1, source_target_pairs={{0,16},{16,32},{32,48},{48,64},{64,80},{80,96},{96,112},{112,128},... | collective-permute-start | bytes 196616 | tf_op jit(solution)/shard_map/while/body/eval_jaxpr/ppermute | solution.py:12
  400.1 13.3 %collective-permute-start = (bf16[128,256]{0,1:T(8,128)(2,1)S(1)}, bf16[128,256]{0,1:T(8,128)(2,1)S(1)}, u32[]{:S(2)}, u32[]{:S(2)}) collective-permute-start(bf16[128,256]{0,1:T(8,128)(2,1)S(1)} %get-tuple-element.189), channel_id=1, source_target_pairs={{0,16},{16,32},{32,48},{48,64},{64,80},{80,96},{96,112},{112,128},... | collective-permute-start | bytes 196616 | tf_op jit(solution)/shard_map/while/body/eval_jaxpr/ppermute | solution.py:12
  402.1 11.6 %collective-permute-start.1 = (bf16[128,256]{0,1:T(8,128)(2,1)S(1)}, bf16[128,256]{0,1:T(8,128)(2,1)S(1)}, u32[]{:S(2)}, u32[]{:S(2)}) collective-permute-start(bf16[128,256]{0,1:T(8,128)(2,1)S(1)} %get-tuple-element.190), channel_id=1, source_target_pairs={{0,16},{16,32},{32,48},{48,64},{64,80},{80,96},{96,112},{112,128},... | collective-permute-start | bytes 196616 | tf_op jit(solution)/shard_map/while/body/eval_jaxpr/ppermute | solution.py:12
  404.5 10.2 %collective-permute-start.3 = (f32[128,256]{0,1:T(8,128)S(1)}, f32[128,256]{0,1:T(8,128)S(1)}, u32[]{:S(2)}, u32[]{:S(2)}) collective-permute-start(f32[128,256]{0,1:T(8,128)S(1)} %get-tuple-element.192), channel_id=1, source_target_pairs={{0,16},{16,32},{32,48},{48,64},{64,80},{80,96},{96,112},{112,128},... | collective-permute-start | bytes 393224 | tf_op jit(solution)/shard_map/while/body/eval_jaxpr/ppermute | solution.py:12
  416.9 15.3 %collective-permute-start = (bf16[128,256]{0,1:T(8,128)(2,1)S(1)}, bf16[128,256]{0,1:T(8,128)(2,1)S(1)}, u32[]{:S(2)}, u32[]{:S(2)}) collective-permute-start(bf16[128,256]{0,1:T(8,128)(2,1)S(1)} %get-tuple-element.189), channel_id=1, source_target_pairs={{0,16},{16,32},{32,48},{48,64},{64,80},{80,96},{96,112},{112,128},... | collective-permute-start | bytes 196616 | tf_op jit(solution)/shard_map/while/body/eval_jaxpr/ppermute | solution.py:12
  420.3 12.2 %collective-permute-start.1 = (bf16[128,256]{0,1:T(8,128)(2,1)S(1)}, bf16[128,256]{0,1:T(8,128)(2,1)S(1)}, u32[]{:S(2)}, u32[]{:S(2)}) collective-permute-start(bf16[128,256]{0,1:T(8,128)(2,1)S(1)} %get-tuple-element.190), channel_id=1, source_target_pairs={{0,16},{16,32},{32,48},{48,64},{64,80},{80,96},{96,112},{112,128},... | collective-permute-start | bytes 196616 | tf_op jit(solution)/shard_map/while/body/eval_jaxpr/ppermute | solution.py:12
  423.2 10.4 %collective-permute-start.3 = (f32[128,256]{0,1:T(8,128)S(1)}, f32[128,256]{0,1:T(8,128)S(1)}, u32[]{:S(2)}, u32[]{:S(2)}) collective-permute-start(f32[128,256]{0,1:T(8,128)S(1)} %get-tuple-element.192), channel_id=1, source_target_pairs={{0,16},{16,32},{32,48},{48,64},{64,80},{80,96},{96,112},{112,128},... | collective-permute-start | bytes 393224 | tf_op jit(solution)/shard_map/while/body/eval_jaxpr/ppermute | solution.py:12
  436.4 12.1 %collective-permute-start = (bf16[128,256]{0,1:T(8,128)(2,1)S(1)}, bf16[128,256]{0,1:T(8,128)(2,1)S(1)}, u32[]{:S(2)}, u32[]{:S(2)}) collective-permute-start(bf16[128,256]{0,1:T(8,128)(2,1)S(1)} %get-tuple-element.189), channel_id=1, source_target_pairs={{0,16},{16,32},{32,48},{48,64},{64,80},{80,96},{96,112},{112,128},... | collective-permute-start | bytes 196616 | tf_op jit(solution)/shard_map/while/body/eval_jaxpr/ppermute | solution.py:12
  453.2 12.4 %collective-permute-start = (bf16[128,256]{0,1:T(8,128)(2,1)S(1)}, bf16[128,256]{0,1:T(8,128)(2,1)S(1)}, u32[]{:S(2)}, u32[]{:S(2)}) collective-permute-start(bf16[128,256]{0,1:T(8,128)(2,1)S(1)} %get-tuple-element.189), channel_id=1, source_target_pairs={{0,16},{16,32},{32,48},{48,64},{64,80},{80,96},{96,112},{112,128},... | collective-permute-start | bytes 196616 | tf_op jit(solution)/shard_map/while/body/eval_jaxpr/ppermute | solution.py:12
  455.4 10.5 %collective-permute-start.1 = (bf16[128,256]{0,1:T(8,128)(2,1)S(1)}, bf16[128,256]{0,1:T(8,128)(2,1)S(1)}, u32[]{:S(2)}, u32[]{:S(2)}) collective-permute-start(bf16[128,256]{0,1:T(8,128)(2,1)S(1)} %get-tuple-element.190), channel_id=1, source_target_pairs={{0,16},{16,32},{32,48},{48,64},{64,80},{80,96},{96,112},{112,128},... | collective-permute-start | bytes 196616 | tf_op jit(solution)/shard_map/while/body/eval_jaxpr/ppermute | solution.py:12
  470.6 11.0 %collective-permute-start = (bf16[128,256]{0,1:T(8,128)(2,1)S(1)}, bf16[128,256]{0,1:T(8,128)(2,1)S(1)}, u32[]{:S(2)}, u32[]{:S(2)}) collective-permute-start(bf16[128,256]{0,1:T(8,128)(2,1)S(1)} %get-tuple-element.189), channel_id=1, source_target_pairs={{0,16},{16,32},{32,48},{48,64},{64,80},{80,96},{96,112},{112,128},... | collective-permute-start | bytes 196616 | tf_op jit(solution)/shard_map/while/body/eval_jaxpr/ppermute | solution.py:12
  503.4 13.3 %collective-permute-start = (bf16[128,256]{0,1:T(8,128)(2,1)S(1)}, bf16[128,256]{0,1:T(8,128)(2,1)S(1)}, u32[]{:S(2)}, u32[]{:S(2)}) collective-permute-start(bf16[128,256]{0,1:T(8,128)(2,1)S(1)} %get-tuple-element.189), channel_id=1, source_target_pairs={{0,16},{16,32},{32,48},{48,64},{64,80},{80,96},{96,112},{112,128},... | collective-permute-start | bytes 196616 | tf_op jit(solution)/shard_map/while/body/eval_jaxpr/ppermute | solution.py:12
  505.3 11.6 %collective-permute-start.1 = (bf16[128,256]{0,1:T(8,128)(2,1)S(1)}, bf16[128,256]{0,1:T(8,128)(2,1)S(1)}, u32[]{:S(2)}, u32[]{:S(2)}) collective-permute-start(bf16[128,256]{0,1:T(8,128)(2,1)S(1)} %get-tuple-element.190), channel_id=1, source_target_pairs={{0,16},{16,32},{32,48},{48,64},{64,80},{80,96},{96,112},{112,128},... | collective-permute-start | bytes 196616 | tf_op jit(solution)/shard_map/while/body/eval_jaxpr/ppermute | solution.py:12
  520.6 11.7 %collective-permute-start = (bf16[128,256]{0,1:T(8,128)(2,1)S(1)}, bf16[128,256]{0,1:T(8,128)(2,1)S(1)}, u32[]{:S(2)}, u32[]{:S(2)}) collective-permute-start(bf16[128,256]{0,1:T(8,128)(2,1)S(1)} %get-tuple-element.189), channel_id=1, source_target_pairs={{0,16},{16,32},{32,48},{48,64},{64,80},{80,96},{96,112},{112,128},... | collective-permute-start | bytes 196616 | tf_op jit(solution)/shard_map/while/body/eval_jaxpr/ppermute | solution.py:12
  (82 other events, 731.5 us)
where the time goes:
time: 556 us; the launch traced here: 550 us
  starting transfers between devices  377 us (68%)
  waiting for transfers between devices  124 us (22%)
  matrix products  31.4 us (6%)
  local copies, waits for them, and re-layouts  10.4 us (2%)
    ppermute x124, starting transfers between devices, shifted(): return lax.ppermute(value, axis, pairs)  370 us
    ppermute x124, waiting for transfers between devices, shifted(): return lax.ppermute(value, axis, pairs)  124 us
  transfers between devices with their start and end apart: 125, of which 61 were waited for; matrix products, arithmetic and copies ran while one was open for 7% of the time, Pallas kernels for 0%

commit v1 on v0

v1 whole, which is shorter than its diff:
```python
import functools
import math

import jax
import jax.numpy as jnp
from jax import lax
from jax.experimental import pallas as pl
from jax.experimental.pallas import tpu as pltpu
from jax.sharding import Mesh, PartitionSpec as P

HD = 128
TOK = 128
ROWS = 2 * TOK
AUX = 16
PAY = 2 * ROWS + AUX
RING = 16
LOG2E = math.log2(math.e)
FACTOR = 1.0 / math.sqrt(HD)
BF = jnp.bfloat16
F32 = jnp.float32
K_STEPS = (1, -1, -2)
Q_STEPS = (4, -4, 8)


def pieces(value):
    high = value.astype(BF)
    rest = value - high.astype(F32)
    mid = rest.astype(BF)
    low = (rest - mid.astype(F32)).astype(BF)
    return [high.astype(F32), mid.astype(F32), low.astype(F32)]


def local(kernel, outs, *args):
    scalars = [pl.BlockSpec(memory_space=pltpu.SMEM)]
    whole = [pl.BlockSpec(memory_space=pltpu.VMEM)]
    return pl.pallas_call(
        kernel,
        out_shape=[jax.ShapeDtypeStruct(shape, dtype) for shape, dtype in outs],
        in_specs=[(scalars if arg.dtype == jnp.int32 else whole)[0] for arg in args],
        out_specs=whole * len(outs),
        compiler_params=pltpu.CompilerParams(vmem_limit_bytes=48 * 1024 * 1024),
    )(*args)


def split_kernel(side, key, value, query, out, lnorm, keep, send):
    def put(mine, other):
        for slot, rows in enumerate((key, value, query, out)):
            at = slice(slot * TOK, (slot + 1) * TOK)
            keep[at, :] = rows[:, mine * HD : (mine + 1) * HD]
            send[at, :] = rows[:, other * HD : (other + 1) * HD]
        for head, dest in ((mine, keep), (other, send)):
            norm = lnorm[head : head + 1, :] * LOG2E
            blank = jnp.zeros((AUX - 3, TOK), F32)
            dest[4 * TOK :, :] = jnp.concatenate(pieces(norm) + [blank], axis=0).astype(BF)

    @pl.when(side[0] == 0)
    def _():
        put(0, 1)

    @pl.when(side[0] != 0)
    def _():
        put(1, 0)


def merge_kernel(side, keep, got, keys, query, out, norm):
    def put(first, second):
        for slot, (dest, at) in enumerate(((keys, 0), (keys, ROWS), (query, 0), (out, 0))):
            rows = slice(slot * TOK, (slot + 1) * TOK)
            dest[at : at + TOK, :] = first[rows, :]
            dest[at + TOK : at + ROWS, :] = second[rows, :]
        norm[:AUX, :] = first[4 * TOK :, :]
        norm[AUX:, :] = second[4 * TOK :, :]

    @pl.when(side[0] == 0)
    def _():
        put(keep, got)

    @pl.when(side[0] != 0)
    def _():
        put(got, keep)


def delta_kernel(query, out, norm, dout, pay):
    pay[:ROWS, :] = query[...]
    pay[ROWS : 2 * ROWS, :] = dout[...]
    product = dout[...].astype(F32) * out[...].astype(F32)
    delta = jnp.sum(product.T, axis=0, keepdims=True)
    first = norm[:AUX, :].astype(F32)
    second = norm[AUX:, :].astype(F32)
    rows = (
        [first[:3, :], second[:3, :]]
        + pieces(delta[:, :TOK])
        + pieces(delta[:, TOK:])
        + [jnp.zeros((AUX - 12, TOK), F32)]
    )
    pay[2 * ROWS :, :] = jnp.concatenate(rows, axis=0).astype(BF)


def dot(left, right, left_dim, right_dim):
    return lax.dot_general(
        left, right, (((left_dim,), (right_dim,)), ((), ())), preferred_element_type=F32
    )


def row_of(aux, at):
    first = aux[at : at + 1, :] + aux[at + 1 : at + 2, :] + aux[at + 2 : at + 3, :]
    second = aux[at + 3 : at + 4, :] + aux[at + 4 : at + 5, :] + aux[at + 5 : at + 6, :]
    return jnp.concatenate([first, second], axis=1)


def tile(pay, keys):
    query = pay[:ROWS, :]
    dout = pay[ROWS : 2 * ROWS, :]
    aux = pay[2 * ROWS :, :].astype(F32)
    key = keys[:ROWS, :]
    value = keys[ROWS:, :]
    probs = jnp.exp2(dot(key, query, 1, 1) * (FACTOR * LOG2E) - row_of(aux, 0))
    dprobs = dot(value, dout, 1, 1)
    dscore = (probs * (dprobs - row_of(aux, 6))).astype(BF)
    grad_v = dot(probs.astype(BF), dout, 1, 0)
    grad_k = dot(dscore, query, 1, 0)
    grad_q = dot(dscore, key, 0, 0)
    return grad_q, grad_k, grad_v


def own_kernel(pay, keys0, keys1, keys2, keys3, grad_q, acc):
    total = None
    for slot, keys in enumerate((keys0, keys1, keys2, keys3)):
        part_q, part_k, part_v = tile(pay, keys)
        total = part_q if total is None else total + part_q
        acc[slot, :ROWS, :] = part_k
        acc[slot, ROWS:, :] = part_v
    grad_q[...] = total * FACTOR


def rest_kernel(pay1, pay2, pay3, keys0, keys1, keys2, keys3, acc, *outs):
    grads_q, grads_kv = outs[:3], outs[3:7]
    pays = (pay1, pay2, pay3)
    totals = [None] * 3
    for slot, keys in enumerate((keys0, keys1, keys2, keys3)):
        sum_k = acc[slot, :ROWS, :]
        sum_v = acc[slot, ROWS:, :]
        for at, pay in enumerate(pays):
            part_q, part_k, part_v = tile(pay, keys)
            totals[at] = part_q if totals[at] is None else totals[at] + part_q
            sum_k += part_k
            sum_v += part_v
        dest = grads_kv[slot]
        dest[:ROWS, :] = (sum_k * FACTOR).astype(dest.dtype)
        dest[ROWS:, :] = sum_v.astype(dest.dtype)
    for at in range(3):
        grads_q[at][...] = (totals[at] * FACTOR).astype(BF)


def sum_kernel(side, own_q, got_q1, got_q2, got_q3, own_kv, got_kv1, got_kv2, got_kv3, keep, send):
    total_q = own_q[...]
    for got in (got_q1, got_q2, got_q3):
        total_q += got[...].astype(F32)
    total_kv = own_kv[...]
    for got in (got_kv1, got_kv2, got_kv3):
        total_kv += got[...].astype(F32)
    total_q = total_q.astype(BF)
    total_kv = total_kv.astype(BF)

    def put(first, second):
        for slot, (rows, at) in enumerate(((total_q, 0), (total_kv, 0), (total_kv, ROWS))):
            dest = slice(slot * TOK, (slot + 1) * TOK)
            first[dest, :] = rows[at : at + TOK, :]
            second[dest, :] = rows[at + TOK : at + ROWS, :]

    @pl.when(side[0] == 0)
    def _():
        put(keep, send)

    @pl.when(side[0] != 0)
    def _():
        put(send, keep)


def join_kernel(side, keep, got, *outs):
    def put(first, second):
        for slot, dest in enumerate(outs):
            rows = slice(slot * TOK, (slot + 1) * TOK)
            dest[:, :HD] = first[rows, :]
            dest[:, HD:] = second[rows, :]

    @pl.when(side[0] == 0)
    def _():
        put(keep, got)

    @pl.when(side[0] != 0)
    def _():
        put(got, keep)


def along(value, steps):
    return lax.ppermute(value, "z", [(at, (at + steps) % RING) for at in range(RING)])


def across(value):
    return lax.ppermute(value, "x_lo", [(0, 1), (1, 0)])


def body(query_rows, key_rows, value_rows, output_rows, grad_output, log_norm):
    side = lax.axis_index("x_lo").astype(jnp.int32).reshape(1)
    heads = grad_output.reshape(8, 16, 2, HD).transpose(2, 1, 0, 3).reshape(32, 8, HD)
    dout = lax.all_to_all(heads, ("x_lo", "x_hi", "y", "core"), 0, 0, tiled=True)
    dout = dout.reshape(ROWS, HD)
    swap = ((4 * TOK + AUX, HD), BF)
    keep, send = local(
        split_kernel,
        [swap, swap],
        side,
        key_rows,
        value_rows,
        query_rows,
        output_rows,
        log_norm.T,
    )
    got = across(send)
    block = ((ROWS, HD), BF)
    pair = ((2 * ROWS, HD), BF)
    keys, query, out, norm = local(
        merge_kernel, [pair, block, block, ((2 * AUX, HD), BF)], side, keep, got
    )
    all_keys = [keys] + [along(keys, step) for step in K_STEPS]
    (pay,) = local(delta_kernel, [((PAY, HD), BF)], query, out, norm, dout)
    pays = [along(pay, step) for step in Q_STEPS]
    own_q, acc = local(
        own_kernel, [((ROWS, HD), F32), ((4, 2 * ROWS, HD), F32)], pay, *all_keys
    )
    outs = local(
        rest_kernel,
        [block] * 3 + [((2 * ROWS, HD), F32)] + [pair] * 3,
        *pays,
        *all_keys,
        acc,
    )
    got_q = [along(part, -step) for part, step in zip(outs[:3], Q_STEPS)]
    got_kv = [along(part, -step) for part, step in zip(outs[4:], K_STEPS)]
    half = ((3 * TOK, HD), BF)
    keep, send = local(sum_kernel, [half, half], side, own_q, *got_q, outs[3], *got_kv)
    got = across(send)
    return tuple(local(join_kernel, [((TOK, 2 * HD), BF)] * 3, side, keep, got))


def solution(mesh):
    fine = Mesh(
        mesh.devices.reshape(2, RING, 2, 4, 2), ("x_lo", "z", "x_hi", "y", "core")
    )
    blk, uly = ("x_lo", "z"), ("x_hi", "y", "core")
    placed = P(blk, uly)
    return jax.shard_map(
        body,
        mesh=fine,
        in_specs=(placed, placed, placed, placed, P(blk + uly, None), placed),
        out_specs=(placed, placed, placed),
        check_vma=False,
    )
```

time: 556 us -> 130 us (0.23)
  starting transfers between devices: 377 us -> 67.7 us
  waiting for transfers between devices: 124 us -> 36.5 us
  matrix products: 31.4 us -> 0 us
  blocking collectives: 0 us -> 13 us
  local copies, waits for them, and re-layouts: 10.4 us -> 4.04 us
  Pallas kernels: 0 us -> 6.06 us
    ppermute x124 -> x14, starting transfers between devices: 370 us -> 67.7 us  [the longest x12 62.3 us: along(): lax.ppermute(value, 'z', [(at, (at + steps) % RING) for at in range(RING)])]
    ppermute x124 -> x14, waiting for transfers between devices: 124 us -> 36.5 us  [the longest x12 28.2 us: along(): lax.ppermute(value, 'z', [(at, (at + steps) % RING) for at in range(RING)])]
    dot_general x160 -> x0, matrix products: 31.4 us -> none  [the longest x32 7.14 us: pair_grads(): jnp.einsum('qhd,khd->hqk', query_h, key_h, preferred_element_type=jnp.flo...]
    all_to_all x0 -> x1, blocking collectives: none -> 13 us  [body(): lax.all_to_all(heads, ('x_lo', 'x_hi', 'y', 'core'), 0, 0, tiled=True)]
    all_to_all x1 -> x0, starting transfers between devices: 7.6 us -> none  [body(): lax.all_to_all(grad_output, 'uly', split_axis=1, concat_axis=0, tiled=True)]
    pallas_call x0 -> x7, Pallas kernels: none -> 6.06 us  [local(): pl.pallas_call(kernel, out_shape=[jax.ShapeDtypeStruct(shape, dtype) for...]
    mul x62 -> x0, local copies, waits for them, and re-layouts: 6.01 us -> none  [the longest x32 3.04 us: pair_grads(): jnp.einsum('hqk,qhd->khd', dscore, query_h, preferred_element_type=jnp.fl...]
  transfers between devices with their start and end apart: 125 -> 14, of which waited for: 61 -> 5; matrix products, arithmetic and copies ran while one was open for 7% -> 0% of each run, Pallas kernels for 0% -> 1%
where the time goes in v1:
time: 130 us; the launch traced here: 128 us
  starting transfers between devices  67.7 us (52%)
  waiting for transfers between devices  36.5 us (28%)
  blocking collectives  13 us (10%)
  Pallas kernels  6.06 us (5%)
  local copies, waits for them, and re-layouts  4.04 us (3%)
    ppermute x12, starting transfers between devices, along(): lax.ppermute(value, 'z', [(at, (at + steps) % RING) for at in range(RING)])  62.3 us
    ppermute x12, waiting for transfers between devices, along(): lax.ppermute(value, 'z', [(at, (at + steps) % RING) for at in range(RING)])  28.2 us
    all_to_all x1, blocking collectives, body(): lax.all_to_all(heads, ('x_lo', 'x_hi', 'y', 'core'), 0, 0, tiled=True)  13 us
    ppermute x2, waiting for transfers between devices, across(): return lax.ppermute(value, 'x_lo', [(0, 1), (1, 0)])  8.3 us
    pallas_call x7, Pallas kernels, local(): pl.pallas_call(kernel, out_shape=[jax.ShapeDtypeStruct(shape, dtype) for...  6.06 us
    ppermute x2, starting transfers between devices, across(): return lax.ppermute(value, 'x_lo', [(0, 1), (1, 0)])  5.41 us
    unnamed x12, local copies, waits for them, and re-layouts  4.03 us
  transfers between devices with their start and end apart: 14, of which 5 were waited for; matrix products, arithmetic and copies ran while one was open for 0% of the time, Pallas kernels for 1%

profile of v1, /device:TPU:6, one launch (start us, length us, event | category | flops | bytes accessed | tf_op | source)
XLA Modules:
  0.0 128.2 jit_solution(4746659288416752274)
XLA Ops:
  0.6 0.0 copy-start.4
  0.6 0.7 copy-done.4
  1.3 0.0 copy-start
  1.3 0.8 copy-done
  2.2 0.0 copy-start.1
  2.2 0.8 copy-done.1
  3.0 0.0 copy-start.2
  3.0 0.8 copy-done.2
  3.8 0.0 copy-start.3
  3.8 0.8 copy-done.3
  4.7 0.1 shard_map.85
  4.7 2.7 %collective-permute-start = (bf16[528,128]{1,0:T(8,128)(2,1)S(1)}, bf16[528,128]{1,0:T(8,128)(2,1)S(1)}, u32[]{:S(2)}, u32[]{:S(2)}) collective-permute-start(bf16[528,128]{1,0:T(8,128)(2,1)S(1)} %get-tuple-element.21), channel_id=1, source_target_pairs={{0,256},{256,0},{1,257},{257,1},{2,258},{258,2},{3,259},{259,3},{4... | collective-permute-start | bytes 405512 | tf_op jit(solution)/shard_map/ppermute | solution.py:201
  7.5 4.5 %collective-permute-done.got = bf16[528,128]{1,0:T(8,128)(2,1)S(1)} collective-permute-done((bf16[528,128]{1,0:T(8,128)(2,1)S(1)}, bf16[528,128]{1,0:T(8,128)(2,1)S(1)}, u32[]{:S(2)}, u32[]{:S(2)}) %collective-permute-start) | collective-permute-done | bytes 135200 | tf_op jit(solution)/shard_map/ppermute | solution.py:201
  12.0 0.0 copy-start.5
  12.0 3.8 %collective-permute-start.1 = (bf16[512,128]{1,0:T(8,128)(2,1)S(1)}, bf16[512,128]{1,0:T(8,128)(2,1)S(1)}, u32[]{:S(2)}, u32[]{:S(2)}) collective-permute-start(bf16[512,128]{1,0:T(8,128)(2,1)S(1)} %get-tuple-element.25.keys0), channel_id=1, source_target_pairs={{0,16},{16,32},{32,48},{48,64},{64,80},{80,96},{96,112},{112,128},... | collective-permute-start | bytes 393224 | tf_op jit(solution)/shard_map/ppermute | solution.py:197
  15.8 0.0 copy-done.5
  15.8 13.0 %all_to_all.5 = bf16[32,8,128]{2,1,0:T(8,128)(2,1)S(1)} all-to-all(bf16[32,8,128]{2,1,0:T(8,128)(2,1)S(1)} %bitcast.9), channel_id=1, replica_groups=mesh['x_lo'=2,'z'=16,'x_hi'=2,'y'=4,'core'=2] {'x_lo','x_hi','y','core'}, dimensions={0} | all-to-all | bytes 131072 | tf_op jit(solution)/shard_map/all_to_all | solution.py:207
  28.9 0.1 shard_map.87.pay
  29.0 9.1 %collective-permute-start.4 = (bf16[528,128]{1,0:T(8,128)(2,1)S(1)}, bf16[528,128]{1,0:T(8,128)(2,1)S(1)}, u32[]{:S(2)}, u32[]{:S(2)}) collective-permute-start(bf16[528,128]{1,0:T(8,128)(2,1)S(1)} %shard_map.87.pay), channel_id=1, source_target_pairs={{0,64},{16,80},{32,96},{48,112},{64,128},{80,144},{96,160},{112,17... | collective-permute-start | bytes 405512 | tf_op jit(solution)/shard_map/ppermute | solution.py:197
  38.1 4.7 %collective-permute-start.5 = (bf16[528,128]{1,0:T(8,128)(2,1)S(1)}, bf16[528,128]{1,0:T(8,128)(2,1)S(1)}, u32[]{:S(2)}, u32[]{:S(2)}) collective-permute-start(bf16[528,128]{1,0:T(8,128)(2,1)S(1)} %shard_map.87.pay), channel_id=1, source_target_pairs={{0,192},{16,208},{32,224},{48,240},{64,0},{80,16},{96,32},{112,48}... | collective-permute-start | bytes 405512 | tf_op jit(solution)/shard_map/ppermute | solution.py:197
  42.8 10.8 %collective-permute-start.6 = (bf16[528,128]{1,0:T(8,128)(2,1)S(1)}, bf16[528,128]{1,0:T(8,128)(2,1)S(1)}, u32[]{:S(2)}, u32[]{:S(2)}) collective-permute-start(bf16[528,128]{1,0:T(8,128)(2,1)S(1)} %shard_map.87.pay), channel_id=1, source_target_pairs={{0,128},{16,144},{32,160},{48,176},{64,192},{80,208},{96,224},{112... | collective-permute-start | bytes 405512 | tf_op jit(solution)/shard_map/ppermute | solution.py:197
  53.6 4.1 %collective-permute-start.2 = (bf16[512,128]{1,0:T(8,128)(2,1)S(1)}, bf16[512,128]{1,0:T(8,128)(2,1)S(1)}, u32[]{:S(2)}, u32[]{:S(2)}) collective-permute-start(bf16[512,128]{1,0:T(8,128)(2,1)S(1)} %get-tuple-element.25.keys0), channel_id=1, source_target_pairs={{0,240},{16,0},{32,16},{48,32},{64,48},{80,64},{96,80},{112,96},{1... | collective-permute-start | bytes 393224 | tf_op jit(solution)/shard_map/ppermute | solution.py:197
  57.7 0.0 collective-permute-done.1.keys1
  57.7 1.9 %collective-permute-start.3 = (bf16[512,128]{1,0:T(8,128)(2,1)S(1)}, bf16[512,128]{1,0:T(8,128)(2,1)S(1)}, u32[]{:S(2)}, u32[]{:S(2)}) collective-permute-start(bf16[512,128]{1,0:T(8,128)(2,1)S(1)} %get-tuple-element.25.keys0), channel_id=1, source_target_pairs={{0,224},{16,240},{32,0},{48,16},{64,32},{80,48},{96,64},{112,80},{... | collective-permute-start | bytes 393224 | tf_op jit(solution)/shard_map/ppermute | solution.py:197
  59.7 13.7 %collective-permute-done.2.keys2 = bf16[512,128]{1,0:T(8,128)(2,1)S(1)} collective-permute-done((bf16[512,128]{1,0:T(8,128)(2,1)S(1)}, bf16[512,128]{1,0:T(8,128)(2,1)S(1)}, u32[]{:S(2)}, u32[]{:S(2)}) %collective-permute-start.2) | collective-permute-done | bytes 131104 | tf_op jit(solution)/shard_map/ppermute | solution.py:197
  73.3 4.9 %collective-permute-done.3.keys3 = bf16[512,128]{1,0:T(8,128)(2,1)S(1)} collective-permute-done((bf16[512,128]{1,0:T(8,128)(2,1)S(1)}, bf16[512,128]{1,0:T(8,128)(2,1)S(1)}, u32[]{:S(2)}, u32[]{:S(2)}) %collective-permute-start.3) | collective-permute-done | bytes 131104 | tf_op jit(solution)/shard_map/ppermute | solution.py:197
  78.2 1.3 %shard_map.88 = (f32[256,128]{1,0:T(8,128)S(1)}, f32[4,512,128]{2,1,0:T(8,128)S(1)}) custom-call(bf16[528,128]{1,0:T(8,128)(2,1)S(1)} %shard_map.87.pay, bf16[512,128]{1,0:T(8,128)(2,1)S(1)} %get-tuple-element.25.keys0, bf16[512,128]{1,0:T(8,128)(2,1)S(1)} %collective-permute-done.1.keys1, bf16[512,128]{1,0:T(8,128)(2,1)S(1)} %collective-permute-done.2.keys2, ...), custom_call_target="tpu_custom_call" | custom-call | tf_op jit(solution)/shard_map/pallas_call | solution.py:36
  79.5 0.0 collective-permute-done.4.pay1
  79.6 0.0 collective-permute-done.5.pay2
  79.6 0.0 collective-permute-done.6.pay3
  79.6 3.7 %shard_map.89 = (bf16[256,128]{1,0:T(8,128)(2,1)S(1)}, bf16[256,128]{1,0:T(8,128)(2,1)S(1)}, bf16[256,128]{1,0:T(8,128)(2,1)S(1)}, f32[512,128]{1,0:T(8,128)S(1)...) custom-call(bf16[528,128]{1,0:T(8,128)(2,1)S(1)} %collective-permute-done.4.pay1, ...), custom_call_target="tpu_custom_call" | custom-call | tf_op jit(solution)/shard_map/pallas_call | solution.py:36
  83.3 4.8 %collective-permute-start.7 = (bf16[256,128]{1,0:T(8,128)(2,1)S(1)}, bf16[256,128]{1,0:T(8,128)(2,1)S(1)}, u32[]{:S(2)}, u32[]{:S(2)}) collective-permute-start(bf16[256,128]{1,0:T(8,128)(2,1)S(1)} %get-tuple-element.28), channel_id=1, source_target_pairs={{0,192},{16,208},{32,224},{48,240},{64,0},{80,16},{96,32},{112,48}... | collective-permute-start | bytes 196616 | tf_op jit(solution)/shard_map/ppermute | solution.py:197
  88.1 4.8 %collective-permute-start.10 = (bf16[512,128]{1,0:T(8,128)(2,1)S(1)}, bf16[512,128]{1,0:T(8,128)(2,1)S(1)}, u32[]{:S(2)}, u32[]{:S(2)}) collective-permute-start(bf16[512,128]{1,0:T(8,128)(2,1)S(1)} %get-tuple-element.32), channel_id=1, source_target_pairs={{0,240},{16,0},{32,16},{48,32},{64,48},{80,64},{96,80},{112,96},{1... | collective-permute-start | bytes 393224 | tf_op jit(solution)/shard_map/ppermute | solution.py:197
  92.9 1.9 %collective-permute-start.11 = (bf16[512,128]{1,0:T(8,128)(2,1)S(1)}, bf16[512,128]{1,0:T(8,128)(2,1)S(1)}, u32[]{:S(2)}, u32[]{:S(2)}) collective-permute-start(bf16[512,128]{1,0:T(8,128)(2,1)S(1)} %get-tuple-element.33), channel_id=1, source_target_pairs={{0,16},{16,32},{32,48},{48,64},{64,80},{80,96},{96,112},{112,128},... | collective-permute-start | bytes 393224 | tf_op jit(solution)/shard_map/ppermute | solution.py:197
  94.8 3.2 %collective-permute-start.12 = (bf16[512,128]{1,0:T(8,128)(2,1)S(1)}, bf16[512,128]{1,0:T(8,128)(2,1)S(1)}, u32[]{:S(2)}, u32[]{:S(2)}) collective-permute-start(bf16[512,128]{1,0:T(8,128)(2,1)S(1)} %get-tuple-element.34), channel_id=1, source_target_pairs={{0,32},{16,48},{32,64},{48,80},{64,96},{80,112},{96,128},{112,144}... | collective-permute-start | bytes 393224 | tf_op jit(solution)/shard_map/ppermute | solution.py:197
  98.0 4.3 %collective-permute-start.8 = (bf16[256,128]{1,0:T(8,128)(2,1)S(1)}, bf16[256,128]{1,0:T(8,128)(2,1)S(1)}, u32[]{:S(2)}, u32[]{:S(2)}) collective-permute-start(bf16[256,128]{1,0:T(8,128)(2,1)S(1)} %get-tuple-element.29), channel_id=1, source_target_pairs={{0,64},{16,80},{32,96},{48,112},{64,128},{80,144},{96,160},{112,17... | collective-permute-start | bytes 196616 | tf_op jit(solution)/shard_map/ppermute | solution.py:197
  102.3 0.0 collective-permute-done.7.got_q1
  102.3 8.8 %collective-permute-start.9 = (bf16[256,128]{1,0:T(8,128)(2,1)S(1)}, bf16[256,128]{1,0:T(8,128)(2,1)S(1)}, u32[]{:S(2)}, u32[]{:S(2)}) collective-permute-start(bf16[256,128]{1,0:T(8,128)(2,1)S(1)} %get-tuple-element.30), channel_id=1, source_target_pairs={{0,128},{16,144},{32,160},{48,176},{64,192},{80,208},{96,224},{112... | collective-permute-start | bytes 196616 | tf_op jit(solution)/shard_map/ppermute | solution.py:197
  111.2 0.0 collective-permute-done.8.got_q2
  111.2 9.6 %collective-permute-done.9.got_q3 = bf16[256,128]{1,0:T(8,128)(2,1)S(1)} collective-permute-done((bf16[256,128]{1,0:T(8,128)(2,1)S(1)}, bf16[256,128]{1,0:T(8,128)(2,1)S(1)}, u32[]{:S(2)}, u32[]{:S(2)}) %collective-permute-start.9) | collective-permute-done | bytes 65568 | tf_op jit(solution)/shard_map/ppermute | solution.py:197
  120.8 0.0 collective-permute-done.10.got_kv1
  120.8 0.0 collective-permute-done.11.got_kv2
  120.8 0.0 collective-permute-done.12.got_kv3
  120.8 0.1 shard_map.90
  121.0 2.7 %collective-permute-start.13 = (bf16[384,128]{1,0:T(8,128)(2,1)S(1)}, bf16[384,128]{1,0:T(8,128)(2,1)S(1)}, u32[]{:S(2)}, u32[]{:S(2)}) collective-permute-start(bf16[384,128]{1,0:T(8,128)(2,1)S(1)} %get-tuple-element.36), channel_id=1, source_target_pairs={{0,256},{256,0},{1,257},{257,1},{2,258},{258,2},{3,259},{259,3},{4... | collective-permute-start | bytes 294920 | tf_op jit(solution)/shard_map/ppermute | solution.py:201
  123.6 3.8 %collective-permute-done.13.got = bf16[384,128]{1,0:T(8,128)(2,1)S(1)} collective-permute-done((bf16[384,128]{1,0:T(8,128)(2,1)S(1)}, bf16[384,128]{1,0:T(8,128)(2,1)S(1)}, u32[]{:S(2)}, u32[]{:S(2)}) %collective-permute-start.13) | collective-permute-done | bytes 98336 | tf_op jit(solution)/shard_map/ppermute | solution.py:201
  127.5 0.7 shard_map.91
  (2 shorter events, 0.0 us)
Async XLA Ops:
  0.6 0.7 copy-start.4
  1.3 0.8 copy-start
  2.2 0.8 copy-start.1
  3.0 0.8 copy-start.2
  3.8 0.8 copy-start.3
  4.7 7.2 %collective-permute-start = (bf16[528,128]{1,0:T(8,128)(2,1)S(1)}, bf16[528,128]{1,0:T(8,128)(2,1)S(1)}, u32[]{:S(2)}, u32[]{:S(2)}) collective-permute-start(bf16[528,128]{1,0:T(8,128)(2,1)S(1)} %get-tuple-element.21), channel_id=1, source_target_pairs={{0,256},{256,0},{1,257},{257,1},{2,258},{258,2},{3,259},{259,3},{4... | collective-permute-start | bytes 405512 | tf_op jit(solution)/shard_map/ppermute | solution.py:201
  12.0 3.9 %copy-start.5 = (bf16[8,4096]{1,0:T(8,128)(2,1)S(1)}, bf16[8,4096]{1,0:T(8,128)(2,1)}, u32[]{:S(2)}) copy-start(bf16[8,4096]{1,0:T(8,128)(2,1)} %param.10) | copy-start | bytes 196612
  12.0 45.7 %collective-permute-start.1 = (bf16[512,128]{1,0:T(8,128)(2,1)S(1)}, bf16[512,128]{1,0:T(8,128)(2,1)S(1)}, u32[]{:S(2)}, u32[]{:S(2)}) collective-permute-start(bf16[512,128]{1,0:T(8,128)(2,1)S(1)} %get-tuple-element.25.keys0), channel_id=1, source_target_pairs={{0,16},{16,32},{32,48},{48,64},{64,80},{80,96},{96,112},{112,128},... | collective-permute-start | bytes 393224 | tf_op jit(solution)/shard_map/ppermute | solution.py:197
  29.0 50.6 %collective-permute-start.4 = (bf16[528,128]{1,0:T(8,128)(2,1)S(1)}, bf16[528,128]{1,0:T(8,128)(2,1)S(1)}, u32[]{:S(2)}, u32[]{:S(2)}) collective-permute-start(bf16[528,128]{1,0:T(8,128)(2,1)S(1)} %shard_map.87.pay), channel_id=1, source_target_pairs={{0,64},{16,80},{32,96},{48,112},{64,128},{80,144},{96,160},{112,17... | collective-permute-start | bytes 405512 | tf_op jit(solution)/shard_map/ppermute | solution.py:197
  38.1 41.5 %collective-permute-start.5 = (bf16[528,128]{1,0:T(8,128)(2,1)S(1)}, bf16[528,128]{1,0:T(8,128)(2,1)S(1)}, u32[]{:S(2)}, u32[]{:S(2)}) collective-permute-start(bf16[528,128]{1,0:T(8,128)(2,1)S(1)} %shard_map.87.pay), channel_id=1, source_target_pairs={{0,192},{16,208},{32,224},{48,240},{64,0},{80,16},{96,32},{112,48}... | collective-permute-start | bytes 405512 | tf_op jit(solution)/shard_map/ppermute | solution.py:197
  42.8 36.8 %collective-permute-start.6 = (bf16[528,128]{1,0:T(8,128)(2,1)S(1)}, bf16[528,128]{1,0:T(8,128)(2,1)S(1)}, u32[]{:S(2)}, u32[]{:S(2)}) collective-permute-start(bf16[528,128]{1,0:T(8,128)(2,1)S(1)} %shard_map.87.pay), channel_id=1, source_target_pairs={{0,128},{16,144},{32,160},{48,176},{64,192},{80,208},{96,224},{112... | collective-permute-start | bytes 405512 | tf_op jit(solution)/shard_map/ppermute | solution.py:197
  53.6 19.7 %collective-permute-start.2 = (bf16[512,128]{1,0:T(8,128)(2,1)S(1)}, bf16[512,128]{1,0:T(8,128)(2,1)S(1)}, u32[]{:S(2)}, u32[]{:S(2)}) collective-permute-start(bf16[512,128]{1,0:T(8,128)(2,1)S(1)} %get-tuple-element.25.keys0), channel_id=1, source_target_pairs={{0,240},{16,0},{32,16},{48,32},{64,48},{80,64},{96,80},{112,96},{1... | collective-permute-start | bytes 393224 | tf_op jit(solution)/shard_map/ppermute | solution.py:197
  57.7 20.5 %collective-permute-start.3 = (bf16[512,128]{1,0:T(8,128)(2,1)S(1)}, bf16[512,128]{1,0:T(8,128)(2,1)S(1)}, u32[]{:S(2)}, u32[]{:S(2)}) collective-permute-start(bf16[512,128]{1,0:T(8,128)(2,1)S(1)} %get-tuple-element.25.keys0), channel_id=1, source_target_pairs={{0,224},{16,240},{32,0},{48,16},{64,32},{80,48},{96,64},{112,80},{... | collective-permute-start | bytes 393224 | tf_op jit(solution)/shard_map/ppermute | solution.py:197
  83.3 19.1 %collective-permute-start.7 = (bf16[256,128]{1,0:T(8,128)(2,1)S(1)}, bf16[256,128]{1,0:T(8,128)(2,1)S(1)}, u32[]{:S(2)}, u32[]{:S(2)}) collective-permute-start(bf16[256,128]{1,0:T(8,128)(2,1)S(1)} %get-tuple-element.28), channel_id=1, source_target_pairs={{0,192},{16,208},{32,224},{48,240},{64,0},{80,16},{96,32},{112,48}... | collective-permute-start | bytes 196616 | tf_op jit(solution)/shard_map/ppermute | solution.py:197
  88.1 32.7 %collective-permute-start.10 = (bf16[512,128]{1,0:T(8,128)(2,1)S(1)}, bf16[512,128]{1,0:T(8,128)(2,1)S(1)}, u32[]{:S(2)}, u32[]{:S(2)}) collective-permute-start(bf16[512,128]{1,0:T(8,128)(2,1)S(1)} %get-tuple-element.32), channel_id=1, source_target_pairs={{0,240},{16,0},{32,16},{48,32},{64,48},{80,64},{96,80},{112,96},{1... | collective-permute-start | bytes 393224 | tf_op jit(solution)/shard_map/ppermute | solution.py:197
  92.9 27.9 %collective-permute-start.11 = (bf16[512,128]{1,0:T(8,128)(2,1)S(1)}, bf16[512,128]{1,0:T(8,128)(2,1)S(1)}, u32[]{:S(2)}, u32[]{:S(2)}) collective-permute-start(bf16[512,128]{1,0:T(8,128)(2,1)S(1)} %get-tuple-element.33), channel_id=1, source_target_pairs={{0,16},{16,32},{32,48},{48,64},{64,80},{80,96},{96,112},{112,128},... | collective-permute-start | bytes 393224 | tf_op jit(solution)/shard_map/ppermute | solution.py:197
  94.8 26.0 %collective-permute-start.12 = (bf16[512,128]{1,0:T(8,128)(2,1)S(1)}, bf16[512,128]{1,0:T(8,128)(2,1)S(1)}, u32[]{:S(2)}, u32[]{:S(2)}) collective-permute-start(bf16[512,128]{1,0:T(8,128)(2,1)S(1)} %get-tuple-element.34), channel_id=1, source_target_pairs={{0,32},{16,48},{32,64},{48,80},{64,96},{80,112},{96,128},{112,144}... | collective-permute-start | bytes 393224 | tf_op jit(solution)/shard_map/ppermute | solution.py:197
  98.0 13.2 %collective-permute-start.8 = (bf16[256,128]{1,0:T(8,128)(2,1)S(1)}, bf16[256,128]{1,0:T(8,128)(2,1)S(1)}, u32[]{:S(2)}, u32[]{:S(2)}) collective-permute-start(bf16[256,128]{1,0:T(8,128)(2,1)S(1)} %get-tuple-element.29), channel_id=1, source_target_pairs={{0,64},{16,80},{32,96},{48,112},{64,128},{80,144},{96,160},{112,17... | collective-permute-start | bytes 196616 | tf_op jit(solution)/shard_map/ppermute | solution.py:197
  102.3 18.5 %collective-permute-start.9 = (bf16[256,128]{1,0:T(8,128)(2,1)S(1)}, bf16[256,128]{1,0:T(8,128)(2,1)S(1)}, u32[]{:S(2)}, u32[]{:S(2)}) collective-permute-start(bf16[256,128]{1,0:T(8,128)(2,1)S(1)} %get-tuple-element.30), channel_id=1, source_target_pairs={{0,128},{16,144},{32,160},{48,176},{64,192},{80,208},{96,224},{112... | collective-permute-start | bytes 196616 | tf_op jit(solution)/shard_map/ppermute | solution.py:197
  121.0 6.5 %collective-permute-start.13 = (bf16[384,128]{1,0:T(8,128)(2,1)S(1)}, bf16[384,128]{1,0:T(8,128)(2,1)S(1)}, u32[]{:S(2)}, u32[]{:S(2)}) collective-permute-start(bf16[384,128]{1,0:T(8,128)(2,1)S(1)} %get-tuple-element.36), channel_id=1, source_target_pairs={{0,256},{256,0},{1,257},{257,1},{2,258},{258,2},{3,259},{259,3},{4... | collective-permute-start | bytes 294920 | tf_op jit(solution)/shard_map/ppermute | solution.py:201

commit v2 on v1

v2 whole, which is shorter than its diff:
```python
import functools
import math

import jax
import jax.numpy as jnp
from jax import lax
from jax.experimental import pallas as pl
from jax.experimental.pallas import tpu as pltpu
from jax.sharding import Mesh, PartitionSpec as P

HD = 128
TOK = 128
ROWS = 2 * TOK
AUX = 16
PAY = 2 * ROWS + AUX
RING = 16
LOG2E = math.log2(math.e)
FACTOR = 1.0 / math.sqrt(HD)
BF = jnp.bfloat16
F32 = jnp.float32
K_STEPS = (1, -1, -2)
GROUP = 4


def pieces(value):
    high = value.astype(BF)
    rest = value - high.astype(F32)
    mid = rest.astype(BF)
    low = (rest - mid.astype(F32)).astype(BF)
    return [high.astype(F32), mid.astype(F32), low.astype(F32)]


def local(kernel, outs, *args, far=(), scratch=()):
    scalars = [pl.BlockSpec(memory_space=pltpu.SMEM)]
    whole = [pl.BlockSpec(memory_space=pltpu.VMEM)]
    return pl.pallas_call(
        kernel,
        out_shape=[jax.ShapeDtypeStruct(shape, dtype) for shape, dtype in outs],
        in_specs=[
            pl.BlockSpec(memory_space=pltpu.HBM)
            if at in far
            else (scalars if arg.dtype == jnp.int32 else whole)[0]
            for at, arg in enumerate(args)
        ],
        out_specs=whole * len(outs),
        scratch_shapes=list(scratch),
        compiler_params=pltpu.CompilerParams(vmem_limit_bytes=48 * 1024 * 1024),
    )(*args)


def split_kernel(
    side, dout, key, value, query, out, lnorm, heads, keep, send, dout_in, rows_in, dout_sem, rows_sem
):
    load = pltpu.make_async_copy(dout, dout_in, dout_sem)
    load.start()
    loads = []
    for slot, rows in enumerate((key, value, query, out)):
        loads.append(pltpu.make_async_copy(rows, rows_in.at[slot], rows_sem.at[slot]))
        loads[-1].start()
    load.wait()
    for head in range(32):
        heads[(head % 2) * 16 + head // 2] = dout_in[:, head * HD : (head + 1) * HD]
    for each in loads:
        each.wait()

    def put(mine, other):
        for slot in range(4):
            at = slice(slot * TOK, (slot + 1) * TOK)
            keep[at, :] = rows_in[slot, :, mine * HD : (mine + 1) * HD]
            send[at, :] = rows_in[slot, :, other * HD : (other + 1) * HD]
        for head, dest in ((mine, keep), (other, send)):
            norm = lnorm[head : head + 1, :] * LOG2E
            blank = jnp.zeros((AUX - 3, TOK), F32)
            dest[4 * TOK :, :] = jnp.concatenate(pieces(norm) + [blank], axis=0).astype(BF)

    @pl.when(side[0] == 0)
    def _():
        put(0, 1)

    @pl.when(side[0] != 0)
    def _():
        put(1, 0)


def merge_kernel(side, keep, got, keys, query, out, norm):
    def put(first, second):
        for slot, (dest, at) in enumerate(((keys, 0), (keys, ROWS), (query, 0), (out, 0))):
            rows = slice(slot * TOK, (slot + 1) * TOK)
            dest[at : at + TOK, :] = first[rows, :]
            dest[at + TOK : at + ROWS, :] = second[rows, :]
        norm[:AUX, :] = first[4 * TOK :, :]
        norm[AUX:, :] = second[4 * TOK :, :]

    @pl.when(side[0] == 0)
    def _():
        put(keep, got)

    @pl.when(side[0] != 0)
    def _():
        put(got, keep)


def delta_kernel(query, out, norm, dout, pay):
    pay[:ROWS, :] = query[...]
    pay[ROWS : 2 * ROWS, :] = dout[...]
    product = dout[...].astype(F32) * out[...].astype(F32)
    delta = jnp.sum(product.T, axis=0, keepdims=True)
    first = norm[:AUX, :].astype(F32)
    second = norm[AUX:, :].astype(F32)
    rows = (
        [first[:3, :], second[:3, :]]
        + pieces(delta[:, :TOK])
        + pieces(delta[:, TOK:])
        + [jnp.zeros((AUX - 12, TOK), F32)]
    )
    pay[2 * ROWS :, :] = jnp.concatenate(rows, axis=0).astype(BF)


def dot(left, right, left_dim, right_dim):
    return lax.dot_general(
        left, right, (((left_dim,), (right_dim,)), ((), ())), preferred_element_type=F32
    )


def row_of(aux, at):
    first = aux[at : at + 1, :] + aux[at + 1 : at + 2, :] + aux[at + 2 : at + 3, :]
    second = aux[at + 3 : at + 4, :] + aux[at + 4 : at + 5, :] + aux[at + 5 : at + 6, :]
    return jnp.concatenate([first, second], axis=1)


def tile(pay, keys):
    query = pay[:ROWS, :]
    dout = pay[ROWS : 2 * ROWS, :]
    aux = pay[2 * ROWS :, :].astype(F32)
    probs = jnp.exp2(dot(keys[:ROWS, :], query, 1, 1) * (FACTOR * LOG2E) - row_of(aux, 0))
    dprobs = dot(keys[ROWS:, :], dout, 1, 1)
    dscore = (probs * (dprobs - row_of(aux, 6))).astype(BF)
    grad_v = dot(probs.astype(BF), dout, 1, 0)
    grad_k = dot(dscore, query, 1, 0)
    return dscore, grad_k, grad_v


def pairs_kernel(pays, keys0, keys1, keys2, keys3, dscores, *grads_kv):
    for slot, keys in enumerate((keys0, keys1, keys2, keys3)):
        sum_k = sum_v = None
        for at in range(GROUP):
            dscore, part_k, part_v = tile(pays.at[at], keys)
            dscores[at, slot * ROWS : (slot + 1) * ROWS, :] = dscore
            sum_k = part_k if at == 0 else sum_k + part_k
            sum_v = part_v if at == 0 else sum_v + part_v
        dest = grads_kv[slot]
        dest[:ROWS, :] = (sum_k * FACTOR).astype(dest.dtype)
        dest[ROWS:, :] = sum_v.astype(dest.dtype)


def query_kernel(dscores, keys0, keys1, keys2, keys3, grads_q):
    for at in range(GROUP):
        total = None
        for slot, keys in enumerate((keys0, keys1, keys2, keys3)):
            part = dot(keys[:ROWS, :], dscores[at, slot * ROWS : (slot + 1) * ROWS, :], 0, 0)
            total = part if slot == 0 else total + part
        grads_q[at] = (total * FACTOR).astype(BF)


def sum_kernel(side, got_q, own, got1, got2, got3, keep, send):
    total_q = got_q[0].astype(F32)
    for at in range(1, GROUP):
        total_q += got_q[at].astype(F32)
    total_q = total_q.T.astype(BF)
    total = own[...]
    for got in (got1, got2, got3):
        total += got[...].astype(F32)
    total = total.astype(BF)

    def put(first, second):
        for slot, (rows, at) in enumerate(((total_q, 0), (total, 0), (total, ROWS))):
            dest = slice(slot * TOK, (slot + 1) * TOK)
            first[dest, :] = rows[at : at + TOK, :]
            second[dest, :] = rows[at + TOK : at + ROWS, :]

    @pl.when(side[0] == 0)
    def _():
        put(keep, send)

    @pl.when(side[0] != 0)
    def _():
        put(send, keep)


def join_kernel(side, keep, got, *outs):
    def put(first, second):
        for slot, dest in enumerate(outs):
            rows = slice(slot * TOK, (slot + 1) * TOK)
            dest[:, :HD] = first[rows, :]
            dest[:, HD:] = second[rows, :]

    @pl.when(side[0] == 0)
    def _():
        put(keep, got)

    @pl.when(side[0] != 0)
    def _():
        put(got, keep)


def along(value, steps):
    pairs = []
    for at in range(RING):
        for core, shift in enumerate((steps, -steps)):
            pairs.append((2 * at + core, 2 * ((at + shift) % RING) + core))
    return lax.ppermute(value, ("z_hi", "z_lo", "core"), pairs)


def across(value):
    return lax.ppermute(value, "x_lo", [(0, 1), (1, 0)])


def body(query_rows, key_rows, value_rows, output_rows, grad_output, log_norm):
    side = lax.axis_index("x_lo").astype(jnp.int32).reshape(1)
    swap = ((4 * TOK + AUX, HD), BF)
    heads, keep, send = local(
        split_kernel,
        [((32, 8, HD), BF), swap, swap],
        side,
        *[
            pltpu.with_memory_space_constraint(rows, pltpu.HBM)
            for rows in (grad_output, key_rows, value_rows, query_rows, output_rows)
        ],
        log_norm.T,
        far=range(1, 6),
        scratch=(
            pltpu.VMEM((8, 32 * HD), BF),
            pltpu.VMEM((4, TOK, 2 * HD), BF),
            pltpu.SemaphoreType.DMA,
            pltpu.SemaphoreType.DMA((4,)),
        ),
    )
    dout = lax.all_to_all(heads, ("x_lo", "x_hi", "y", "core"), 0, 0, tiled=True)
    dout = dout.reshape(ROWS, HD)
    got = across(send)
    block = ((ROWS, HD), BF)
    pair = ((2 * ROWS, HD), BF)
    keys, query, out, norm = local(
        merge_kernel, [pair, block, block, ((2 * AUX, HD), BF)], side, keep, got
    )
    all_keys = [keys] + [along(keys, step) for step in K_STEPS]
    (pay,) = local(delta_kernel, [((PAY, HD), BF)], query, out, norm, dout)
    pays = lax.all_gather(pay, "z_hi")
    outs = local(
        pairs_kernel,
        [((GROUP, 4 * ROWS, ROWS), BF), ((2 * ROWS, HD), F32)] + [pair] * 3,
        pays,
        *all_keys,
    )
    got_kv = [along(part, -step) for part, step in zip(outs[2:], K_STEPS)]
    (parts_q,) = local(query_kernel, [((GROUP, HD, ROWS), BF)], outs[0], *all_keys)
    got_q = lax.all_to_all(parts_q, "z_hi", 0, 0, tiled=True)
    got_kv = [along(part, -step) for part, step in zip(outs[2:], K_STEPS)]
    half = ((3 * TOK, HD), BF)
    keep, send = local(sum_kernel, [half, half], side, got_q, outs[1], *got_kv)
    got = across(send)
    return tuple(local(join_kernel, [((TOK, 2 * HD), BF)] * 3, side, keep, got))


def solution(mesh):
    fine = Mesh(
        mesh.devices.reshape(2, 4, 4, 2, 4, 2), ("x_lo", "z_hi", "z_lo", "x_hi", "y", "core")
    )
    blk, uly = ("x_lo", "z_hi", "z_lo"), ("x_hi", "y", "core")
    placed = P(blk, uly)
    return jax.shard_map(
        body,
        mesh=fine,
        in_specs=(placed, placed, placed, placed, P(blk + uly, None), placed),
        out_specs=(placed, placed, placed),
        check_vma=False,
    )
```

time: 130 us -> 96.4 us (0.74)
  waiting for transfers between devices: 36.5 us -> 13.9 us
  starting transfers between devices: 67.7 us -> 46 us
  blocking collectives: 13 us -> 27.2 us
  local copies, waits for them, and re-layouts: 4.04 us -> 0.67 us
    ppermute x12 -> x6, starting transfers between devices: 62.3 us -> 25.1 us  [along(): return lax.ppermute(value, ('z_hi', 'z_lo', 'core'), pairs)]
    all_gather x0 -> x1, blocking collectives: none -> 27.2 us  [body(): pays = lax.all_gather(pay, 'z_hi')]
    ppermute x12 -> x6, waiting for transfers between devices: 28.2 us -> 10.2 us  [along(): return lax.ppermute(value, ('z_hi', 'z_lo', 'core'), pairs)]
    all_to_all x0 -> x2, starting transfers between devices: none -> 15.4 us  [the longest x1 8.71 us: body(): lax.all_to_all(heads, ('x_lo', 'x_hi', 'y', 'core'), 0, 0, tiled=True)]
    all_to_all x1 -> x0, blocking collectives: 13 us -> none  [body(): lax.all_to_all(heads, ('x_lo', 'x_hi', 'y', 'core'), 0, 0, tiled=True)]
    ppermute x2, waiting for transfers between devices: 8.3 us -> 3.74 us  [across(): return lax.ppermute(value, 'x_lo', [(0, 1), (1, 0)])]
    unnamed x12 -> x2, local copies, waits for them, and re-layouts: 4.03 us -> 0.67 us
  transfers between devices with their start and end apart: 14 -> 10, of which waited for: 5 -> 4; matrix products, arithmetic and copies ran while one was open for 0% -> 0% of each run, Pallas kernels for 1% -> 0%
where the time goes in v2:
time: 96.4 us; the launch traced here: 95.8 us
  starting transfers between devices  46 us (48%)
  blocking collectives  27.2 us (28%)
  waiting for transfers between devices  13.9 us (14%)
  Pallas kernels  7.2 us (7%)
    all_gather x1, blocking collectives, body(): pays = lax.all_gather(pay, 'z_hi')  27.2 us
    ppermute x6, starting transfers between devices, along(): return lax.ppermute(value, ('z_hi', 'z_lo', 'core'), pairs)  25.1 us
    ppermute x6, waiting for transfers between devices, along(): return lax.ppermute(value, ('z_hi', 'z_lo', 'core'), pairs)  10.2 us
    all_to_all x1, starting transfers between devices, body(): lax.all_to_all(heads, ('x_lo', 'x_hi', 'y', 'core'), 0, 0, tiled=True)  8.71 us
    pallas_call x7, Pallas kernels, local(): pl.pallas_call(kernel, out_shape=[jax.ShapeDtypeStruct(shape, dtype) for...  7.2 us
    all_to_all x1, starting transfers between devices, body(): got_q = lax.all_to_all(parts_q, 'z_hi', 0, 0, tiled=True)  6.71 us
    ppermute x2, starting transfers between devices, across(): return lax.ppermute(value, 'x_lo', [(0, 1), (1, 0)])  5.5 us
    ppermute x2, waiting for transfers between devices, across(): return lax.ppermute(value, 'x_lo', [(0, 1), (1, 0)])  3.74 us
  transfers between devices with their start and end apart: 10, of which 4 were waited for; matrix products, arithmetic and copies ran while one was open for 0% of the time, Pallas kernels for 0%

profile of v2, /device:TPU:6, one launch (start us, length us, event | category | flops | bytes accessed | tf_op | source)
XLA Modules:
  0.0 95.8 jit_solution(2452497522064181312)
XLA Ops:
  0.6 0.0 copy-start
  0.6 0.7 copy-done
  1.3 1.7 %shard_map.85 = (bf16[32,8,128]{2,1,0:T(8,128)(2,1)}, bf16[528,128]{1,0:T(8,128)(2,1)S(1)}, bf16[528,128]{1,0:T(8,128)(2,1)S(1)}) custom-call(s32[1]{0:T(128)} %bitcast.side, bf16[8,4096]{1,0:T(8,128)(2,1)} %dout.1, bf16[128,256]{1,0:T(8,128)(2,1)} %key.1, bf16[128,256]{1,0:T(8,128)(2,1)} %value.1, bf16[128,256]{1,0:T(8,128)(2,1)} %query.1, ...), custom_call_target="tpu_custom_call" | custom-call | tf_op jit(solution)/shard_map/pallas_call | solution.py:36
  3.0 2.7 %collective-permute-start = (bf16[528,128]{1,0:T(8,128)(2,1)S(1)}, bf16[528,128]{1,0:T(8,128)(2,1)S(1)}, u32[]{:S(2)}, u32[]{:S(2)}) collective-permute-start(bf16[528,128]{1,0:T(8,128)(2,1)S(1)} %get-tuple-element.18), channel_id=1, source_target_pairs={{0,256},{256,0},{1,257},{257,1},{2,258},{258,2},{3,259},{259,3},{4... | collective-permute-start | bytes 405512 | tf_op jit(solution)/shard_map/ppermute | solution.py:215
  5.8 8.7 %all-to-all-start = ((bf16[32,8,128]{2,1,0:T(8,128)(2,1)}), bf16[32,8,128]{2,1,0:T(8,128)(2,1)S(1)}, u32[]{:S(2)}, u32[]{:S(2)}) async-start(bf16[32,8,128]{2,1,0:T(8,128)(2,1)} %get-tuple-element.22), calls=%async_computation | async-start | bytes 131072 | tf_op jit(solution)/shard_map/all_to_all | solution.py:238
  14.5 0.0 collective-permute-done.got
  14.5 11.1 %collective-permute-start.3 = (bf16[512,128]{1,0:T(8,128)(2,1)S(1)}, bf16[512,128]{1,0:T(8,128)(2,1)S(1)}, u32[]{:S(2)}, u32[]{:S(2)}) collective-permute-start(bf16[512,128]{1,0:T(8,128)(2,1)S(1)} %get-tuple-element.23.keys0), channel_id=1, source_target_pairs={{0,224},{1,33},{16,240},{17,49},{32,0},{33,65},{48,16},{49,81},{64... | collective-permute-start | bytes 393224 | tf_op jit(solution)/shard_map/ppermute | solution.py:211
  25.7 2.9 %collective-permute-start.2 = (bf16[512,128]{1,0:T(8,128)(2,1)S(1)}, bf16[512,128]{1,0:T(8,128)(2,1)S(1)}, u32[]{:S(2)}, u32[]{:S(2)}) collective-permute-start(bf16[512,128]{1,0:T(8,128)(2,1)S(1)} %get-tuple-element.23.keys0), channel_id=1, source_target_pairs={{0,240},{1,17},{16,0},{17,33},{32,16},{33,49},{48,32},{49,65},{64,... | collective-permute-start | bytes 393224 | tf_op jit(solution)/shard_map/ppermute | solution.py:211
  28.6 2.9 %collective-permute-start.1 = (bf16[512,128]{1,0:T(8,128)(2,1)S(1)}, bf16[512,128]{1,0:T(8,128)(2,1)S(1)}, u32[]{:S(2)}, u32[]{:S(2)}) collective-permute-start(bf16[512,128]{1,0:T(8,128)(2,1)S(1)} %get-tuple-element.23.keys0), channel_id=1, source_target_pairs={{0,16},{1,241},{16,32},{17,1},{32,48},{33,17},{48,64},{49,33},{64,... | collective-permute-start | bytes 393224 | tf_op jit(solution)/shard_map/ppermute | solution.py:211
  31.5 0.0 all-to-all-done
  31.5 0.1 shard_map.87
  31.7 27.2 %all-gather = bf16[2112,128]{1,0:T(8,128)(2,1)S(1)} all-gather(bf16[528,128]{1,0:T(8,128)(2,1)S(1)} %shard_map.87), channel_id=2, replica_groups=mesh['x_lo'=2,'z_hi'=4,'z_lo'=4,'x_hi'=2,'y'=4,'core'=2] {'z_hi'}, dimensions={0}, use_global_device_ids=true | all-gather | bytes 675840 | tf_op jit(solution)/shard_map/all_gather | solution.py:248
  58.9 0.0 collective-permute-done.3.keys3
  58.9 0.0 collective-permute-done.2.keys2
  58.9 0.0 collective-permute-done.1.keys1
  58.9 3.3 %shard_map.88 = (bf16[4,1024,256]{2,1,0:T(8,128)(2,1)S(1)}, f32[512,128]{1,0:T(8,128)S(1)}, bf16[512,128]{1,0:T(8,128)(2,1)S(1)}, bf16[512,128]{1,0:T(8,128)(2,1)S(1)}, bf16[512,128]{1,0:T(8,128)(2,1)S(1)}) custom-call(bf16[4,528,128]{2,1,0:T(8,128)(2,1)S(1)} %bitcast.4, bf16[512,128]{1,0:T(8,128)(2,1)S(1)} %get-tuple-element.23.keys0, ...), custom_call_target="tpu_custom_call" | custom-call | tf_op jit(solution)/shard_map/pallas_call | solution.py:36
  62.2 1.2 %shard_map.89 = bf16[4,128,256]{2,1,0:T(8,128)(2,1)} custom-call(bf16[4,1024,256]{2,1,0:T(8,128)(2,1)S(1)} %get-tuple-element.24.dscores, bf16[512,128]{1,0:T(8,128)(2,1)S(1)} %get-tuple-element.23.keys0, bf16[512,128]{1,0:T(8,128)(2,1)S(1)} %collective-permute-done.1.keys1, bf16[512,128]{1,0:T(8,128)(2,1)S(1)} %collective-permute-done.2.keys2, ...), custom_call_target="tpu_custom_call" | custom-call | tf_op jit(solution)/shard_map/pallas_call | solution.py:36
  63.4 6.7 %all-to-all-start.1 = ((bf16[4,128,256]{2,1,0:T(8,128)(2,1)}), bf16[4,128,256]{2,1,0:T(8,128)(2,1)S(1)}, u32[]{:S(2)}, u32[]{:S(2)}) async-start(bf16[4,128,256]{2,1,0:T(8,128)(2,1)} %shard_map.89), calls=%async_computation.1 | async-start | bytes 524288 | tf_op jit(solution)/shard_map/all_to_all | solution.py:257
  70.1 4.3 %collective-permute-start.4 = (bf16[512,128]{1,0:T(8,128)(2,1)S(1)}, bf16[512,128]{1,0:T(8,128)(2,1)S(1)}, u32[]{:S(2)}, u32[]{:S(2)}) collective-permute-start(bf16[512,128]{1,0:T(8,128)(2,1)S(1)} %get-tuple-element.26), channel_id=1, source_target_pairs={{0,240},{1,17},{16,0},{17,33},{32,16},{33,49},{48,32},{49,65},{64,... | collective-permute-start | bytes 393224 | tf_op jit(solution)/shard_map/ppermute | solution.py:211
  74.4 1.9 %collective-permute-start.5 = (bf16[512,128]{1,0:T(8,128)(2,1)S(1)}, bf16[512,128]{1,0:T(8,128)(2,1)S(1)}, u32[]{:S(2)}, u32[]{:S(2)}) collective-permute-start(bf16[512,128]{1,0:T(8,128)(2,1)S(1)} %get-tuple-element.27), channel_id=1, source_target_pairs={{0,16},{1,241},{16,32},{17,1},{32,48},{33,17},{48,64},{49,33},{64,... | collective-permute-start | bytes 393224 | tf_op jit(solution)/shard_map/ppermute | solution.py:211
  76.4 1.9 %collective-permute-start.6 = (bf16[512,128]{1,0:T(8,128)(2,1)S(1)}, bf16[512,128]{1,0:T(8,128)(2,1)S(1)}, u32[]{:S(2)}, u32[]{:S(2)}) collective-permute-start(bf16[512,128]{1,0:T(8,128)(2,1)S(1)} %get-tuple-element.28), channel_id=1, source_target_pairs={{0,32},{1,225},{16,48},{17,241},{32,64},{33,1},{48,80},{49,17},{64... | collective-permute-start | bytes 393224 | tf_op jit(solution)/shard_map/ppermute | solution.py:211
  78.3 1.9 %collective-permute-done.4.got1 = bf16[512,128]{1,0:T(8,128)(2,1)S(1)} collective-permute-done((bf16[512,128]{1,0:T(8,128)(2,1)S(1)}, bf16[512,128]{1,0:T(8,128)(2,1)S(1)}, u32[]{:S(2)}, u32[]{:S(2)}) %collective-permute-start.4) | collective-permute-done | bytes 131104 | tf_op jit(solution)/shard_map/ppermute | solution.py:211
  80.2 5.0 %collective-permute-done.5.got2 = bf16[512,128]{1,0:T(8,128)(2,1)S(1)} collective-permute-done((bf16[512,128]{1,0:T(8,128)(2,1)S(1)}, bf16[512,128]{1,0:T(8,128)(2,1)S(1)}, u32[]{:S(2)}, u32[]{:S(2)}) %collective-permute-start.5) | collective-permute-done | bytes 131104 | tf_op jit(solution)/shard_map/ppermute | solution.py:211
  85.2 3.2 %collective-permute-done.6.got3 = bf16[512,128]{1,0:T(8,128)(2,1)S(1)} collective-permute-done((bf16[512,128]{1,0:T(8,128)(2,1)S(1)}, bf16[512,128]{1,0:T(8,128)(2,1)S(1)}, u32[]{:S(2)}, u32[]{:S(2)}) %collective-permute-start.6) | collective-permute-done | bytes 131104 | tf_op jit(solution)/shard_map/ppermute | solution.py:211
  88.5 0.0 all-to-all-done.1.got_q
  88.5 0.1 shard_map.90
  88.6 2.8 %collective-permute-start.7 = (bf16[384,128]{1,0:T(8,128)(2,1)S(1)}, bf16[384,128]{1,0:T(8,128)(2,1)S(1)}, u32[]{:S(2)}, u32[]{:S(2)}) collective-permute-start(bf16[384,128]{1,0:T(8,128)(2,1)S(1)} %get-tuple-element.30), channel_id=1, source_target_pairs={{0,256},{256,0},{1,257},{257,1},{2,258},{258,2},{3,259},{259,3},{4... | collective-permute-start | bytes 294920 | tf_op jit(solution)/shard_map/ppermute | solution.py:215
  91.4 3.7 %collective-permute-done.7.got = bf16[384,128]{1,0:T(8,128)(2,1)S(1)} collective-permute-done((bf16[384,128]{1,0:T(8,128)(2,1)S(1)}, bf16[384,128]{1,0:T(8,128)(2,1)S(1)}, u32[]{:S(2)}, u32[]{:S(2)}) %collective-permute-start.7) | collective-permute-done | bytes 98336 | tf_op jit(solution)/shard_map/ppermute | solution.py:215
  95.1 0.7 shard_map.91
  (1 shorter events, 0.0 us)
Async XLA Ops:
  0.6 0.7 copy-start
  3.0 11.5 %collective-permute-start = (bf16[528,128]{1,0:T(8,128)(2,1)S(1)}, bf16[528,128]{1,0:T(8,128)(2,1)S(1)}, u32[]{:S(2)}, u32[]{:S(2)}) collective-permute-start(bf16[528,128]{1,0:T(8,128)(2,1)S(1)} %get-tuple-element.18), channel_id=1, source_target_pairs={{0,256},{256,0},{1,257},{257,1},{2,258},{258,2},{3,259},{259,3},{4... | collective-permute-start | bytes 405512 | tf_op jit(solution)/shard_map/ppermute | solution.py:215
  5.8 25.8 %all-to-all-start = ((bf16[32,8,128]{2,1,0:T(8,128)(2,1)}), bf16[32,8,128]{2,1,0:T(8,128)(2,1)S(1)}, u32[]{:S(2)}, u32[]{:S(2)}) async-start(bf16[32,8,128]{2,1,0:T(8,128)(2,1)} %get-tuple-element.22), calls=%async_computation | async-start | bytes 131072 | tf_op jit(solution)/shard_map/all_to_all | solution.py:238
  14.5 44.4 %collective-permute-start.3 = (bf16[512,128]{1,0:T(8,128)(2,1)S(1)}, bf16[512,128]{1,0:T(8,128)(2,1)S(1)}, u32[]{:S(2)}, u32[]{:S(2)}) collective-permute-start(bf16[512,128]{1,0:T(8,128)(2,1)S(1)} %get-tuple-element.23.keys0), channel_id=1, source_target_pairs={{0,224},{1,33},{16,240},{17,49},{32,0},{33,65},{48,16},{49,81},{64... | collective-permute-start | bytes 393224 | tf_op jit(solution)/shard_map/ppermute | solution.py:211
  25.7 33.2 %collective-permute-start.2 = (bf16[512,128]{1,0:T(8,128)(2,1)S(1)}, bf16[512,128]{1,0:T(8,128)(2,1)S(1)}, u32[]{:S(2)}, u32[]{:S(2)}) collective-permute-start(bf16[512,128]{1,0:T(8,128)(2,1)S(1)} %get-tuple-element.23.keys0), channel_id=1, source_target_pairs={{0,240},{1,17},{16,0},{17,33},{32,16},{33,49},{48,32},{49,65},{64,... | collective-permute-start | bytes 393224 | tf_op jit(solution)/shard_map/ppermute | solution.py:211
  28.6 30.3 %collective-permute-start.1 = (bf16[512,128]{1,0:T(8,128)(2,1)S(1)}, bf16[512,128]{1,0:T(8,128)(2,1)S(1)}, u32[]{:S(2)}, u32[]{:S(2)}) collective-permute-start(bf16[512,128]{1,0:T(8,128)(2,1)S(1)} %get-tuple-element.23.keys0), channel_id=1, source_target_pairs={{0,16},{1,241},{16,32},{17,1},{32,48},{33,17},{48,64},{49,33},{64,... | collective-permute-start | bytes 393224 | tf_op jit(solution)/shard_map/ppermute | solution.py:211
  63.4 25.0 %all-to-all-start.1 = ((bf16[4,128,256]{2,1,0:T(8,128)(2,1)}), bf16[4,128,256]{2,1,0:T(8,128)(2,1)S(1)}, u32[]{:S(2)}, u32[]{:S(2)}) async-start(bf16[4,128,256]{2,1,0:T(8,128)(2,1)} %shard_map.89), calls=%async_computation.1 | async-start | bytes 524288 | tf_op jit(solution)/shard_map/all_to_all | solution.py:257
  70.1 10.0 %collective-permute-start.4 = (bf16[512,128]{1,0:T(8,128)(2,1)S(1)}, bf16[512,128]{1,0:T(8,128)(2,1)S(1)}, u32[]{:S(2)}, u32[]{:S(2)}) collective-permute-start(bf16[512,128]{1,0:T(8,128)(2,1)S(1)} %get-tuple-element.26), channel_id=1, source_target_pairs={{0,240},{1,17},{16,0},{17,33},{32,16},{33,49},{48,32},{49,65},{64,... | collective-permute-start | bytes 393224 | tf_op jit(solution)/shard_map/ppermute | solution.py:211
  74.4 10.8 %collective-permute-start.5 = (bf16[512,128]{1,0:T(8,128)(2,1)S(1)}, bf16[512,128]{1,0:T(8,128)(2,1)S(1)}, u32[]{:S(2)}, u32[]{:S(2)}) collective-permute-start(bf16[512,128]{1,0:T(8,128)(2,1)S(1)} %get-tuple-element.27), channel_id=1, source_target_pairs={{0,16},{1,241},{16,32},{17,1},{32,48},{33,17},{48,64},{49,33},{64,... | collective-permute-start | bytes 393224 | tf_op jit(solution)/shard_map/ppermute | solution.py:211
  76.4 12.1 %collective-permute-start.6 = (bf16[512,128]{1,0:T(8,128)(2,1)S(1)}, bf16[512,128]{1,0:T(8,128)(2,1)S(1)}, u32[]{:S(2)}, u32[]{:S(2)}) collective-permute-start(bf16[512,128]{1,0:T(8,128)(2,1)S(1)} %get-tuple-element.28), channel_id=1, source_target_pairs={{0,32},{1,225},{16,48},{17,241},{32,64},{33,1},{48,80},{49,17},{64... | collective-permute-start | bytes 393224 | tf_op jit(solution)/shard_map/ppermute | solution.py:211
  88.6 6.5 %collective-permute-start.7 = (bf16[384,128]{1,0:T(8,128)(2,1)S(1)}, bf16[384,128]{1,0:T(8,128)(2,1)S(1)}, u32[]{:S(2)}, u32[]{:S(2)}) collective-permute-start(bf16[384,128]{1,0:T(8,128)(2,1)S(1)} %get-tuple-element.30), channel_id=1, source_target_pairs={{0,256},{256,0},{1,257},{257,1},{2,258},{258,2},{3,259},{259,3},{4... | collective-permute-start | bytes 294920 | tf_op jit(solution)/shard_map/ppermute | solution.py:215

commit v3 on v2

v3 whole, which is shorter than its diff:
```python
import functools
import math

import jax
import jax.numpy as jnp
from jax import lax
from jax.experimental import pallas as pl
from jax.experimental.pallas import tpu as pltpu
from jax.sharding import Mesh, PartitionSpec as P

HD = 128
TOK = 128
ROWS = 2 * TOK
AUX = 16
PAY = 2 * ROWS + AUX
RING = 16
LOG2E = math.log2(math.e)
FACTOR = 1.0 / math.sqrt(HD)
BF = jnp.bfloat16
F32 = jnp.float32
KEYS = 4 * ROWS
CHUNK = 512
LONG = pl.CostEstimate(flops=10**11, bytes_accessed=10**8, transcendentals=0)
K_STEPS = (1, -1, -2)
GROUP = 4


def pieces(value):
    high = value.astype(BF)
    rest = value - high.astype(F32)
    mid = rest.astype(BF)
    low = (rest - mid.astype(F32)).astype(BF)
    return [high.astype(F32), mid.astype(F32), low.astype(F32)]


def local(kernel, outs, *args, far=(), scratch=(), cost=None):
    scalars = [pl.BlockSpec(memory_space=pltpu.SMEM)]
    whole = [pl.BlockSpec(memory_space=pltpu.VMEM)]
    return pl.pallas_call(
        kernel,
        out_shape=[jax.ShapeDtypeStruct(shape, dtype) for shape, dtype in outs],
        in_specs=[
            pl.BlockSpec(memory_space=pltpu.HBM)
            if at in far
            else (scalars if arg.dtype == jnp.int32 else whole)[0]
            for at, arg in enumerate(args)
        ],
        out_specs=whole * len(outs),
        scratch_shapes=list(scratch),
        cost_estimate=cost,
        compiler_params=pltpu.CompilerParams(vmem_limit_bytes=48 * 1024 * 1024),
    )(*args)


def split_kernel(
    side, dout, key, value, query, out, lnorm, heads, keep, send, dout_in, rows_in, norm_in, dout_sem, rows_sem, norm_sem
):
    load = pltpu.make_async_copy(dout, dout_in, dout_sem)
    load.start()
    norm_load = pltpu.make_async_copy(lnorm, norm_in, norm_sem)
    norm_load.start()
    loads = []
    for slot, rows in enumerate((key, value, query, out)):
        loads.append(pltpu.make_async_copy(rows, rows_in.at[slot], rows_sem.at[slot]))
        loads[-1].start()
    load.wait()
    for head in range(32):
        heads[(head % 2) * 16 + head // 2] = dout_in[:, head * HD : (head + 1) * HD]
    for each in loads:
        each.wait()
    norm_load.wait()

    def put(mine, other):
        for slot in range(4):
            at = slice(slot * TOK, (slot + 1) * TOK)
            keep[at, :] = rows_in[slot, :, mine * HD : (mine + 1) * HD]
            send[at, :] = rows_in[slot, :, other * HD : (other + 1) * HD]
        for head, dest in ((mine, keep), (other, send)):
            norm = norm_in[head : head + 1, :] * LOG2E
            blank = jnp.zeros((AUX - 3, TOK), F32)
            dest[4 * TOK :, :] = jnp.concatenate(pieces(norm) + [blank], axis=0).astype(BF)

    @pl.when(side[0] == 0)
    def _():
        put(0, 1)

    @pl.when(side[0] != 0)
    def _():
        put(1, 0)


def merge_kernel(side, keep, got, keys, query, out, norm):
    for slot in range(2):
        rows = slice(slot * TOK, (slot + 1) * TOK)
        keys[slot * ROWS : slot * ROWS + TOK, :] = keep[rows, :]
        keys[slot * ROWS + TOK : (slot + 1) * ROWS, :] = got[rows, :]

    def put(first, second):
        for slot, dest in ((2, query), (3, out)):
            rows = slice(slot * TOK, (slot + 1) * TOK)
            dest[:TOK, :] = first[rows, :]
            dest[TOK:, :] = second[rows, :]
        norm[:AUX, :] = first[4 * TOK :, :]
        norm[AUX:, :] = second[4 * TOK :, :]

    @pl.when(side[0] == 0)
    def _():
        put(keep, got)

    @pl.when(side[0] != 0)
    def _():
        put(got, keep)


def delta_kernel(query, out, norm, dout, pay):
    pay[:ROWS, :] = query[...]
    pay[ROWS : 2 * ROWS, :] = dout[...]
    product = dout[...].astype(F32) * out[...].astype(F32)
    delta = jnp.sum(product.T, axis=0, keepdims=True)
    first = norm[:AUX, :].astype(F32)
    second = norm[AUX:, :].astype(F32)
    rows = (
        [first[:3, :], second[:3, :]]
        + pieces(delta[:, :TOK])
        + pieces(delta[:, TOK:])
        + [jnp.zeros((AUX - 12, TOK), F32)]
    )
    pay[2 * ROWS :, :] = jnp.concatenate(rows, axis=0).astype(BF)


def dot(left, right, left_dim, right_dim):
    return lax.dot_general(
        left, right, (((left_dim,), (right_dim,)), ((), ())), preferred_element_type=F32
    )


def row_of(aux, at):
    first = aux[at : at + 1, :] + aux[at + 1 : at + 2, :] + aux[at + 2 : at + 3, :]
    second = aux[at + 3 : at + 4, :] + aux[at + 4 : at + 5, :] + aux[at + 5 : at + 6, :]
    return jnp.concatenate([first, second], axis=1)


def pairs_kernel(
    pays, keys0, keys1, keys2, keys3, grads_q, own, send, keys, values, sum_k, sum_v
):
    for slot, shard in enumerate((keys0, keys1, keys2, keys3)):
        rows = slice(slot * ROWS, (slot + 1) * ROWS)
        keys[rows, :] = shard[:ROWS, :]
        values[rows, :] = shard[ROWS:, :]
    for block in range(GROUP):
        query = pays[block, :ROWS, :]
        dout = pays[block, ROWS : 2 * ROWS, :]
        aux = pays[block, 2 * ROWS :, :].astype(F32)
        norm, delta = row_of(aux, 0), row_of(aux, 6)
        grad_q = None
        for at in range(0, KEYS, CHUNK):
            rows = slice(at, at + CHUNK)
            key = keys[rows, :]
            probs = jnp.exp2(dot(key, query, 1, 1) * (FACTOR * LOG2E) - norm)
            dprobs = dot(values[rows, :], dout, 1, 1)
            dscore = (probs * (dprobs - delta)).astype(BF)
            part_v = dot(probs.astype(BF), dout, 1, 0)
            part_k = dot(dscore, query, 1, 0)
            part_q = dot(key, dscore, 0, 0)
            if block == 0:
                sum_k[rows, :] = part_k
                sum_v[rows, :] = part_v
            else:
                sum_k[rows, :] += part_k
                sum_v[rows, :] += part_v
            grad_q = part_q if at == 0 else grad_q + part_q
        grad_q = (grad_q * FACTOR).astype(BF)
        grads_q[block] = grad_q[:, :TOK]
        grads_q[GROUP + block] = grad_q[:, TOK:]
    for slot in range(GROUP):
        for half, dest in enumerate((own, send)):
            rows = slice(slot * ROWS + half * TOK, slot * ROWS + (half + 1) * TOK)
            dest[slot, :TOK, :] = (sum_k[rows, :] * FACTOR).astype(dest.dtype)
            dest[slot, TOK:, :] = sum_v[rows, :].astype(dest.dtype)


def fold_kernel(own, got, total, send1, send2, send3):
    for slot, dest in enumerate((total, send1, send2, send3)):
        dest[:, :HD] = own[slot].astype(dest.dtype)
        dest[:, HD:] = got[slot].astype(dest.dtype)


def join_kernel(side, parts_q, total, got1, got2, got3, grad_q, grad_k, grad_v):
    for head in range(2):
        sum_q = parts_q[head * GROUP].astype(F32)
        for at in range(1, GROUP):
            sum_q += parts_q[head * GROUP + at].astype(F32)
        grad_q[:, head * HD : (head + 1) * HD] = sum_q.T.astype(BF)
    sum_kv = total[...]
    for got in (got1, got2, got3):
        sum_kv += got[...].astype(F32)
    sum_kv = sum_kv.astype(BF)

    def put(first, second):
        for at, dest in enumerate((grad_k, grad_v)):
            rows = slice(at * TOK, (at + 1) * TOK)
            dest[:, :HD] = sum_kv[rows, first * HD : (first + 1) * HD]
            dest[:, HD:] = sum_kv[rows, second * HD : (second + 1) * HD]

    @pl.when(side[0] == 0)
    def _():
        put(0, 1)

    @pl.when(side[0] != 0)
    def _():
        put(1, 0)


def along(value, steps):
    pairs = []
    for at in range(RING):
        for core, shift in enumerate((steps, -steps)):
            pairs.append((2 * at + core, 2 * ((at + shift) % RING) + core))
    return lax.ppermute(value, ("z_hi", "z_lo", "core"), pairs)


def across(value):
    return lax.ppermute(value, "x_lo", [(0, 1), (1, 0)])


def body(query_rows, key_rows, value_rows, output_rows, grad_output, log_norm):
    side = lax.axis_index("x_lo").astype(jnp.int32).reshape(1)
    swap = ((4 * TOK + AUX, HD), BF)
    heads, keep, send = local(
        split_kernel,
        [((32, 8, HD), BF), swap, swap],
        side,
        *[
            pltpu.with_memory_space_constraint(rows, pltpu.HBM)
            for rows in (grad_output, key_rows, value_rows, query_rows, output_rows, log_norm.T)
        ],
        far=range(1, 7),
        scratch=(
            pltpu.VMEM((8, 32 * HD), BF),
            pltpu.VMEM((4, TOK, 2 * HD), BF),
            pltpu.VMEM((2, TOK), F32),
            pltpu.SemaphoreType.DMA,
            pltpu.SemaphoreType.DMA((4,)),
            pltpu.SemaphoreType.DMA,
        ),
    )
    dout = lax.all_to_all(heads, ("x_lo", "x_hi", "y", "core"), 0, 0, tiled=True)
    dout = dout.reshape(ROWS, HD)
    got = across(send)
    block = ((ROWS, HD), BF)
    pair = ((2 * ROWS, HD), BF)
    keys, query, out, norm = local(
        merge_kernel, [pair, block, block, ((2 * AUX, HD), BF)], side, keep, got
    )
    all_keys = [keys] + [along(keys, step) for step in K_STEPS]
    (pay,) = local(delta_kernel, [((PAY, HD), BF)], query, out, norm, dout)
    pays = lax.all_gather(pay, "z_hi")
    shards = ((GROUP, ROWS, HD), BF)
    parts_q, own, send = local(
        pairs_kernel,
        [((2 * GROUP, HD, TOK), BF), (shards[0], F32), shards],
        pays,
        *all_keys,
        scratch=(pltpu.VMEM((KEYS, HD), BF),) * 2 + (pltpu.VMEM((KEYS, HD), F32),) * 2,
    )
    got = across(send)
    parts_q = lax.all_to_all(parts_q, ("x_lo", "z_hi"), 0, 0, tiled=True)
    wide = ((ROWS, 2 * HD), BF)
    total, *sends = local(
        fold_kernel, [(wide[0], F32)] + [wide] * 3, own, got, cost=LONG
    )
    gots = [along(part, -step) for part, step in zip(sends, K_STEPS)]
    return tuple(
        local(join_kernel, [((TOK, 2 * HD), BF)] * 3, side, parts_q, total, *gots)
    )


def solution(mesh):
    fine = Mesh(
        mesh.devices.reshape(2, 4, 4, 2, 4, 2), ("x_lo", "z_hi", "z_lo", "x_hi", "y", "core")
    )
    blk, uly = ("x_lo", "z_hi", "z_lo"), ("x_hi", "y", "core")
    placed = P(blk, uly)
    return jax.shard_map(
        body,
        mesh=fine,
        in_specs=(placed, placed, placed, placed, P(blk + uly, None), placed),
        out_specs=(placed, placed, placed),
        check_vma=False,
    )
```

time: 96.4 us -> 92 us (0.954)
  waiting for transfers between devices: 13.9 us -> 10.1 us
  starting transfers between devices: 46 us -> 47.1 us
    ppermute x2, waiting for transfers between devices: 3.74 us -> 0.01 us  [across(): return lax.ppermute(value, 'x_lo', [(0, 1), (1, 0)])]
    all_to_all x1, starting transfers between devices: 6.71 us -> 8.18 us  [body(): parts_q = lax.all_to_all(parts_q, ('x_lo', 'z_hi'), 0, 0, tiled=True)]
    pallas_call x7 -> x6, Pallas kernels: 7.2 us -> 6.33 us  [local(): pl.pallas_call(kernel, out_shape=[jax.ShapeDtypeStruct(shape, dtype) for...]
  transfers between devices with their start and end apart: 10 -> 10, of which waited for: 4 -> 3; matrix products, arithmetic and copies ran while one was open for 0% -> 0% of each run, Pallas kernels for 0% -> 0%
where the time goes in v3:
time: 92 us; the launch traced here: 91.5 us
  starting transfers between devices  47.1 us (51%)
  blocking collectives  27.2 us (30%)
  waiting for transfers between devices  10.1 us (11%)
  Pallas kernels  6.33 us (7%)
    all_gather x1, blocking collectives, body(): pays = lax.all_gather(pay, 'z_hi')  27.2 us
    ppermute x6, starting transfers between devices, along(): return lax.ppermute(value, ('z_hi', 'z_lo', 'core'), pairs)  24.7 us
    ppermute x6, waiting for transfers between devices, along(): return lax.ppermute(value, ('z_hi', 'z_lo', 'core'), pairs)  10.1 us
    all_to_all x1, starting transfers between devices, body(): lax.all_to_all(heads, ('x_lo', 'x_hi', 'y', 'core'), 0, 0, tiled=True)  8.71 us
    all_to_all x1, starting transfers between devices, body(): parts_q = lax.all_to_all(parts_q, ('x_lo', 'z_hi'), 0, 0, tiled=True)  8.18 us
    pallas_call x6, Pallas kernels, local(): pl.pallas_call(kernel, out_shape=[jax.ShapeDtypeStruct(shape, dtype) for...  6.33 us
    ppermute x2, starting transfers between devices, across(): return lax.ppermute(value, 'x_lo', [(0, 1), (1, 0)])  5.45 us
  transfers between devices with their start and end apart: 10, of which 3 were waited for; matrix products, arithmetic and copies ran while one was open for 0% of the time, Pallas kernels for 0%

profile of v3, /device:TPU:6, one launch (start us, length us, event | category | flops | bytes accessed | tf_op | source)
XLA Modules:
  0.0 91.5 jit_solution(16212527315157514600)
XLA Ops:
  0.6 1.7 %shard_map.85 = (bf16[32,8,128]{2,1,0:T(8,128)(2,1)}, bf16[528,128]{1,0:T(8,128)(2,1)S(1)}, bf16[528,128]{1,0:T(8,128)(2,1)S(1)}) custom-call(s32[1]{0:T(128)} %bitcast.side, bf16[8,4096]{1,0:T(8,128)(2,1)} %dout.1, bf16[128,256]{1,0:T(8,128)(2,1)} %key.1, bf16[128,256]{1,0:T(8,128)(2,1)} %value.1, bf16[128,256]{1,0:T(8,128)(2,1)} %query.1, ...), custom_call_target="tpu_custom_call" | custom-call | tf_op jit(solution)/shard_map/pallas_call | solution.py:39
  2.4 2.7 %collective-permute-start = (bf16[528,128]{1,0:T(8,128)(2,1)S(1)}, bf16[528,128]{1,0:T(8,128)(2,1)S(1)}, u32[]{:S(2)}, u32[]{:S(2)}) collective-permute-start(bf16[528,128]{1,0:T(8,128)(2,1)S(1)} %get-tuple-element.18), channel_id=1, source_target_pairs={{0,256},{256,0},{1,257},{257,1},{2,258},{258,2},{3,259},{259,3},{4... | collective-permute-start | bytes 405512 | tf_op jit(solution)/shard_map/ppermute | solution.py:223
  5.1 8.7 %all-to-all-start = ((bf16[32,8,128]{2,1,0:T(8,128)(2,1)}), bf16[32,8,128]{2,1,0:T(8,128)(2,1)S(1)}, u32[]{:S(2)}, u32[]{:S(2)}) async-start(bf16[32,8,128]{2,1,0:T(8,128)(2,1)} %get-tuple-element.22), calls=%async_computation | async-start | bytes 131072 | tf_op jit(solution)/shard_map/all_to_all | solution.py:247
  13.8 0.0 collective-permute-done.got
  13.9 11.1 %collective-permute-start.3 = (bf16[512,128]{1,0:T(8,128)(2,1)S(1)}, bf16[512,128]{1,0:T(8,128)(2,1)S(1)}, u32[]{:S(2)}, u32[]{:S(2)}) collective-permute-start(bf16[512,128]{1,0:T(8,128)(2,1)S(1)} %get-tuple-element.23.keys0), channel_id=1, source_target_pairs={{0,224},{1,33},{16,240},{17,49},{32,0},{33,65},{48,16},{49,81},{64... | collective-permute-start | bytes 393224 | tf_op jit(solution)/shard_map/ppermute | solution.py:219
  25.0 2.9 %collective-permute-start.2 = (bf16[512,128]{1,0:T(8,128)(2,1)S(1)}, bf16[512,128]{1,0:T(8,128)(2,1)S(1)}, u32[]{:S(2)}, u32[]{:S(2)}) collective-permute-start(bf16[512,128]{1,0:T(8,128)(2,1)S(1)} %get-tuple-element.23.keys0), channel_id=1, source_target_pairs={{0,240},{1,17},{16,0},{17,33},{32,16},{33,49},{48,32},{49,65},{64,... | collective-permute-start | bytes 393224 | tf_op jit(solution)/shard_map/ppermute | solution.py:219
  27.9 2.9 %collective-permute-start.1 = (bf16[512,128]{1,0:T(8,128)(2,1)S(1)}, bf16[512,128]{1,0:T(8,128)(2,1)S(1)}, u32[]{:S(2)}, u32[]{:S(2)}) collective-permute-start(bf16[512,128]{1,0:T(8,128)(2,1)S(1)} %get-tuple-element.23.keys0), channel_id=1, source_target_pairs={{0,16},{1,241},{16,32},{17,1},{32,48},{33,17},{48,64},{49,33},{64,... | collective-permute-start | bytes 393224 | tf_op jit(solution)/shard_map/ppermute | solution.py:219
  30.9 0.0 all-to-all-done
  30.9 0.1 shard_map.87
  31.0 27.2 %all-gather = bf16[2112,128]{1,0:T(8,128)(2,1)S(1)} all-gather(bf16[528,128]{1,0:T(8,128)(2,1)S(1)} %shard_map.87), channel_id=2, replica_groups=mesh['x_lo'=2,'z_hi'=4,'z_lo'=4,'x_hi'=2,'y'=4,'core'=2] {'z_hi'}, dimensions={0}, use_global_device_ids=true | all-gather | bytes 675840 | tf_op jit(solution)/shard_map/all_gather | solution.py:257
  58.2 0.0 collective-permute-done.3.keys3
  58.2 0.0 collective-permute-done.2.keys2
  58.2 0.0 collective-permute-done.1.keys1
  58.2 3.6 %shard_map.88 = (bf16[8,128,128]{2,1,0:T(8,128)(2,1)}, f32[4,256,128]{2,1,0:T(8,128)S(1)}, bf16[4,256,128]{2,1,0:T(8,128)(2,1)S(1)}) custom-call(bf16[4,528,128]{2,1,0:T(8,128)(2,1)S(1)} %bitcast.4, bf16[512,128]{1,0:T(8,128)(2,1)S(1)} %get-tuple-element.23.keys0, bf16[512,128]{1,0:T(8,128)(2,1)S(1)} %collective-permute-done.1.keys1, ...), custom_call_target="tpu_custom_call" | custom-call | tf_op jit(solution)/shard_map/pallas_call | solution.py:39
  61.8 2.7 %collective-permute-start.4 = (bf16[4,256,128]{2,1,0:T(8,128)(2,1)S(1)}, bf16[4,256,128]{2,1,0:T(8,128)(2,1)S(1)}, u32[]{:S(2)}, u32[]{:S(2)}) collective-permute-start(bf16[4,256,128]{2,1,0:T(8,128)(2,1)S(1)} %get-tuple-element.26), channel_id=1, source_target_pairs={{0,256},{256,0},{1,257},{257,1},{2,258},{258,2},{3,259},{259,3},{4... | collective-permute-start | bytes 786440 | tf_op jit(solution)/shard_map/ppermute | solution.py:223
  64.5 8.2 %all-to-all-start.1 = ((bf16[8,128,128]{2,1,0:T(8,128)(2,1)}), bf16[8,128,128]{2,1,0:T(8,128)(2,1)S(1)}, u32[]{:S(2)}, u32[]{:S(2)}) async-start(bf16[8,128,128]{2,1,0:T(8,128)(2,1)} %get-tuple-element.24), calls=%async_computation.1 | async-start | bytes 524288 | tf_op jit(solution)/shard_map/all_to_all | solution.py:267
  72.7 0.0 collective-permute-done.4.got
  72.7 0.1 shard_map.89
  72.8 3.7 %collective-permute-start.5 = (bf16[256,256]{1,0:T(8,128)(2,1)S(1)}, bf16[256,256]{1,0:T(8,128)(2,1)S(1)}, u32[]{:S(2)}, u32[]{:S(2)}) collective-permute-start(bf16[256,256]{1,0:T(8,128)(2,1)S(1)} %get-tuple-element.28), channel_id=1, source_target_pairs={{0,240},{1,17},{16,0},{17,33},{32,16},{33,49},{48,32},{49,65},{64,... | collective-permute-start | bytes 393224 | tf_op jit(solution)/shard_map/ppermute | solution.py:219
  76.6 2.1 %collective-permute-start.6 = (bf16[256,256]{1,0:T(8,128)(2,1)S(1)}, bf16[256,256]{1,0:T(8,128)(2,1)S(1)}, u32[]{:S(2)}, u32[]{:S(2)}) collective-permute-start(bf16[256,256]{1,0:T(8,128)(2,1)S(1)} %get-tuple-element.29), channel_id=1, source_target_pairs={{0,16},{1,241},{16,32},{17,1},{32,48},{33,17},{48,64},{49,33},{64,... | collective-permute-start | bytes 393224 | tf_op jit(solution)/shard_map/ppermute | solution.py:219
  78.7 1.9 %collective-permute-start.7 = (bf16[256,256]{1,0:T(8,128)(2,1)S(1)}, bf16[256,256]{1,0:T(8,128)(2,1)S(1)}, u32[]{:S(2)}, u32[]{:S(2)}) collective-permute-start(bf16[256,256]{1,0:T(8,128)(2,1)S(1)} %get-tuple-element.30), channel_id=1, source_target_pairs={{0,32},{1,225},{16,48},{17,241},{32,64},{33,1},{48,80},{49,17},{64... | collective-permute-start | bytes 393224 | tf_op jit(solution)/shard_map/ppermute | solution.py:219
  80.6 2.1 %collective-permute-done.5.got1 = bf16[256,256]{1,0:T(8,128)(2,1)S(1)} collective-permute-done((bf16[256,256]{1,0:T(8,128)(2,1)S(1)}, bf16[256,256]{1,0:T(8,128)(2,1)S(1)}, u32[]{:S(2)}, u32[]{:S(2)}) %collective-permute-start.5) | collective-permute-done | bytes 131104 | tf_op jit(solution)/shard_map/ppermute | solution.py:219
  82.7 5.4 %collective-permute-done.6.got2 = bf16[256,256]{1,0:T(8,128)(2,1)S(1)} collective-permute-done((bf16[256,256]{1,0:T(8,128)(2,1)S(1)}, bf16[256,256]{1,0:T(8,128)(2,1)S(1)}, u32[]{:S(2)}, u32[]{:S(2)}) %collective-permute-start.6) | collective-permute-done | bytes 131104 | tf_op jit(solution)/shard_map/ppermute | solution.py:219
  88.1 2.6 %collective-permute-done.7.got3 = bf16[256,256]{1,0:T(8,128)(2,1)S(1)} collective-permute-done((bf16[256,256]{1,0:T(8,128)(2,1)S(1)}, bf16[256,256]{1,0:T(8,128)(2,1)S(1)}, u32[]{:S(2)}, u32[]{:S(2)}) %collective-permute-start.7) | collective-permute-done | bytes 131104 | tf_op jit(solution)/shard_map/ppermute | solution.py:219
  90.6 0.0 all-to-all-done.1.parts_q
  90.6 0.8 shard_map.90
  (1 shorter events, 0.0 us)
Async XLA Ops:
  2.4 11.5 %collective-permute-start = (bf16[528,128]{1,0:T(8,128)(2,1)S(1)}, bf16[528,128]{1,0:T(8,128)(2,1)S(1)}, u32[]{:S(2)}, u32[]{:S(2)}) collective-permute-start(bf16[528,128]{1,0:T(8,128)(2,1)S(1)} %get-tuple-element.18), channel_id=1, source_target_pairs={{0,256},{256,0},{1,257},{257,1},{2,258},{258,2},{3,259},{259,3},{4... | collective-permute-start | bytes 405512 | tf_op jit(solution)/shard_map/ppermute | solution.py:223
  5.1 25.8 %all-to-all-start = ((bf16[32,8,128]{2,1,0:T(8,128)(2,1)}), bf16[32,8,128]{2,1,0:T(8,128)(2,1)S(1)}, u32[]{:S(2)}, u32[]{:S(2)}) async-start(bf16[32,8,128]{2,1,0:T(8,128)(2,1)} %get-tuple-element.22), calls=%async_computation | async-start | bytes 131072 | tf_op jit(solution)/shard_map/all_to_all | solution.py:247
  13.9 44.4 %collective-permute-start.3 = (bf16[512,128]{1,0:T(8,128)(2,1)S(1)}, bf16[512,128]{1,0:T(8,128)(2,1)S(1)}, u32[]{:S(2)}, u32[]{:S(2)}) collective-permute-start(bf16[512,128]{1,0:T(8,128)(2,1)S(1)} %get-tuple-element.23.keys0), channel_id=1, source_target_pairs={{0,224},{1,33},{16,240},{17,49},{32,0},{33,65},{48,16},{49,81},{64... | collective-permute-start | bytes 393224 | tf_op jit(solution)/shard_map/ppermute | solution.py:219
  25.0 33.2 %collective-permute-start.2 = (bf16[512,128]{1,0:T(8,128)(2,1)S(1)}, bf16[512,128]{1,0:T(8,128)(2,1)S(1)}, u32[]{:S(2)}, u32[]{:S(2)}) collective-permute-start(bf16[512,128]{1,0:T(8,128)(2,1)S(1)} %get-tuple-element.23.keys0), channel_id=1, source_target_pairs={{0,240},{1,17},{16,0},{17,33},{32,16},{33,49},{48,32},{49,65},{64,... | collective-permute-start | bytes 393224 | tf_op jit(solution)/shard_map/ppermute | solution.py:219
  27.9 30.3 %collective-permute-start.1 = (bf16[512,128]{1,0:T(8,128)(2,1)S(1)}, bf16[512,128]{1,0:T(8,128)(2,1)S(1)}, u32[]{:S(2)}, u32[]{:S(2)}) collective-permute-start(bf16[512,128]{1,0:T(8,128)(2,1)S(1)} %get-tuple-element.23.keys0), channel_id=1, source_target_pairs={{0,16},{1,241},{16,32},{17,1},{32,48},{33,17},{48,64},{49,33},{64,... | collective-permute-start | bytes 393224 | tf_op jit(solution)/shard_map/ppermute | solution.py:219
  61.8 10.9 %collective-permute-start.4 = (bf16[4,256,128]{2,1,0:T(8,128)(2,1)S(1)}, bf16[4,256,128]{2,1,0:T(8,128)(2,1)S(1)}, u32[]{:S(2)}, u32[]{:S(2)}) collective-permute-start(bf16[4,256,128]{2,1,0:T(8,128)(2,1)S(1)} %get-tuple-element.26), channel_id=1, source_target_pairs={{0,256},{256,0},{1,257},{257,1},{2,258},{258,2},{3,259},{259,3},{4... | collective-permute-start | bytes 786440 | tf_op jit(solution)/shard_map/ppermute | solution.py:223
  64.5 26.1 %all-to-all-start.1 = ((bf16[8,128,128]{2,1,0:T(8,128)(2,1)}), bf16[8,128,128]{2,1,0:T(8,128)(2,1)S(1)}, u32[]{:S(2)}, u32[]{:S(2)}) async-start(bf16[8,128,128]{2,1,0:T(8,128)(2,1)} %get-tuple-element.24), calls=%async_computation.1 | async-start | bytes 524288 | tf_op jit(solution)/shard_map/all_to_all | solution.py:267
  72.8 9.9 %collective-permute-start.5 = (bf16[256,256]{1,0:T(8,128)(2,1)S(1)}, bf16[256,256]{1,0:T(8,128)(2,1)S(1)}, u32[]{:S(2)}, u32[]{:S(2)}) collective-permute-start(bf16[256,256]{1,0:T(8,128)(2,1)S(1)} %get-tuple-element.28), channel_id=1, source_target_pairs={{0,240},{1,17},{16,0},{17,33},{32,16},{33,49},{48,32},{49,65},{64,... | collective-permute-start | bytes 393224 | tf_op jit(solution)/shard_map/ppermute | solution.py:219
  76.6 11.5 %collective-permute-start.6 = (bf16[256,256]{1,0:T(8,128)(2,1)S(1)}, bf16[256,256]{1,0:T(8,128)(2,1)S(1)}, u32[]{:S(2)}, u32[]{:S(2)}) collective-permute-start(bf16[256,256]{1,0:T(8,128)(2,1)S(1)} %get-tuple-element.29), channel_id=1, source_target_pairs={{0,16},{1,241},{16,32},{17,1},{32,48},{33,17},{48,64},{49,33},{64,... | collective-permute-start | bytes 393224 | tf_op jit(solution)/shard_map/ppermute | solution.py:219
  78.7 12.0 %collective-permute-start.7 = (bf16[256,256]{1,0:T(8,128)(2,1)S(1)}, bf16[256,256]{1,0:T(8,128)(2,1)S(1)}, u32[]{:S(2)}, u32[]{:S(2)}) collective-permute-start(bf16[256,256]{1,0:T(8,128)(2,1)S(1)} %get-tuple-element.30), channel_id=1, source_target_pairs={{0,32},{1,225},{16,48},{17,241},{32,64},{33,1},{48,80},{49,17},{64... | collective-permute-start | bytes 393224 | tf_op jit(solution)/shard_map/ppermute | solution.py:219

commit v4 on v3

--- a/solution.py
+++ b/solution.py
@@ -52,41 +52,35 @@
     )(*args)
 
 
-def split_kernel(
-    side, dout, key, value, query, out, lnorm, heads, keep, send, dout_in, rows_in, norm_in, dout_sem, rows_sem, norm_sem
-):
-    load = pltpu.make_async_copy(dout, dout_in, dout_sem)
-    load.start()
-    norm_load = pltpu.make_async_copy(lnorm, norm_in, norm_sem)
-    norm_load.start()
-    loads = []
+def split_kernel(side, key, value, query, out, lnorm, keep, send, norm_in, sems):
+    copies = [pltpu.make_async_copy(lnorm, norm_in, sems.at[8])]
     for slot, rows in enumerate((key, value, query, out)):
-        loads.append(pltpu.make_async_copy(rows, rows_in.at[slot], rows_sem.at[slot]))
-        loads[-1].start()
-    load.wait()
-    for head in range(32):
-        heads[(head % 2) * 16 + head // 2] = dout_in[:, head * HD : (head + 1) * HD]
-    for each in loads:
-        each.wait()
-    norm_load.wait()
-
-    def put(mine, other):
-        for slot in range(4):
-            at = slice(slot * TOK, (slot + 1) * TOK)
-            keep[at, :] = rows_in[slot, :, mine * HD : (mine + 1) * HD]
-            send[at, :] = rows_in[slot, :, other * HD : (other + 1) * HD]
-        for head, dest in ((mine, keep), (other, send)):
+        for to, (head, dest) in enumerate(((side[0], keep), (1 - side[0], send))):
+            columns = pl.ds(pl.multiple_of(head * HD, HD), HD)
+            target = dest.at[pl.ds(slot * TOK, TOK)]
+            copies.append(
+                pltpu.make_async_copy(rows.at[:, columns], target, sems.at[2 * slot + to])
+            )
+    for copy in copies:
+        copy.start()
+    copies[0].wait()
+
+    def put(first, second):
+        for head, dest in enumerate((first, second)):
             norm = norm_in[head : head + 1, :] * LOG2E
             blank = jnp.zeros((AUX - 3, TOK), F32)
             dest[4 * TOK :, :] = jnp.concatenate(pieces(norm) + [blank], axis=0).astype(BF)
 
     @pl.when(side[0] == 0)
     def _():
-        put(0, 1)
+        put(keep, send)
 
     @pl.when(side[0] != 0)
     def _():
-        put(1, 0)
+        put(send, keep)
+
+    for copy in copies[1:]:
+        copy.wait()
 
 
 def merge_kernel(side, keep, got, keys, query, out, norm):
@@ -114,8 +108,10 @@
 
 def delta_kernel(query, out, norm, dout, pay):
     pay[:ROWS, :] = query[...]
-    pay[ROWS : 2 * ROWS, :] = dout[...]
-    product = dout[...].astype(F32) * out[...].astype(F32)
+    blocks = dout[...].astype(F32).reshape(16, 2, 8, HD)
+    ordered = jnp.concatenate([blocks[:, at].reshape(TOK, HD) for at in range(2)], axis=0)
+    pay[ROWS : 2 * ROWS, :] = ordered.astype(BF)
+    product = ordered * out[...].astype(F32)
     delta = jnp.sum(product.T, axis=0, keepdims=True)
     first = norm[:AUX, :].astype(F32)
     second = norm[AUX:, :].astype(F32)
@@ -147,31 +143,26 @@
         rows = slice(slot * ROWS, (slot + 1) * ROWS)
         keys[rows, :] = shard[:ROWS, :]
         values[rows, :] = shard[ROWS:, :]
-    for block in range(GROUP):
-        query = pays[block, :ROWS, :]
-        dout = pays[block, ROWS : 2 * ROWS, :]
-        aux = pays[block, 2 * ROWS :, :].astype(F32)
-        norm, delta = row_of(aux, 0), row_of(aux, 6)
-        grad_q = None
-        for at in range(0, KEYS, CHUNK):
-            rows = slice(at, at + CHUNK)
-            key = keys[rows, :]
-            probs = jnp.exp2(dot(key, query, 1, 1) * (FACTOR * LOG2E) - norm)
-            dprobs = dot(values[rows, :], dout, 1, 1)
-            dscore = (probs * (dprobs - delta)).astype(BF)
-            part_v = dot(probs.astype(BF), dout, 1, 0)
-            part_k = dot(dscore, query, 1, 0)
-            part_q = dot(key, dscore, 0, 0)
-            if block == 0:
-                sum_k[rows, :] = part_k
-                sum_v[rows, :] = part_v
-            else:
-                sum_k[rows, :] += part_k
-                sum_v[rows, :] += part_v
-            grad_q = part_q if at == 0 else grad_q + part_q
-        grad_q = (grad_q * FACTOR).astype(BF)
-        grads_q[block] = grad_q[:, :TOK]
-        grads_q[GROUP + block] = grad_q[:, TOK:]
+    query = jnp.concatenate([pays[at, :ROWS, :] for at in range(GROUP)], axis=0)
+    dout = jnp.concatenate([pays[at, ROWS : 2 * ROWS, :] for at in range(GROUP)], axis=0)
+    aux = [pays[at, 2 * ROWS :, :].astype(F32) for at in range(GROUP)]
+    norm = jnp.concatenate([row_of(rows, 0) for rows in aux], axis=1)
+    delta = jnp.concatenate([row_of(rows, 6) for rows in aux], axis=1)
+    grad_q = None
+    for at in range(0, KEYS, CHUNK):
+        rows = slice(at, at + CHUNK)
+        key = keys[rows, :]
+        probs = jnp.exp2(dot(key, query, 1, 1) * (FACTOR * LOG2E) - norm)
+        dprobs = dot(values[rows, :], dout, 1, 1)
+        dscore = (probs * (dprobs - delta)).astype(BF)
+        sum_v[rows, :] = dot(probs.astype(BF), dout, 1, 0)
+        sum_k[rows, :] = dot(dscore, query, 1, 0)
+        part_q = dot(key, dscore, 0, 0)
+        grad_q = part_q if at == 0 else grad_q + part_q
+    grad_q = (grad_q * FACTOR).astype(BF)
+    for at in range(GROUP):
+        grads_q[at] = grad_q[:, at * ROWS : at * ROWS + TOK]
+        grads_q[GROUP + at] = grad_q[:, at * ROWS + TOK : (at + 1) * ROWS]
     for slot in range(GROUP):
         for half, dest in enumerate((own, send)):
             rows = slice(slot * ROWS + half * TOK, slot * ROWS + (half + 1) * TOK)
@@ -226,26 +217,18 @@
 def body(query_rows, key_rows, value_rows, output_rows, grad_output, log_norm):
     side = lax.axis_index("x_lo").astype(jnp.int32).reshape(1)
     swap = ((4 * TOK + AUX, HD), BF)
-    heads, keep, send = local(
+    dout = lax.all_to_all(grad_output, ("x_hi", "y", "core", "x_lo"), 1, 0, tiled=True)
+    keep, send = local(
         split_kernel,
-        [((32, 8, HD), BF), swap, swap],
+        [swap, swap],
         side,
         *[
             pltpu.with_memory_space_constraint(rows, pltpu.HBM)
-            for rows in (grad_output, key_rows, value_rows, query_rows, output_rows, log_norm.T)
+            for rows in (key_rows, value_rows, query_rows, output_rows, log_norm.T)
         ],
-        far=range(1, 7),
-        scratch=(
-            pltpu.VMEM((8, 32 * HD), BF),
-            pltpu.VMEM((4, TOK, 2 * HD), BF),
-            pltpu.VMEM((2, TOK), F32),
-            pltpu.SemaphoreType.DMA,
-            pltpu.SemaphoreType.DMA((4,)),
-            pltpu.SemaphoreType.DMA,
-        ),
-    )
-    dout = lax.all_to_all(heads, ("x_lo", "x_hi", "y", "core"), 0, 0, tiled=True)
-    dout = dout.reshape(ROWS, HD)
+        far=range(1, 6),
+        scratch=(pltpu.VMEM((2, TOK), F32), pltpu.SemaphoreType.DMA((9,))),
+    )
     got = across(send)
     block = ((ROWS, HD), BF)
     pair = ((2 * ROWS, HD), BF)

time: 92 us -> 91.1 us (level)
  Pallas kernels: 6.33 us -> 5.36 us
    pallas_call x6, Pallas kernels: 6.33 us -> 5.36 us  [local(): pl.pallas_call(kernel, out_shape=[jax.ShapeDtypeStruct(shape, dtype) for...]
where the time goes in v4:
time: 91.1 us; the launch traced here: 90.5 us
  starting transfers between devices  47.1 us (52%)
  blocking collectives  27.2 us (30%)
  waiting for transfers between devices  10.1 us (11%)
  Pallas kernels  5.36 us (6%)
    all_gather x1, blocking collectives, body(): pays = lax.all_gather(pay, 'z_hi')  27.2 us
    ppermute x6, starting transfers between devices, along(): return lax.ppermute(value, ('z_hi', 'z_lo', 'core'), pairs)  24.7 us
    ppermute x6, waiting for transfers between devices, along(): return lax.ppermute(value, ('z_hi', 'z_lo', 'core'), pairs)  10.1 us
    all_to_all x1, starting transfers between devices, body(): lax.all_to_all(grad_output, ('x_hi', 'y', 'core', 'x_lo'), 1, 0, tiled=True)  8.67 us
    all_to_all x1, starting transfers between devices, body(): parts_q = lax.all_to_all(parts_q, ('x_lo', 'z_hi'), 0, 0, tiled=True)  8.18 us
    ppermute x2, starting transfers between devices, across(): return lax.ppermute(value, 'x_lo', [(0, 1), (1, 0)])  5.49 us
    pallas_call x6, Pallas kernels, local(): pl.pallas_call(kernel, out_shape=[jax.ShapeDtypeStruct(shape, dtype) for...  5.36 us
  transfers between devices with their start and end apart: 10, of which 3 were waited for; matrix products, arithmetic and copies ran while one was open for 0% of the time, Pallas kernels for 0%

profile of v4, /device:TPU:6, one launch (start us, length us, event | category | flops | bytes accessed | tf_op | source)
XLA Modules:
  0.0 90.5 jit_solution(11715029366848395994)
XLA Ops:
  0.6 1.0 %shard_map.85 = (bf16[528,128]{1,0:T(8,128)(2,1)S(1)}, bf16[528,128]{1,0:T(8,128)(2,1)S(1)}) custom-call(s32[1]{0:T(128)} %bitcast.side, bf16[128,256]{1,0:T(8,128)(2,1)} %key.1, bf16[128,256]{1,0:T(8,128)(2,1)} %value.1, bf16[128,256]{1,0:T(8,128)(2,1)} %query.1, bf16[128,256]{1,0:T(8,128)(2,1)} %out.1, f32[2,128]{1,0:T(2,128)} %bitcast.9), custom_call_target="tpu_custom_call" | custom-call | tf_op jit(solution)/shard_map/pallas_call | solution.py:39
  1.6 2.7 %collective-permute-start = (bf16[528,128]{1,0:T(8,128)(2,1)S(1)}, bf16[528,128]{1,0:T(8,128)(2,1)S(1)}, u32[]{:S(2)}, u32[]{:S(2)}) collective-permute-start(bf16[528,128]{1,0:T(8,128)(2,1)S(1)} %get-tuple-element.17), channel_id=1, source_target_pairs={{0,256},{256,0},{1,257},{257,1},{2,258},{258,2},{3,259},{259,3},{4... | collective-permute-start | bytes 405512 | tf_op jit(solution)/shard_map/ppermute | solution.py:214
  4.4 8.7 %all-to-all-start = ((bf16[8,32,128]{2,0,1:T(8,128)(2,1)}), bf16[8,32,128]{2,0,1:T(8,128)(2,1)S(1)}, u32[]{:S(2)}, u32[]{:S(2)}) async-start(bf16[8,32,128]{2,0,1:T(8,128)(2,1)} %bitcast.2), calls=%async_computation | async-start | bytes 131072 | tf_op jit(solution)/shard_map/all_to_all | solution.py:220
  13.0 0.0 collective-permute-done.got
  13.1 11.1 %collective-permute-start.3 = (bf16[512,128]{1,0:T(8,128)(2,1)S(1)}, bf16[512,128]{1,0:T(8,128)(2,1)S(1)}, u32[]{:S(2)}, u32[]{:S(2)}) collective-permute-start(bf16[512,128]{1,0:T(8,128)(2,1)S(1)} %get-tuple-element.21.keys0), channel_id=1, source_target_pairs={{0,224},{1,33},{16,240},{17,49},{32,0},{33,65},{48,16},{49,81},{64... | collective-permute-start | bytes 393224 | tf_op jit(solution)/shard_map/ppermute | solution.py:210
  24.2 2.9 %collective-permute-start.2 = (bf16[512,128]{1,0:T(8,128)(2,1)S(1)}, bf16[512,128]{1,0:T(8,128)(2,1)S(1)}, u32[]{:S(2)}, u32[]{:S(2)}) collective-permute-start(bf16[512,128]{1,0:T(8,128)(2,1)S(1)} %get-tuple-element.21.keys0), channel_id=1, source_target_pairs={{0,240},{1,17},{16,0},{17,33},{32,16},{33,49},{48,32},{49,65},{64,... | collective-permute-start | bytes 393224 | tf_op jit(solution)/shard_map/ppermute | solution.py:210
  27.1 2.9 %collective-permute-start.1 = (bf16[512,128]{1,0:T(8,128)(2,1)S(1)}, bf16[512,128]{1,0:T(8,128)(2,1)S(1)}, u32[]{:S(2)}, u32[]{:S(2)}) collective-permute-start(bf16[512,128]{1,0:T(8,128)(2,1)S(1)} %get-tuple-element.21.keys0), channel_id=1, source_target_pairs={{0,16},{1,241},{16,32},{17,1},{32,48},{33,17},{48,64},{49,33},{64,... | collective-permute-start | bytes 393224 | tf_op jit(solution)/shard_map/ppermute | solution.py:210
  30.1 0.0 all-to-all-done
  30.1 0.1 shard_map.87
  30.2 27.2 %all-gather = bf16[2112,128]{1,0:T(8,128)(2,1)S(1)} all-gather(bf16[528,128]{1,0:T(8,128)(2,1)S(1)} %shard_map.87), channel_id=2, replica_groups=mesh['x_lo'=2,'z_hi'=4,'z_lo'=4,'x_hi'=2,'y'=4,'core'=2] {'z_hi'}, dimensions={0}, use_global_device_ids=true | all-gather | bytes 675840 | tf_op jit(solution)/shard_map/all_gather | solution.py:240
  57.4 0.0 collective-permute-done.3.keys3
  57.4 0.0 collective-permute-done.2.keys2
  57.4 0.0 collective-permute-done.1.keys1
  57.5 3.4 %shard_map.88 = (bf16[8,128,128]{2,1,0:T(8,128)(2,1)}, f32[4,256,128]{2,1,0:T(8,128)S(1)}, bf16[4,256,128]{2,1,0:T(8,128)(2,1)S(1)}) custom-call(bf16[4,528,128]{2,1,0:T(8,128)(2,1)S(1)} %bitcast.7, bf16[512,128]{1,0:T(8,128)(2,1)S(1)} %get-tuple-element.21.keys0, bf16[512,128]{1,0:T(8,128)(2,1)S(1)} %collective-permute-done.1.keys1, ...), custom_call_target="tpu_custom_call" | custom-call | tf_op jit(solution)/shard_map/pallas_call | solution.py:39
  60.8 2.8 %collective-permute-start.4 = (bf16[4,256,128]{2,1,0:T(8,128)(2,1)S(1)}, bf16[4,256,128]{2,1,0:T(8,128)(2,1)S(1)}, u32[]{:S(2)}, u32[]{:S(2)}) collective-permute-start(bf16[4,256,128]{2,1,0:T(8,128)(2,1)S(1)} %get-tuple-element.24), channel_id=1, source_target_pairs={{0,256},{256,0},{1,257},{257,1},{2,258},{258,2},{3,259},{259,3},{4... | collective-permute-start | bytes 786440 | tf_op jit(solution)/shard_map/ppermute | solution.py:214
  63.6 8.2 %all-to-all-start.1 = ((bf16[8,128,128]{2,1,0:T(8,128)(2,1)}), bf16[8,128,128]{2,1,0:T(8,128)(2,1)S(1)}, u32[]{:S(2)}, u32[]{:S(2)}) async-start(bf16[8,128,128]{2,1,0:T(8,128)(2,1)} %get-tuple-element.22), calls=%async_computation.1 | async-start | bytes 524288 | tf_op jit(solution)/shard_map/all_to_all | solution.py:250
  71.7 0.0 collective-permute-done.4.got
  71.7 0.1 shard_map.89
  71.8 3.7 %collective-permute-start.5 = (bf16[256,256]{1,0:T(8,128)(2,1)S(1)}, bf16[256,256]{1,0:T(8,128)(2,1)S(1)}, u32[]{:S(2)}, u32[]{:S(2)}) collective-permute-start(bf16[256,256]{1,0:T(8,128)(2,1)S(1)} %get-tuple-element.26), channel_id=1, source_target_pairs={{0,240},{1,17},{16,0},{17,33},{32,16},{33,49},{48,32},{49,65},{64,... | collective-permute-start | bytes 393224 | tf_op jit(solution)/shard_map/ppermute | solution.py:210
  75.6 2.1 %collective-permute-start.6 = (bf16[256,256]{1,0:T(8,128)(2,1)S(1)}, bf16[256,256]{1,0:T(8,128)(2,1)S(1)}, u32[]{:S(2)}, u32[]{:S(2)}) collective-permute-start(bf16[256,256]{1,0:T(8,128)(2,1)S(1)} %get-tuple-element.27), channel_id=1, source_target_pairs={{0,16},{1,241},{16,32},{17,1},{32,48},{33,17},{48,64},{49,33},{64,... | collective-permute-start | bytes 393224 | tf_op jit(solution)/shard_map/ppermute | solution.py:210
  77.7 1.9 %collective-permute-start.7 = (bf16[256,256]{1,0:T(8,128)(2,1)S(1)}, bf16[256,256]{1,0:T(8,128)(2,1)S(1)}, u32[]{:S(2)}, u32[]{:S(2)}) collective-permute-start(bf16[256,256]{1,0:T(8,128)(2,1)S(1)} %get-tuple-element.28), channel_id=1, source_target_pairs={{0,32},{1,225},{16,48},{17,241},{32,64},{33,1},{48,80},{49,17},{64... | collective-permute-start | bytes 393224 | tf_op jit(solution)/shard_map/ppermute | solution.py:210
  79.6 2.1 %collective-permute-done.5.got1 = bf16[256,256]{1,0:T(8,128)(2,1)S(1)} collective-permute-done((bf16[256,256]{1,0:T(8,128)(2,1)S(1)}, bf16[256,256]{1,0:T(8,128)(2,1)S(1)}, u32[]{:S(2)}, u32[]{:S(2)}) %collective-permute-start.5) | collective-permute-done | bytes 131104 | tf_op jit(solution)/shard_map/ppermute | solution.py:210
  81.7 5.4 %collective-permute-done.6.got2 = bf16[256,256]{1,0:T(8,128)(2,1)S(1)} collective-permute-done((bf16[256,256]{1,0:T(8,128)(2,1)S(1)}, bf16[256,256]{1,0:T(8,128)(2,1)S(1)}, u32[]{:S(2)}, u32[]{:S(2)}) %collective-permute-start.6) | collective-permute-done | bytes 131104 | tf_op jit(solution)/shard_map/ppermute | solution.py:210
  87.1 2.6 %collective-permute-done.7.got3 = bf16[256,256]{1,0:T(8,128)(2,1)S(1)} collective-permute-done((bf16[256,256]{1,0:T(8,128)(2,1)S(1)}, bf16[256,256]{1,0:T(8,128)(2,1)S(1)}, u32[]{:S(2)}, u32[]{:S(2)}) %collective-permute-start.7) | collective-permute-done | bytes 131104 | tf_op jit(solution)/shard_map/ppermute | solution.py:210
  89.7 0.0 all-to-all-done.1.parts_q
  89.7 0.8 shard_map.90
  (1 shorter events, 0.0 us)
Async XLA Ops:
  1.6 11.4 %collective-permute-start = (bf16[528,128]{1,0:T(8,128)(2,1)S(1)}, bf16[528,128]{1,0:T(8,128)(2,1)S(1)}, u32[]{:S(2)}, u32[]{:S(2)}) collective-permute-start(bf16[528,128]{1,0:T(8,128)(2,1)S(1)} %get-tuple-element.17), channel_id=1, source_target_pairs={{0,256},{256,0},{1,257},{257,1},{2,258},{258,2},{3,259},{259,3},{4... | collective-permute-start | bytes 405512 | tf_op jit(solution)/shard_map/ppermute | solution.py:214
  4.4 25.7 %all-to-all-start = ((bf16[8,32,128]{2,0,1:T(8,128)(2,1)}), bf16[8,32,128]{2,0,1:T(8,128)(2,1)S(1)}, u32[]{:S(2)}, u32[]{:S(2)}) async-start(bf16[8,32,128]{2,0,1:T(8,128)(2,1)} %bitcast.2), calls=%async_computation | async-start | bytes 131072 | tf_op jit(solution)/shard_map/all_to_all | solution.py:220
  13.1 44.4 %collective-permute-start.3 = (bf16[512,128]{1,0:T(8,128)(2,1)S(1)}, bf16[512,128]{1,0:T(8,128)(2,1)S(1)}, u32[]{:S(2)}, u32[]{:S(2)}) collective-permute-start(bf16[512,128]{1,0:T(8,128)(2,1)S(1)} %get-tuple-element.21.keys0), channel_id=1, source_target_pairs={{0,224},{1,33},{16,240},{17,49},{32,0},{33,65},{48,16},{49,81},{64... | collective-permute-start | bytes 393224 | tf_op jit(solution)/shard_map/ppermute | solution.py:210
  24.2 33.2 %collective-permute-start.2 = (bf16[512,128]{1,0:T(8,128)(2,1)S(1)}, bf16[512,128]{1,0:T(8,128)(2,1)S(1)}, u32[]{:S(2)}, u32[]{:S(2)}) collective-permute-start(bf16[512,128]{1,0:T(8,128)(2,1)S(1)} %get-tuple-element.21.keys0), channel_id=1, source_target_pairs={{0,240},{1,17},{16,0},{17,33},{32,16},{33,49},{48,32},{49,65},{64,... | collective-permute-start | bytes 393224 | tf_op jit(solution)/shard_map/ppermute | solution.py:210
  27.1 30.3 %collective-permute-start.1 = (bf16[512,128]{1,0:T(8,128)(2,1)S(1)}, bf16[512,128]{1,0:T(8,128)(2,1)S(1)}, u32[]{:S(2)}, u32[]{:S(2)}) collective-permute-start(bf16[512,128]{1,0:T(8,128)(2,1)S(1)} %get-tuple-element.21.keys0), channel_id=1, source_target_pairs={{0,16},{1,241},{16,32},{17,1},{32,48},{33,17},{48,64},{49,33},{64,... | collective-permute-start | bytes 393224 | tf_op jit(solution)/shard_map/ppermute | solution.py:210
  60.8 10.9 %collective-permute-start.4 = (bf16[4,256,128]{2,1,0:T(8,128)(2,1)S(1)}, bf16[4,256,128]{2,1,0:T(8,128)(2,1)S(1)}, u32[]{:S(2)}, u32[]{:S(2)}) collective-permute-start(bf16[4,256,128]{2,1,0:T(8,128)(2,1)S(1)} %get-tuple-element.24), channel_id=1, source_target_pairs={{0,256},{256,0},{1,257},{257,1},{2,258},{258,2},{3,259},{259,3},{4... | collective-permute-start | bytes 786440 | tf_op jit(solution)/shard_map/ppermute | solution.py:214
  63.6 26.1 %all-to-all-start.1 = ((bf16[8,128,128]{2,1,0:T(8,128)(2,1)}), bf16[8,128,128]{2,1,0:T(8,128)(2,1)S(1)}, u32[]{:S(2)}, u32[]{:S(2)}) async-start(bf16[8,128,128]{2,1,0:T(8,128)(2,1)} %get-tuple-element.22), calls=%async_computation.1 | async-start | bytes 524288 | tf_op jit(solution)/shard_map/all_to_all | solution.py:250
  71.8 9.9 %collective-permute-start.5 = (bf16[256,256]{1,0:T(8,128)(2,1)S(1)}, bf16[256,256]{1,0:T(8,128)(2,1)S(1)}, u32[]{:S(2)}, u32[]{:S(2)}) collective-permute-start(bf16[256,256]{1,0:T(8,128)(2,1)S(1)} %get-tuple-element.26), channel_id=1, source_target_pairs={{0,240},{1,17},{16,0},{17,33},{32,16},{33,49},{48,32},{49,65},{64,... | collective-permute-start | bytes 393224 | tf_op jit(solution)/shard_map/ppermute | solution.py:210
  75.6 11.5 %collective-permute-start.6 = (bf16[256,256]{1,0:T(8,128)(2,1)S(1)}, bf16[256,256]{1,0:T(8,128)(2,1)S(1)}, u32[]{:S(2)}, u32[]{:S(2)}) collective-permute-start(bf16[256,256]{1,0:T(8,128)(2,1)S(1)} %get-tuple-element.27), channel_id=1, source_target_pairs={{0,16},{1,241},{16,32},{17,1},{32,48},{33,17},{48,64},{49,33},{64,... | collective-permute-start | bytes 393224 | tf_op jit(solution)/shard_map/ppermute | solution.py:210
  77.7 12.0 %collective-permute-start.7 = (bf16[256,256]{1,0:T(8,128)(2,1)S(1)}, bf16[256,256]{1,0:T(8,128)(2,1)S(1)}, u32[]{:S(2)}, u32[]{:S(2)}) collective-permute-start(bf16[256,256]{1,0:T(8,128)(2,1)S(1)} %get-tuple-element.28), channel_id=1, source_target_pairs={{0,32},{1,225},{16,48},{17,241},{32,64},{33,1},{48,80},{49,17},{64... | collective-permute-start | bytes 393224 | tf_op jit(solution)/shard_map/ppermute | solution.py:210

commit v5 on v4

--- a/solution.py
+++ b/solution.py
@@ -176,12 +176,15 @@
         dest[:, HD:] = got[slot].astype(dest.dtype)
 
 
-def join_kernel(side, parts_q, total, got1, got2, got3, grad_q, grad_k, grad_v):
+def query_kernel(parts_q, grad_q):
     for head in range(2):
         sum_q = parts_q[head * GROUP].astype(F32)
         for at in range(1, GROUP):
             sum_q += parts_q[head * GROUP + at].astype(F32)
         grad_q[:, head * HD : (head + 1) * HD] = sum_q.T.astype(BF)
+
+
+def join_kernel(side, total, got1, got2, got3, grad_k, grad_v):
     sum_kv = total[...]
     for got in (got1, got2, got3):
         sum_kv += got[...].astype(F32)
@@ -253,9 +256,11 @@
         fold_kernel, [(wide[0], F32)] + [wide] * 3, own, got, cost=LONG
     )
     gots = [along(part, -step) for part, step in zip(sends, K_STEPS)]
-    return tuple(
-        local(join_kernel, [((TOK, 2 * HD), BF)] * 3, side, parts_q, total, *gots)
-    )
+    final = ((TOK, 2 * HD), BF)
+    (grad_q,) = local(query_kernel, [final], parts_q)
+    grad_q, gots[0] = lax.optimization_barrier((grad_q, gots[0]))
+    grad_k, grad_v = local(join_kernel, [final] * 2, side, total, *gots)
+    return grad_q, grad_k, grad_v
 
 
 def solution(mesh):

time: 91.1 us -> 91 us (level)
    ppermute x6, waiting for transfers between devices: 10.1 us -> 2.67 us  [along(): return lax.ppermute(value, ('z_hi', 'z_lo', 'core'), pairs)]
    all_to_all x1, waiting for transfers between devices: 0.01 us -> 6.65 us  [body(): parts_q = lax.all_to_all(parts_q, ('x_lo', 'z_hi'), 0, 0, tiled=True)]
    pallas_call x6 -> x7, Pallas kernels: 5.36 us -> 6.01 us  [local(): pl.pallas_call(kernel, out_shape=[jax.ShapeDtypeStruct(shape, dtype) for...]
  transfers between devices with their start and end apart: 10 -> 10, of which waited for: 3 -> 3; matrix products, arithmetic and copies ran while one was open for 0% -> 0% of each run, Pallas kernels for 0% -> 1%
where the time goes in v5:
time: 91 us; the launch traced here: 90.4 us
  starting transfers between devices  47.1 us (52%)
  blocking collectives  27.2 us (30%)
  waiting for transfers between devices  9.33 us (10%)
  Pallas kernels  6.01 us (7%)
    all_gather x1, blocking collectives, body(): pays = lax.all_gather(pay, 'z_hi')  27.2 us
    ppermute x6, starting transfers between devices, along(): return lax.ppermute(value, ('z_hi', 'z_lo', 'core'), pairs)  24.7 us
    all_to_all x1, starting transfers between devices, body(): lax.all_to_all(grad_output, ('x_hi', 'y', 'core', 'x_lo'), 1, 0, tiled=True)  8.67 us
    all_to_all x1, starting transfers between devices, body(): parts_q = lax.all_to_all(parts_q, ('x_lo', 'z_hi'), 0, 0, tiled=True)  8.18 us
    all_to_all x1, waiting for transfers between devices, body(): parts_q = lax.all_to_all(parts_q, ('x_lo', 'z_hi'), 0, 0, tiled=True)  6.65 us
    pallas_call x7, Pallas kernels, local(): pl.pallas_call(kernel, out_shape=[jax.ShapeDtypeStruct(shape, dtype) for...  6.01 us
    ppermute x2, starting transfers between devices, across(): return lax.ppermute(value, 'x_lo', [(0, 1), (1, 0)])  5.49 us
    ppermute x6, waiting for transfers between devices, along(): return lax.ppermute(value, ('z_hi', 'z_lo', 'core'), pairs)  2.67 us
  transfers between devices with their start and end apart: 10, of which 3 were waited for; matrix products, arithmetic and copies ran while one was open for 0% of the time, Pallas kernels for 1%

profile of v5, /device:TPU:6, one launch (start us, length us, event | category | flops | bytes accessed | tf_op | source)
XLA Modules:
  0.0 90.4 jit_solution(15799144195666451917)
XLA Ops:
  0.6 1.0 %shard_map.85 = (bf16[528,128]{1,0:T(8,128)(2,1)S(1)}, bf16[528,128]{1,0:T(8,128)(2,1)S(1)}) custom-call(s32[1]{0:T(128)} %bitcast.side, bf16[128,256]{1,0:T(8,128)(2,1)} %key.1, bf16[128,256]{1,0:T(8,128)(2,1)} %value.1, bf16[128,256]{1,0:T(8,128)(2,1)} %query.1, bf16[128,256]{1,0:T(8,128)(2,1)} %out.1, f32[2,128]{1,0:T(2,128)} %bitcast.9), custom_call_target="tpu_custom_call" | custom-call | tf_op jit(solution)/shard_map/pallas_call | solution.py:39
  1.6 2.7 %collective-permute-start = (bf16[528,128]{1,0:T(8,128)(2,1)S(1)}, bf16[528,128]{1,0:T(8,128)(2,1)S(1)}, u32[]{:S(2)}, u32[]{:S(2)}) collective-permute-start(bf16[528,128]{1,0:T(8,128)(2,1)S(1)} %get-tuple-element.21), channel_id=1, source_target_pairs={{0,256},{256,0},{1,257},{257,1},{2,258},{258,2},{3,259},{259,3},{4... | collective-permute-start | bytes 405512 | tf_op jit(solution)/shard_map/ppermute | solution.py:217
  4.4 8.7 %all-to-all-start = ((bf16[8,32,128]{2,0,1:T(8,128)(2,1)}), bf16[8,32,128]{2,0,1:T(8,128)(2,1)S(1)}, u32[]{:S(2)}, u32[]{:S(2)}) async-start(bf16[8,32,128]{2,0,1:T(8,128)(2,1)} %bitcast.2), calls=%async_computation | async-start | bytes 131072 | tf_op jit(solution)/shard_map/all_to_all | solution.py:223
  13.0 0.0 collective-permute-done.got
  13.1 11.1 %collective-permute-start.3 = (bf16[512,128]{1,0:T(8,128)(2,1)S(1)}, bf16[512,128]{1,0:T(8,128)(2,1)S(1)}, u32[]{:S(2)}, u32[]{:S(2)}) collective-permute-start(bf16[512,128]{1,0:T(8,128)(2,1)S(1)} %get-tuple-element.25.keys0), channel_id=1, source_target_pairs={{0,224},{1,33},{16,240},{17,49},{32,0},{33,65},{48,16},{49,81},{64... | collective-permute-start | bytes 393224 | tf_op jit(solution)/shard_map/ppermute | solution.py:213
  24.2 2.9 %collective-permute-start.2 = (bf16[512,128]{1,0:T(8,128)(2,1)S(1)}, bf16[512,128]{1,0:T(8,128)(2,1)S(1)}, u32[]{:S(2)}, u32[]{:S(2)}) collective-permute-start(bf16[512,128]{1,0:T(8,128)(2,1)S(1)} %get-tuple-element.25.keys0), channel_id=1, source_target_pairs={{0,240},{1,17},{16,0},{17,33},{32,16},{33,49},{48,32},{49,65},{64,... | collective-permute-start | bytes 393224 | tf_op jit(solution)/shard_map/ppermute | solution.py:213
  27.1 2.9 %collective-permute-start.1 = (bf16[512,128]{1,0:T(8,128)(2,1)S(1)}, bf16[512,128]{1,0:T(8,128)(2,1)S(1)}, u32[]{:S(2)}, u32[]{:S(2)}) collective-permute-start(bf16[512,128]{1,0:T(8,128)(2,1)S(1)} %get-tuple-element.25.keys0), channel_id=1, source_target_pairs={{0,16},{1,241},{16,32},{17,1},{32,48},{33,17},{48,64},{49,33},{64,... | collective-permute-start | bytes 393224 | tf_op jit(solution)/shard_map/ppermute | solution.py:213
  30.1 0.0 all-to-all-done
  30.1 0.1 shard_map.87
  30.2 27.2 %all-gather = bf16[2112,128]{1,0:T(8,128)(2,1)S(1)} all-gather(bf16[528,128]{1,0:T(8,128)(2,1)S(1)} %shard_map.87), channel_id=2, replica_groups=mesh['x_lo'=2,'z_hi'=4,'z_lo'=4,'x_hi'=2,'y'=4,'core'=2] {'z_hi'}, dimensions={0}, use_global_device_ids=true | all-gather | bytes 675840 | tf_op jit(solution)/shard_map/all_gather | solution.py:243
  57.4 0.0 collective-permute-done.3.keys3
  57.4 0.0 collective-permute-done.2.keys2
  57.4 0.0 collective-permute-done.1.keys1
  57.5 3.3 %shard_map.88 = (bf16[8,128,128]{2,1,0:T(8,128)(2,1)}, f32[4,256,128]{2,1,0:T(8,128)S(1)}, bf16[4,256,128]{2,1,0:T(8,128)(2,1)S(1)}) custom-call(bf16[4,528,128]{2,1,0:T(8,128)(2,1)S(1)} %bitcast.7, bf16[512,128]{1,0:T(8,128)(2,1)S(1)} %get-tuple-element.25.keys0, bf16[512,128]{1,0:T(8,128)(2,1)S(1)} %collective-permute-done.1.keys1, ...), custom_call_target="tpu_custom_call" | custom-call | tf_op jit(solution)/shard_map/pallas_call | solution.py:39
  60.8 2.8 %collective-permute-start.4 = (bf16[4,256,128]{2,1,0:T(8,128)(2,1)S(1)}, bf16[4,256,128]{2,1,0:T(8,128)(2,1)S(1)}, u32[]{:S(2)}, u32[]{:S(2)}) collective-permute-start(bf16[4,256,128]{2,1,0:T(8,128)(2,1)S(1)} %get-tuple-element.28), channel_id=1, source_target_pairs={{0,256},{256,0},{1,257},{257,1},{2,258},{258,2},{3,259},{259,3},{4... | collective-permute-start | bytes 786440 | tf_op jit(solution)/shard_map/ppermute | solution.py:217
  63.6 8.2 %all-to-all-start.1 = ((bf16[8,128,128]{2,1,0:T(8,128)(2,1)}), bf16[8,128,128]{2,1,0:T(8,128)(2,1)S(1)}, u32[]{:S(2)}, u32[]{:S(2)}) async-start(bf16[8,128,128]{2,1,0:T(8,128)(2,1)} %get-tuple-element.26), calls=%async_computation.1 | async-start | bytes 524288 | tf_op jit(solution)/shard_map/all_to_all | solution.py:253
  71.7 0.0 collective-permute-done.4.got
  71.7 0.1 shard_map.90
  71.8 3.7 %collective-permute-start.5 = (bf16[256,256]{1,0:T(8,128)(2,1)S(1)}, bf16[256,256]{1,0:T(8,128)(2,1)S(1)}, u32[]{:S(2)}, u32[]{:S(2)}) collective-permute-start(bf16[256,256]{1,0:T(8,128)(2,1)S(1)} %get-tuple-element.29), channel_id=1, source_target_pairs={{0,240},{1,17},{16,0},{17,33},{32,16},{33,49},{48,32},{49,65},{64,... | collective-permute-start | bytes 393224 | tf_op jit(solution)/shard_map/ppermute | solution.py:213
  75.6 2.1 %collective-permute-start.6 = (bf16[256,256]{1,0:T(8,128)(2,1)S(1)}, bf16[256,256]{1,0:T(8,128)(2,1)S(1)}, u32[]{:S(2)}, u32[]{:S(2)}) collective-permute-start(bf16[256,256]{1,0:T(8,128)(2,1)S(1)} %get-tuple-element.33), channel_id=1, source_target_pairs={{0,16},{1,241},{16,32},{17,1},{32,48},{33,17},{48,64},{49,33},{64,... | collective-permute-start | bytes 393224 | tf_op jit(solution)/shard_map/ppermute | solution.py:213
  77.7 1.9 %collective-permute-start.7 = (bf16[256,256]{1,0:T(8,128)(2,1)S(1)}, bf16[256,256]{1,0:T(8,128)(2,1)S(1)}, u32[]{:S(2)}, u32[]{:S(2)}) collective-permute-start(bf16[256,256]{1,0:T(8,128)(2,1)S(1)} %get-tuple-element.34), channel_id=1, source_target_pairs={{0,32},{1,225},{16,48},{17,241},{32,64},{33,1},{48,80},{49,17},{64... | collective-permute-start | bytes 393224 | tf_op jit(solution)/shard_map/ppermute | solution.py:213
  79.6 6.6 %all-to-all-done.1.parts_q = bf16[8,128,128]{2,1,0:T(8,128)(2,1)S(1)} async-done(((bf16[8,128,128]{2,1,0:T(8,128)(2,1)}), bf16[8,128,128]{2,1,0:T(8,128)(2,1)S(1)}, u32[]{:S(2)}, u32[]{:S(2)}) %all-to-all-start.1) | async-done | bytes 262176 | tf_op jit(solution)/shard_map/all_to_all | solution.py:253
  86.3 0.7 shard_map.89
  87.0 0.0 collective-permute-done.5.got1
  87.0 0.1 collective-permute-done.6.got2
  87.1 2.6 %collective-permute-done.7.got3 = bf16[256,256]{1,0:T(8,128)(2,1)S(1)} collective-permute-done((bf16[256,256]{1,0:T(8,128)(2,1)S(1)}, bf16[256,256]{1,0:T(8,128)(2,1)S(1)}, u32[]{:S(2)}, u32[]{:S(2)}) %collective-permute-start.7) | collective-permute-done | bytes 131104 | tf_op jit(solution)/shard_map/ppermute | solution.py:213
  89.7 0.7 shard_map.91
  (1 shorter events, 0.0 us)
Async XLA Ops:
  1.6 11.4 %collective-permute-start = (bf16[528,128]{1,0:T(8,128)(2,1)S(1)}, bf16[528,128]{1,0:T(8,128)(2,1)S(1)}, u32[]{:S(2)}, u32[]{:S(2)}) collective-permute-start(bf16[528,128]{1,0:T(8,128)(2,1)S(1)} %get-tuple-element.21), channel_id=1, source_target_pairs={{0,256},{256,0},{1,257},{257,1},{2,258},{258,2},{3,259},{259,3},{4... | collective-permute-start | bytes 405512 | tf_op jit(solution)/shard_map/ppermute | solution.py:217
  4.4 25.7 %all-to-all-start = ((bf16[8,32,128]{2,0,1:T(8,128)(2,1)}), bf16[8,32,128]{2,0,1:T(8,128)(2,1)S(1)}, u32[]{:S(2)}, u32[]{:S(2)}) async-start(bf16[8,32,128]{2,0,1:T(8,128)(2,1)} %bitcast.2), calls=%async_computation | async-start | bytes 131072 | tf_op jit(solution)/shard_map/all_to_all | solution.py:223
  13.1 44.4 %collective-permute-start.3 = (bf16[512,128]{1,0:T(8,128)(2,1)S(1)}, bf16[512,128]{1,0:T(8,128)(2,1)S(1)}, u32[]{:S(2)}, u32[]{:S(2)}) collective-permute-start(bf16[512,128]{1,0:T(8,128)(2,1)S(1)} %get-tuple-element.25.keys0), channel_id=1, source_target_pairs={{0,224},{1,33},{16,240},{17,49},{32,0},{33,65},{48,16},{49,81},{64... | collective-permute-start | bytes 393224 | tf_op jit(solution)/shard_map/ppermute | solution.py:213
  24.2 33.2 %collective-permute-start.2 = (bf16[512,128]{1,0:T(8,128)(2,1)S(1)}, bf16[512,128]{1,0:T(8,128)(2,1)S(1)}, u32[]{:S(2)}, u32[]{:S(2)}) collective-permute-start(bf16[512,128]{1,0:T(8,128)(2,1)S(1)} %get-tuple-element.25.keys0), channel_id=1, source_target_pairs={{0,240},{1,17},{16,0},{17,33},{32,16},{33,49},{48,32},{49,65},{64,... | collective-permute-start | bytes 393224 | tf_op jit(solution)/shard_map/ppermute | solution.py:213
  27.1 30.3 %collective-permute-start.1 = (bf16[512,128]{1,0:T(8,128)(2,1)S(1)}, bf16[512,128]{1,0:T(8,128)(2,1)S(1)}, u32[]{:S(2)}, u32[]{:S(2)}) collective-permute-start(bf16[512,128]{1,0:T(8,128)(2,1)S(1)} %get-tuple-element.25.keys0), channel_id=1, source_target_pairs={{0,16},{1,241},{16,32},{17,1},{32,48},{33,17},{48,64},{49,33},{64,... | collective-permute-start | bytes 393224 | tf_op jit(solution)/shard_map/ppermute | solution.py:213
  60.8 10.9 %collective-permute-start.4 = (bf16[4,256,128]{2,1,0:T(8,128)(2,1)S(1)}, bf16[4,256,128]{2,1,0:T(8,128)(2,1)S(1)}, u32[]{:S(2)}, u32[]{:S(2)}) collective-permute-start(bf16[4,256,128]{2,1,0:T(8,128)(2,1)S(1)} %get-tuple-element.28), channel_id=1, source_target_pairs={{0,256},{256,0},{1,257},{257,1},{2,258},{258,2},{3,259},{259,3},{4... | collective-permute-start | bytes 786440 | tf_op jit(solution)/shard_map/ppermute | solution.py:217
  63.6 22.7 %all-to-all-start.1 = ((bf16[8,128,128]{2,1,0:T(8,128)(2,1)}), bf16[8,128,128]{2,1,0:T(8,128)(2,1)S(1)}, u32[]{:S(2)}, u32[]{:S(2)}) async-start(bf16[8,128,128]{2,1,0:T(8,128)(2,1)} %get-tuple-element.26), calls=%async_computation.1 | async-start | bytes 524288 | tf_op jit(solution)/shard_map/all_to_all | solution.py:253
  71.8 15.2 %collective-permute-start.5 = (bf16[256,256]{1,0:T(8,128)(2,1)S(1)}, bf16[256,256]{1,0:T(8,128)(2,1)S(1)}, u32[]{:S(2)}, u32[]{:S(2)}) collective-permute-start(bf16[256,256]{1,0:T(8,128)(2,1)S(1)} %get-tuple-element.29), channel_id=1, source_target_pairs={{0,240},{1,17},{16,0},{17,33},{32,16},{33,49},{48,32},{49,65},{64,... | collective-permute-start | bytes 393224 | tf_op jit(solution)/shard_map/ppermute | solution.py:213
  75.6 11.5 %collective-permute-start.6 = (bf16[256,256]{1,0:T(8,128)(2,1)S(1)}, bf16[256,256]{1,0:T(8,128)(2,1)S(1)}, u32[]{:S(2)}, u32[]{:S(2)}) collective-permute-start(bf16[256,256]{1,0:T(8,128)(2,1)S(1)} %get-tuple-element.33), channel_id=1, source_target_pairs={{0,16},{1,241},{16,32},{17,1},{32,48},{33,17},{48,64},{49,33},{64,... | collective-permute-start | bytes 393224 | tf_op jit(solution)/shard_map/ppermute | solution.py:213
  77.7 12.0 %collective-permute-start.7 = (bf16[256,256]{1,0:T(8,128)(2,1)S(1)}, bf16[256,256]{1,0:T(8,128)(2,1)S(1)}, u32[]{:S(2)}, u32[]{:S(2)}) collective-permute-start(bf16[256,256]{1,0:T(8,128)(2,1)S(1)} %get-tuple-element.34), channel_id=1, source_target_pairs={{0,32},{1,225},{16,48},{17,241},{32,64},{33,1},{48,80},{49,17},{64... | collective-permute-start | bytes 393224 | tf_op jit(solution)/shard_map/ppermute | solution.py:213

commit v6 on v4

--- a/solution.py
+++ b/solution.py
@@ -33,12 +33,15 @@
     return [high.astype(F32), mid.astype(F32), low.astype(F32)]
 
 
-def local(kernel, outs, *args, far=(), scratch=(), cost=None):
+def local(kernel, outs, *args, far=(), near=(), scratch=(), cost=None):
     scalars = [pl.BlockSpec(memory_space=pltpu.SMEM)]
     whole = [pl.BlockSpec(memory_space=pltpu.VMEM)]
     return pl.pallas_call(
         kernel,
-        out_shape=[jax.ShapeDtypeStruct(shape, dtype) for shape, dtype in outs],
+        out_shape=[
+            (pltpu.VMEM if at in near else jax.ShapeDtypeStruct)(shape, dtype)
+            for at, (shape, dtype) in enumerate(outs)
+        ],
         in_specs=[
             pl.BlockSpec(memory_space=pltpu.HBM)
             if at in far
@@ -244,6 +247,7 @@
         [((2 * GROUP, HD, TOK), BF), (shards[0], F32), shards],
         pays,
         *all_keys,
+        near=(0,),
         scratch=(pltpu.VMEM((KEYS, HD), BF),) * 2 + (pltpu.VMEM((KEYS, HD), F32),) * 2,
     )
     got = across(send)

time: 91.1 us -> 91.1 us (level)
  no operation moved by 1% of the time
where the time goes in v6:
time: 91.1 us; the launch traced here: 90.5 us
  starting transfers between devices  47.1 us (52%)
  blocking collectives  27.2 us (30%)
  waiting for transfers between devices  10.1 us (11%)
  Pallas kernels  5.36 us (6%)
    all_gather x1, blocking collectives, body(): pays = lax.all_gather(pay, 'z_hi')  27.2 us
    ppermute x6, starting transfers between devices, along(): return lax.ppermute(value, ('z_hi', 'z_lo', 'core'), pairs)  24.7 us
    ppermute x6, waiting for transfers between devices, along(): return lax.ppermute(value, ('z_hi', 'z_lo', 'core'), pairs)  10.1 us
    all_to_all x1, starting transfers between devices, body(): lax.all_to_all(grad_output, ('x_hi', 'y', 'core', 'x_lo'), 1, 0, tiled=True)  8.67 us
    all_to_all x1, starting transfers between devices, body(): parts_q = lax.all_to_all(parts_q, ('x_lo', 'z_hi'), 0, 0, tiled=True)  8.18 us
    ppermute x2, starting transfers between devices, across(): return lax.ppermute(value, 'x_lo', [(0, 1), (1, 0)])  5.49 us
    pallas_call x6, Pallas kernels, local(): pl.pallas_call(kernel, out_shape=[(pltpu.VMEM if at in near else jax.Shap...  5.36 us
  transfers between devices with their start and end apart: 10, of which 3 were waited for; matrix products, arithmetic and copies ran while one was open for 0% of the time, Pallas kernels for 0%

profile of v6, /device:TPU:6, one launch (start us, length us, event | category | flops | bytes accessed | tf_op | source)
XLA Modules:
  0.0 90.5 jit_solution(11715029366848395994)
XLA Ops:
  0.6 1.0 %shard_map.85 = (bf16[528,128]{1,0:T(8,128)(2,1)S(1)}, bf16[528,128]{1,0:T(8,128)(2,1)S(1)}) custom-call(s32[1]{0:T(128)} %bitcast.side, bf16[128,256]{1,0:T(8,128)(2,1)} %key.1, bf16[128,256]{1,0:T(8,128)(2,1)} %value.1, bf16[128,256]{1,0:T(8,128)(2,1)} %query.1, bf16[128,256]{1,0:T(8,128)(2,1)} %out.1, f32[2,128]{1,0:T(2,128)} %bitcast.9), custom_call_target="tpu_custom_call" | custom-call | tf_op jit(solution)/shard_map/pallas_call | solution.py:39
  1.6 2.7 %collective-permute-start = (bf16[528,128]{1,0:T(8,128)(2,1)S(1)}, bf16[528,128]{1,0:T(8,128)(2,1)S(1)}, u32[]{:S(2)}, u32[]{:S(2)}) collective-permute-start(bf16[528,128]{1,0:T(8,128)(2,1)S(1)} %get-tuple-element.17), channel_id=1, source_target_pairs={{0,256},{256,0},{1,257},{257,1},{2,258},{258,2},{3,259},{259,3},{4... | collective-permute-start | bytes 405512 | tf_op jit(solution)/shard_map/ppermute | solution.py:217
  4.4 8.7 %all-to-all-start = ((bf16[8,32,128]{2,0,1:T(8,128)(2,1)}), bf16[8,32,128]{2,0,1:T(8,128)(2,1)S(1)}, u32[]{:S(2)}, u32[]{:S(2)}) async-start(bf16[8,32,128]{2,0,1:T(8,128)(2,1)} %bitcast.2), calls=%async_computation | async-start | bytes 131072 | tf_op jit(solution)/shard_map/all_to_all | solution.py:223
  13.0 0.0 collective-permute-done.got
  13.1 11.1 %collective-permute-start.3 = (bf16[512,128]{1,0:T(8,128)(2,1)S(1)}, bf16[512,128]{1,0:T(8,128)(2,1)S(1)}, u32[]{:S(2)}, u32[]{:S(2)}) collective-permute-start(bf16[512,128]{1,0:T(8,128)(2,1)S(1)} %get-tuple-element.21.keys0), channel_id=1, source_target_pairs={{0,224},{1,33},{16,240},{17,49},{32,0},{33,65},{48,16},{49,81},{64... | collective-permute-start | bytes 393224 | tf_op jit(solution)/shard_map/ppermute | solution.py:213
  24.2 2.9 %collective-permute-start.2 = (bf16[512,128]{1,0:T(8,128)(2,1)S(1)}, bf16[512,128]{1,0:T(8,128)(2,1)S(1)}, u32[]{:S(2)}, u32[]{:S(2)}) collective-permute-start(bf16[512,128]{1,0:T(8,128)(2,1)S(1)} %get-tuple-element.21.keys0), channel_id=1, source_target_pairs={{0,240},{1,17},{16,0},{17,33},{32,16},{33,49},{48,32},{49,65},{64,... | collective-permute-start | bytes 393224 | tf_op jit(solution)/shard_map/ppermute | solution.py:213
  27.1 2.9 %collective-permute-start.1 = (bf16[512,128]{1,0:T(8,128)(2,1)S(1)}, bf16[512,128]{1,0:T(8,128)(2,1)S(1)}, u32[]{:S(2)}, u32[]{:S(2)}) collective-permute-start(bf16[512,128]{1,0:T(8,128)(2,1)S(1)} %get-tuple-element.21.keys0), channel_id=1, source_target_pairs={{0,16},{1,241},{16,32},{17,1},{32,48},{33,17},{48,64},{49,33},{64,... | collective-permute-start | bytes 393224 | tf_op jit(solution)/shard_map/ppermute | solution.py:213
  30.1 0.0 all-to-all-done
  30.1 0.1 shard_map.87
  30.2 27.2 %all-gather = bf16[2112,128]{1,0:T(8,128)(2,1)S(1)} all-gather(bf16[528,128]{1,0:T(8,128)(2,1)S(1)} %shard_map.87), channel_id=2, replica_groups=mesh['x_lo'=2,'z_hi'=4,'z_lo'=4,'x_hi'=2,'y'=4,'core'=2] {'z_hi'}, dimensions={0}, use_global_device_ids=true | all-gather | bytes 675840 | tf_op jit(solution)/shard_map/all_gather | solution.py:243
  57.4 0.0 collective-permute-done.3.keys3
  57.4 0.0 collective-permute-done.2.keys2
  57.4 0.0 collective-permute-done.1.keys1
  57.5 3.4 %shard_map.88 = (bf16[8,128,128]{2,1,0:T(8,128)(2,1)}, f32[4,256,128]{2,1,0:T(8,128)S(1)}, bf16[4,256,128]{2,1,0:T(8,128)(2,1)S(1)}) custom-call(bf16[4,528,128]{2,1,0:T(8,128)(2,1)S(1)} %bitcast.7, bf16[512,128]{1,0:T(8,128)(2,1)S(1)} %get-tuple-element.21.keys0, bf16[512,128]{1,0:T(8,128)(2,1)S(1)} %collective-permute-done.1.keys1, ...), custom_call_target="tpu_custom_call" | custom-call | tf_op jit(solution)/shard_map/pallas_call | solution.py:39
  60.8 2.8 %collective-permute-start.4 = (bf16[4,256,128]{2,1,0:T(8,128)(2,1)S(1)}, bf16[4,256,128]{2,1,0:T(8,128)(2,1)S(1)}, u32[]{:S(2)}, u32[]{:S(2)}) collective-permute-start(bf16[4,256,128]{2,1,0:T(8,128)(2,1)S(1)} %get-tuple-element.24), channel_id=1, source_target_pairs={{0,256},{256,0},{1,257},{257,1},{2,258},{258,2},{3,259},{259,3},{4... | collective-permute-start | bytes 786440 | tf_op jit(solution)/shard_map/ppermute | solution.py:217
  63.6 8.2 %all-to-all-start.1 = ((bf16[8,128,128]{2,1,0:T(8,128)(2,1)}), bf16[8,128,128]{2,1,0:T(8,128)(2,1)S(1)}, u32[]{:S(2)}, u32[]{:S(2)}) async-start(bf16[8,128,128]{2,1,0:T(8,128)(2,1)} %get-tuple-element.22), calls=%async_computation.1 | async-start | bytes 524288 | tf_op jit(solution)/shard_map/all_to_all | solution.py:254
  71.7 0.0 collective-permute-done.4.got
  71.7 0.1 shard_map.89
  71.8 3.7 %collective-permute-start.5 = (bf16[256,256]{1,0:T(8,128)(2,1)S(1)}, bf16[256,256]{1,0:T(8,128)(2,1)S(1)}, u32[]{:S(2)}, u32[]{:S(2)}) collective-permute-start(bf16[256,256]{1,0:T(8,128)(2,1)S(1)} %get-tuple-element.26), channel_id=1, source_target_pairs={{0,240},{1,17},{16,0},{17,33},{32,16},{33,49},{48,32},{49,65},{64,... | collective-permute-start | bytes 393224 | tf_op jit(solution)/shard_map/ppermute | solution.py:213
  75.6 2.1 %collective-permute-start.6 = (bf16[256,256]{1,0:T(8,128)(2,1)S(1)}, bf16[256,256]{1,0:T(8,128)(2,1)S(1)}, u32[]{:S(2)}, u32[]{:S(2)}) collective-permute-start(bf16[256,256]{1,0:T(8,128)(2,1)S(1)} %get-tuple-element.27), channel_id=1, source_target_pairs={{0,16},{1,241},{16,32},{17,1},{32,48},{33,17},{48,64},{49,33},{64,... | collective-permute-start | bytes 393224 | tf_op jit(solution)/shard_map/ppermute | solution.py:213
  77.7 1.9 %collective-permute-start.7 = (bf16[256,256]{1,0:T(8,128)(2,1)S(1)}, bf16[256,256]{1,0:T(8,128)(2,1)S(1)}, u32[]{:S(2)}, u32[]{:S(2)}) collective-permute-start(bf16[256,256]{1,0:T(8,128)(2,1)S(1)} %get-tuple-element.28), channel_id=1, source_target_pairs={{0,32},{1,225},{16,48},{17,241},{32,64},{33,1},{48,80},{49,17},{64... | collective-permute-start | bytes 393224 | tf_op jit(solution)/shard_map/ppermute | solution.py:213
  79.6 2.1 %collective-permute-done.5.got1 = bf16[256,256]{1,0:T(8,128)(2,1)S(1)} collective-permute-done((bf16[256,256]{1,0:T(8,128)(2,1)S(1)}, bf16[256,256]{1,0:T(8,128)(2,1)S(1)}, u32[]{:S(2)}, u32[]{:S(2)}) %collective-permute-start.5) | collective-permute-done | bytes 131104 | tf_op jit(solution)/shard_map/ppermute | solution.py:213
  81.7 5.4 %collective-permute-done.6.got2 = bf16[256,256]{1,0:T(8,128)(2,1)S(1)} collective-permute-done((bf16[256,256]{1,0:T(8,128)(2,1)S(1)}, bf16[256,256]{1,0:T(8,128)(2,1)S(1)}, u32[]{:S(2)}, u32[]{:S(2)}) %collective-permute-start.6) | collective-permute-done | bytes 131104 | tf_op jit(solution)/shard_map/ppermute | solution.py:213
  87.1 2.6 %collective-permute-done.7.got3 = bf16[256,256]{1,0:T(8,128)(2,1)S(1)} collective-permute-done((bf16[256,256]{1,0:T(8,128)(2,1)S(1)}, bf16[256,256]{1,0:T(8,128)(2,1)S(1)}, u32[]{:S(2)}, u32[]{:S(2)}) %collective-permute-start.7) | collective-permute-done | bytes 131104 | tf_op jit(solution)/shard_map/ppermute | solution.py:213
  89.7 0.0 all-to-all-done.1.parts_q
  89.7 0.8 shard_map.90
  (1 shorter events, 0.0 us)
Async XLA Ops:
  1.6 11.4 %collective-permute-start = (bf16[528,128]{1,0:T(8,128)(2,1)S(1)}, bf16[528,128]{1,0:T(8,128)(2,1)S(1)}, u32[]{:S(2)}, u32[]{:S(2)}) collective-permute-start(bf16[528,128]{1,0:T(8,128)(2,1)S(1)} %get-tuple-element.17), channel_id=1, source_target_pairs={{0,256},{256,0},{1,257},{257,1},{2,258},{258,2},{3,259},{259,3},{4... | collective-permute-start | bytes 405512 | tf_op jit(solution)/shard_map/ppermute | solution.py:217
  4.4 25.7 %all-to-all-start = ((bf16[8,32,128]{2,0,1:T(8,128)(2,1)}), bf16[8,32,128]{2,0,1:T(8,128)(2,1)S(1)}, u32[]{:S(2)}, u32[]{:S(2)}) async-start(bf16[8,32,128]{2,0,1:T(8,128)(2,1)} %bitcast.2), calls=%async_computation | async-start | bytes 131072 | tf_op jit(solution)/shard_map/all_to_all | solution.py:223
  13.1 44.4 %collective-permute-start.3 = (bf16[512,128]{1,0:T(8,128)(2,1)S(1)}, bf16[512,128]{1,0:T(8,128)(2,1)S(1)}, u32[]{:S(2)}, u32[]{:S(2)}) collective-permute-start(bf16[512,128]{1,0:T(8,128)(2,1)S(1)} %get-tuple-element.21.keys0), channel_id=1, source_target_pairs={{0,224},{1,33},{16,240},{17,49},{32,0},{33,65},{48,16},{49,81},{64... | collective-permute-start | bytes 393224 | tf_op jit(solution)/shard_map/ppermute | solution.py:213
  24.2 33.2 %collective-permute-start.2 = (bf16[512,128]{1,0:T(8,128)(2,1)S(1)}, bf16[512,128]{1,0:T(8,128)(2,1)S(1)}, u32[]{:S(2)}, u32[]{:S(2)}) collective-permute-start(bf16[512,128]{1,0:T(8,128)(2,1)S(1)} %get-tuple-element.21.keys0), channel_id=1, source_target_pairs={{0,240},{1,17},{16,0},{17,33},{32,16},{33,49},{48,32},{49,65},{64,... | collective-permute-start | bytes 393224 | tf_op jit(solution)/shard_map/ppermute | solution.py:213
  27.1 30.3 %collective-permute-start.1 = (bf16[512,128]{1,0:T(8,128)(2,1)S(1)}, bf16[512,128]{1,0:T(8,128)(2,1)S(1)}, u32[]{:S(2)}, u32[]{:S(2)}) collective-permute-start(bf16[512,128]{1,0:T(8,128)(2,1)S(1)} %get-tuple-element.21.keys0), channel_id=1, source_target_pairs={{0,16},{1,241},{16,32},{17,1},{32,48},{33,17},{48,64},{49,33},{64,... | collective-permute-start | bytes 393224 | tf_op jit(solution)/shard_map/ppermute | solution.py:213
  60.8 10.9 %collective-permute-start.4 = (bf16[4,256,128]{2,1,0:T(8,128)(2,1)S(1)}, bf16[4,256,128]{2,1,0:T(8,128)(2,1)S(1)}, u32[]{:S(2)}, u32[]{:S(2)}) collective-permute-start(bf16[4,256,128]{2,1,0:T(8,128)(2,1)S(1)} %get-tuple-element.24), channel_id=1, source_target_pairs={{0,256},{256,0},{1,257},{257,1},{2,258},{258,2},{3,259},{259,3},{4... | collective-permute-start | bytes 786440 | tf_op jit(solution)/shard_map/ppermute | solution.py:217
  63.6 26.1 %all-to-all-start.1 = ((bf16[8,128,128]{2,1,0:T(8,128)(2,1)}), bf16[8,128,128]{2,1,0:T(8,128)(2,1)S(1)}, u32[]{:S(2)}, u32[]{:S(2)}) async-start(bf16[8,128,128]{2,1,0:T(8,128)(2,1)} %get-tuple-element.22), calls=%async_computation.1 | async-start | bytes 524288 | tf_op jit(solution)/shard_map/all_to_all | solution.py:254
  71.8 9.9 %collective-permute-start.5 = (bf16[256,256]{1,0:T(8,128)(2,1)S(1)}, bf16[256,256]{1,0:T(8,128)(2,1)S(1)}, u32[]{:S(2)}, u32[]{:S(2)}) collective-permute-start(bf16[256,256]{1,0:T(8,128)(2,1)S(1)} %get-tuple-element.26), channel_id=1, source_target_pairs={{0,240},{1,17},{16,0},{17,33},{32,16},{33,49},{48,32},{49,65},{64,... | collective-permute-start | bytes 393224 | tf_op jit(solution)/shard_map/ppermute | solution.py:213
  75.6 11.5 %collective-permute-start.6 = (bf16[256,256]{1,0:T(8,128)(2,1)S(1)}, bf16[256,256]{1,0:T(8,128)(2,1)S(1)}, u32[]{:S(2)}, u32[]{:S(2)}) collective-permute-start(bf16[256,256]{1,0:T(8,128)(2,1)S(1)} %get-tuple-element.27), channel_id=1, source_target_pairs={{0,16},{1,241},{16,32},{17,1},{32,48},{33,17},{48,64},{49,33},{64,... | collective-permute-start | bytes 393224 | tf_op jit(solution)/shard_map/ppermute | solution.py:213
  77.7 12.0 %collective-permute-start.7 = (bf16[256,256]{1,0:T(8,128)(2,1)S(1)}, bf16[256,256]{1,0:T(8,128)(2,1)S(1)}, u32[]{:S(2)}, u32[]{:S(2)}) collective-permute-start(bf16[256,256]{1,0:T(8,128)(2,1)S(1)} %get-tuple-element.28), channel_id=1, source_target_pairs={{0,32},{1,225},{16,48},{17,241},{32,64},{33,1},{48,80},{49,17},{64... | collective-permute-start | bytes 393224 | tf_op jit(solution)/shard_map/ppermute | solution.py:213

commit v7 on v4

--- a/solution.py
+++ b/solution.py
@@ -83,45 +83,36 @@
         copy.wait()
 
 
-def merge_kernel(side, keep, got, keys, query, out, norm):
+def merge_kernel(keep, got, keys):
     for slot in range(2):
         rows = slice(slot * TOK, (slot + 1) * TOK)
         keys[slot * ROWS : slot * ROWS + TOK, :] = keep[rows, :]
         keys[slot * ROWS + TOK : (slot + 1) * ROWS, :] = got[rows, :]
 
-    def put(first, second):
-        for slot, dest in ((2, query), (3, out)):
-            rows = slice(slot * TOK, (slot + 1) * TOK)
-            dest[:TOK, :] = first[rows, :]
-            dest[TOK:, :] = second[rows, :]
-        norm[:AUX, :] = first[4 * TOK :, :]
-        norm[AUX:, :] = second[4 * TOK :, :]
+
+def delta_kernel(side, keep, got, dout, pay):
+    blocks = dout[...].astype(F32).reshape(16, 2, 8, HD)
+
+    def put(sources):
+        norms, deltas = [], []
+        for half, source in enumerate(sources):
+            rows = slice(half * TOK, (half + 1) * TOK)
+            ordered = blocks[:, half].reshape(TOK, HD)
+            pay[rows, :] = source[2 * TOK : 3 * TOK, :]
+            pay[ROWS + half * TOK : ROWS + (half + 1) * TOK, :] = ordered.astype(BF)
+            product = ordered * source[3 * TOK : 4 * TOK, :].astype(F32)
+            deltas += pieces(jnp.sum(product.T, axis=0, keepdims=True))
+            norms.append(source[4 * TOK :, :].astype(F32)[:3, :])
+        rows = norms + deltas + [jnp.zeros((AUX - 12, TOK), F32)]
+        pay[2 * ROWS :, :] = jnp.concatenate(rows, axis=0).astype(BF)
 
     @pl.when(side[0] == 0)
     def _():
-        put(keep, got)
+        put((keep, got))
 
     @pl.when(side[0] != 0)
     def _():
-        put(got, keep)
-
-
-def delta_kernel(query, out, norm, dout, pay):
-    pay[:ROWS, :] = query[...]
-    blocks = dout[...].astype(F32).reshape(16, 2, 8, HD)
-    ordered = jnp.concatenate([blocks[:, at].reshape(TOK, HD) for at in range(2)], axis=0)
-    pay[ROWS : 2 * ROWS, :] = ordered.astype(BF)
-    product = ordered * out[...].astype(F32)
-    delta = jnp.sum(product.T, axis=0, keepdims=True)
-    first = norm[:AUX, :].astype(F32)
-    second = norm[AUX:, :].astype(F32)
-    rows = (
-        [first[:3, :], second[:3, :]]
-        + pieces(delta[:, :TOK])
-        + pieces(delta[:, TOK:])
-        + [jnp.zeros((AUX - 12, TOK), F32)]
-    )
-    pay[2 * ROWS :, :] = jnp.concatenate(rows, axis=0).astype(BF)
+        put((got, keep))
 
 
 def dot(left, right, left_dim, right_dim):
@@ -232,11 +223,9 @@
     got = across(send)
     block = ((ROWS, HD), BF)
     pair = ((2 * ROWS, HD), BF)
-    keys, query, out, norm = local(
-        merge_kernel, [pair, block, block, ((2 * AUX, HD), BF)], side, keep, got
-    )
+    (keys,) = local(merge_kernel, [pair], keep, got)
     all_keys = [keys] + [along(keys, step) for step in K_STEPS]
-    (pay,) = local(delta_kernel, [((PAY, HD), BF)], query, out, norm, dout)
+    (pay,) = local(delta_kernel, [((PAY, HD), BF)], side, keep, got, dout)
     pays = lax.all_gather(pay, "z_hi")
     shards = ((GROUP, ROWS, HD), BF)
     parts_q, own, send = local(

time: 91.1 us -> 91.1 us (level)
  no operation moved by 1% of the time
where the time goes in v7:
time: 91.1 us; the launch traced here: 90.5 us
  starting transfers between devices  47.1 us (52%)
  blocking collectives  27.2 us (30%)
  waiting for transfers between devices  10.1 us (11%)
  Pallas kernels  5.36 us (6%)
    all_gather x1, blocking collectives, body(): pays = lax.all_gather(pay, 'z_hi')  27.2 us
    ppermute x6, starting transfers between devices, along(): return lax.ppermute(value, ('z_hi', 'z_lo', 'core'), pairs)  24.7 us
    ppermute x6, waiting for transfers between devices, along(): return lax.ppermute(value, ('z_hi', 'z_lo', 'core'), pairs)  10 us
    all_to_all x1, starting transfers between devices, body(): lax.all_to_all(grad_output, ('x_hi', 'y', 'core', 'x_lo'), 1, 0, tiled=True)  8.67 us
    all_to_all x1, starting transfers between devices, body(): parts_q = lax.all_to_all(parts_q, ('x_lo', 'z_hi'), 0, 0, tiled=True)  8.19 us
    ppermute x2, starting transfers between devices, across(): return lax.ppermute(value, 'x_lo', [(0, 1), (1, 0)])  5.5 us
    pallas_call x6, Pallas kernels, local(): pl.pallas_call(kernel, out_shape=[jax.ShapeDtypeStruct(shape, dtype) for...  5.36 us
  transfers between devices with their start and end apart: 10, of which 3 were waited for; matrix products, arithmetic and copies ran while one was open for 0% of the time, Pallas kernels for 0%

profile of v7, /device:TPU:6, one launch (start us, length us, event | category | flops | bytes accessed | tf_op | source)
XLA Modules:
  0.0 90.5 jit_solution(1306173385197351237)
XLA Ops:
  0.6 1.0 %shard_map.85 = (bf16[528,128]{1,0:T(8,128)(2,1)S(1)}, bf16[528,128]{1,0:T(8,128)(2,1)S(1)}) custom-call(s32[1]{0:T(128)} %bitcast.side, bf16[128,256]{1,0:T(8,128)(2,1)} %key.1, bf16[128,256]{1,0:T(8,128)(2,1)} %value.1, bf16[128,256]{1,0:T(8,128)(2,1)} %query.1, bf16[128,256]{1,0:T(8,128)(2,1)} %out.1, f32[2,128]{1,0:T(2,128)} %bitcast.9), custom_call_target="tpu_custom_call" | custom-call | tf_op jit(solution)/shard_map/pallas_call | solution.py:39
  1.6 2.7 %collective-permute-start = (bf16[528,128]{1,0:T(8,128)(2,1)S(1)}, bf16[528,128]{1,0:T(8,128)(2,1)S(1)}, u32[]{:S(2)}, u32[]{:S(2)}) collective-permute-start(bf16[528,128]{1,0:T(8,128)(2,1)S(1)} %get-tuple-element.13), channel_id=1, source_target_pairs={{0,256},{256,0},{1,257},{257,1},{2,258},{258,2},{3,259},{259,3},{4... | collective-permute-start | bytes 405512 | tf_op jit(solution)/shard_map/ppermute | solution.py:205
  4.4 8.7 %all-to-all-start = ((bf16[8,32,128]{2,0,1:T(8,128)(2,1)}), bf16[8,32,128]{2,0,1:T(8,128)(2,1)S(1)}, u32[]{:S(2)}, u32[]{:S(2)}) async-start(bf16[8,32,128]{2,0,1:T(8,128)(2,1)} %bitcast.2), calls=%async_computation | async-start | bytes 131072 | tf_op jit(solution)/shard_map/all_to_all | solution.py:211
  13.0 0.0 collective-permute-done.got
  13.1 11.1 %collective-permute-start.3 = (bf16[512,128]{1,0:T(8,128)(2,1)S(1)}, bf16[512,128]{1,0:T(8,128)(2,1)S(1)}, u32[]{:S(2)}, u32[]{:S(2)}) collective-permute-start(bf16[512,128]{1,0:T(8,128)(2,1)S(1)} %shard_map.87.keys0), channel_id=1, source_target_pairs={{0,224},{1,33},{16,240},{17,49},{32,0},{33,65},{48,16},{49,81},{64... | collective-permute-start | bytes 393224 | tf_op jit(solution)/shard_map/ppermute | solution.py:201
  24.2 2.9 %collective-permute-start.2 = (bf16[512,128]{1,0:T(8,128)(2,1)S(1)}, bf16[512,128]{1,0:T(8,128)(2,1)S(1)}, u32[]{:S(2)}, u32[]{:S(2)}) collective-permute-start(bf16[512,128]{1,0:T(8,128)(2,1)S(1)} %shard_map.87.keys0), channel_id=1, source_target_pairs={{0,240},{1,17},{16,0},{17,33},{32,16},{33,49},{48,32},{49,65},{64,... | collective-permute-start | bytes 393224 | tf_op jit(solution)/shard_map/ppermute | solution.py:201
  27.1 2.9 %collective-permute-start.1 = (bf16[512,128]{1,0:T(8,128)(2,1)S(1)}, bf16[512,128]{1,0:T(8,128)(2,1)S(1)}, u32[]{:S(2)}, u32[]{:S(2)}) collective-permute-start(bf16[512,128]{1,0:T(8,128)(2,1)S(1)} %shard_map.87.keys0), channel_id=1, source_target_pairs={{0,16},{1,241},{16,32},{17,1},{32,48},{33,17},{48,64},{49,33},{64,... | collective-permute-start | bytes 393224 | tf_op jit(solution)/shard_map/ppermute | solution.py:201
  30.1 0.0 all-to-all-done
  30.1 0.1 shard_map.86
  30.2 27.2 %all-gather = bf16[2112,128]{1,0:T(8,128)(2,1)S(1)} all-gather(bf16[528,128]{1,0:T(8,128)(2,1)S(1)} %shard_map.86), channel_id=2, replica_groups=mesh['x_lo'=2,'z_hi'=4,'z_lo'=4,'x_hi'=2,'y'=4,'core'=2] {'z_hi'}, dimensions={0}, use_global_device_ids=true | all-gather | bytes 675840 | tf_op jit(solution)/shard_map/all_gather | solution.py:229
  57.4 0.0 collective-permute-done.3.keys3
  57.4 0.0 collective-permute-done.2.keys2
  57.4 0.0 collective-permute-done.1.keys1
  57.5 3.4 %shard_map.88 = (bf16[8,128,128]{2,1,0:T(8,128)(2,1)}, f32[4,256,128]{2,1,0:T(8,128)S(1)}, bf16[4,256,128]{2,1,0:T(8,128)(2,1)S(1)}) custom-call(bf16[4,528,128]{2,1,0:T(8,128)(2,1)S(1)} %bitcast.7, bf16[512,128]{1,0:T(8,128)(2,1)S(1)} %shard_map.87.keys0, bf16[512,128]{1,0:T(8,128)(2,1)S(1)} %collective-permute-done.1.keys1, ...), custom_call_target="tpu_custom_call" | custom-call | tf_op jit(solution)/shard_map/pallas_call | solution.py:39
  60.8 2.8 %collective-permute-start.4 = (bf16[4,256,128]{2,1,0:T(8,128)(2,1)S(1)}, bf16[4,256,128]{2,1,0:T(8,128)(2,1)S(1)}, u32[]{:S(2)}, u32[]{:S(2)}) collective-permute-start(bf16[4,256,128]{2,1,0:T(8,128)(2,1)S(1)} %get-tuple-element.16), channel_id=1, source_target_pairs={{0,256},{256,0},{1,257},{257,1},{2,258},{258,2},{3,259},{259,3},{4... | collective-permute-start | bytes 786440 | tf_op jit(solution)/shard_map/ppermute | solution.py:205
  63.6 8.2 %all-to-all-start.1 = ((bf16[8,128,128]{2,1,0:T(8,128)(2,1)}), bf16[8,128,128]{2,1,0:T(8,128)(2,1)S(1)}, u32[]{:S(2)}, u32[]{:S(2)}) async-start(bf16[8,128,128]{2,1,0:T(8,128)(2,1)} %get-tuple-element.14), calls=%async_computation.1 | async-start | bytes 524288 | tf_op jit(solution)/shard_map/all_to_all | solution.py:239
  71.8 0.0 collective-permute-done.4.got
  71.8 0.1 shard_map.89
  71.8 3.7 %collective-permute-start.5 = (bf16[256,256]{1,0:T(8,128)(2,1)S(1)}, bf16[256,256]{1,0:T(8,128)(2,1)S(1)}, u32[]{:S(2)}, u32[]{:S(2)}) collective-permute-start(bf16[256,256]{1,0:T(8,128)(2,1)S(1)} %get-tuple-element.18), channel_id=1, source_target_pairs={{0,240},{1,17},{16,0},{17,33},{32,16},{33,49},{48,32},{49,65},{64,... | collective-permute-start | bytes 393224 | tf_op jit(solution)/shard_map/ppermute | solution.py:201
  75.6 2.1 %collective-permute-start.6 = (bf16[256,256]{1,0:T(8,128)(2,1)S(1)}, bf16[256,256]{1,0:T(8,128)(2,1)S(1)}, u32[]{:S(2)}, u32[]{:S(2)}) collective-permute-start(bf16[256,256]{1,0:T(8,128)(2,1)S(1)} %get-tuple-element.19), channel_id=1, source_target_pairs={{0,16},{1,241},{16,32},{17,1},{32,48},{33,17},{48,64},{49,33},{64,... | collective-permute-start | bytes 393224 | tf_op jit(solution)/shard_map/ppermute | solution.py:201
  77.7 1.9 %collective-permute-start.7 = (bf16[256,256]{1,0:T(8,128)(2,1)S(1)}, bf16[256,256]{1,0:T(8,128)(2,1)S(1)}, u32[]{:S(2)}, u32[]{:S(2)}) collective-permute-start(bf16[256,256]{1,0:T(8,128)(2,1)S(1)} %get-tuple-element.20), channel_id=1, source_target_pairs={{0,32},{1,225},{16,48},{17,241},{32,64},{33,1},{48,80},{49,17},{64... | collective-permute-start | bytes 393224 | tf_op jit(solution)/shard_map/ppermute | solution.py:201
  79.6 2.1 %collective-permute-done.5.got1 = bf16[256,256]{1,0:T(8,128)(2,1)S(1)} collective-permute-done((bf16[256,256]{1,0:T(8,128)(2,1)S(1)}, bf16[256,256]{1,0:T(8,128)(2,1)S(1)}, u32[]{:S(2)}, u32[]{:S(2)}) %collective-permute-start.5) | collective-permute-done | bytes 131104 | tf_op jit(solution)/shard_map/ppermute | solution.py:201
  81.7 5.3 %collective-permute-done.6.got2 = bf16[256,256]{1,0:T(8,128)(2,1)S(1)} collective-permute-done((bf16[256,256]{1,0:T(8,128)(2,1)S(1)}, bf16[256,256]{1,0:T(8,128)(2,1)S(1)}, u32[]{:S(2)}, u32[]{:S(2)}) %collective-permute-start.6) | collective-permute-done | bytes 131104 | tf_op jit(solution)/shard_map/ppermute | solution.py:201
  87.1 2.6 %collective-permute-done.7.got3 = bf16[256,256]{1,0:T(8,128)(2,1)S(1)} collective-permute-done((bf16[256,256]{1,0:T(8,128)(2,1)S(1)}, bf16[256,256]{1,0:T(8,128)(2,1)S(1)}, u32[]{:S(2)}, u32[]{:S(2)}) %collective-permute-start.7) | collective-permute-done | bytes 131104 | tf_op jit(solution)/shard_map/ppermute | solution.py:201
  89.7 0.0 all-to-all-done.1.parts_q
  89.7 0.8 shard_map.90
  (1 shorter events, 0.0 us)
Async XLA Ops:
  1.6 11.4 %collective-permute-start = (bf16[528,128]{1,0:T(8,128)(2,1)S(1)}, bf16[528,128]{1,0:T(8,128)(2,1)S(1)}, u32[]{:S(2)}, u32[]{:S(2)}) collective-permute-start(bf16[528,128]{1,0:T(8,128)(2,1)S(1)} %get-tuple-element.13), channel_id=1, source_target_pairs={{0,256},{256,0},{1,257},{257,1},{2,258},{258,2},{3,259},{259,3},{4... | collective-permute-start | bytes 405512 | tf_op jit(solution)/shard_map/ppermute | solution.py:205
  4.4 25.7 %all-to-all-start = ((bf16[8,32,128]{2,0,1:T(8,128)(2,1)}), bf16[8,32,128]{2,0,1:T(8,128)(2,1)S(1)}, u32[]{:S(2)}, u32[]{:S(2)}) async-start(bf16[8,32,128]{2,0,1:T(8,128)(2,1)} %bitcast.2), calls=%async_computation | async-start | bytes 131072 | tf_op jit(solution)/shard_map/all_to_all | solution.py:211
  13.1 44.4 %collective-permute-start.3 = (bf16[512,128]{1,0:T(8,128)(2,1)S(1)}, bf16[512,128]{1,0:T(8,128)(2,1)S(1)}, u32[]{:S(2)}, u32[]{:S(2)}) collective-permute-start(bf16[512,128]{1,0:T(8,128)(2,1)S(1)} %shard_map.87.keys0), channel_id=1, source_target_pairs={{0,224},{1,33},{16,240},{17,49},{32,0},{33,65},{48,16},{49,81},{64... | collective-permute-start | bytes 393224 | tf_op jit(solution)/shard_map/ppermute | solution.py:201
  24.2 33.2 %collective-permute-start.2 = (bf16[512,128]{1,0:T(8,128)(2,1)S(1)}, bf16[512,128]{1,0:T(8,128)(2,1)S(1)}, u32[]{:S(2)}, u32[]{:S(2)}) collective-permute-start(bf16[512,128]{1,0:T(8,128)(2,1)S(1)} %shard_map.87.keys0), channel_id=1, source_target_pairs={{0,240},{1,17},{16,0},{17,33},{32,16},{33,49},{48,32},{49,65},{64,... | collective-permute-start | bytes 393224 | tf_op jit(solution)/shard_map/ppermute | solution.py:201
  27.1 30.3 %collective-permute-start.1 = (bf16[512,128]{1,0:T(8,128)(2,1)S(1)}, bf16[512,128]{1,0:T(8,128)(2,1)S(1)}, u32[]{:S(2)}, u32[]{:S(2)}) collective-permute-start(bf16[512,128]{1,0:T(8,128)(2,1)S(1)} %shard_map.87.keys0), channel_id=1, source_target_pairs={{0,16},{1,241},{16,32},{17,1},{32,48},{33,17},{48,64},{49,33},{64,... | collective-permute-start | bytes 393224 | tf_op jit(solution)/shard_map/ppermute | solution.py:201
  60.8 11.0 %collective-permute-start.4 = (bf16[4,256,128]{2,1,0:T(8,128)(2,1)S(1)}, bf16[4,256,128]{2,1,0:T(8,128)(2,1)S(1)}, u32[]{:S(2)}, u32[]{:S(2)}) collective-permute-start(bf16[4,256,128]{2,1,0:T(8,128)(2,1)S(1)} %get-tuple-element.16), channel_id=1, source_target_pairs={{0,256},{256,0},{1,257},{257,1},{2,258},{258,2},{3,259},{259,3},{4... | collective-permute-start | bytes 786440 | tf_op jit(solution)/shard_map/ppermute | solution.py:205
  63.6 26.1 %all-to-all-start.1 = ((bf16[8,128,128]{2,1,0:T(8,128)(2,1)}), bf16[8,128,128]{2,1,0:T(8,128)(2,1)S(1)}, u32[]{:S(2)}, u32[]{:S(2)}) async-start(bf16[8,128,128]{2,1,0:T(8,128)(2,1)} %get-tuple-element.14), calls=%async_computation.1 | async-start | bytes 524288 | tf_op jit(solution)/shard_map/all_to_all | solution.py:239
  71.8 9.9 %collective-permute-start.5 = (bf16[256,256]{1,0:T(8,128)(2,1)S(1)}, bf16[256,256]{1,0:T(8,128)(2,1)S(1)}, u32[]{:S(2)}, u32[]{:S(2)}) collective-permute-start(bf16[256,256]{1,0:T(8,128)(2,1)S(1)} %get-tuple-element.18), channel_id=1, source_target_pairs={{0,240},{1,17},{16,0},{17,33},{32,16},{33,49},{48,32},{49,65},{64,... | collective-permute-start | bytes 393224 | tf_op jit(solution)/shard_map/ppermute | solution.py:201
  75.6 11.5 %collective-permute-start.6 = (bf16[256,256]{1,0:T(8,128)(2,1)S(1)}, bf16[256,256]{1,0:T(8,128)(2,1)S(1)}, u32[]{:S(2)}, u32[]{:S(2)}) collective-permute-start(bf16[256,256]{1,0:T(8,128)(2,1)S(1)} %get-tuple-element.19), channel_id=1, source_target_pairs={{0,16},{1,241},{16,32},{17,1},{32,48},{33,17},{48,64},{49,33},{64,... | collective-permute-start | bytes 393224 | tf_op jit(solution)/shard_map/ppermute | solution.py:201
  77.7 12.0 %collective-permute-start.7 = (bf16[256,256]{1,0:T(8,128)(2,1)S(1)}, bf16[256,256]{1,0:T(8,128)(2,1)S(1)}, u32[]{:S(2)}, u32[]{:S(2)}) collective-permute-start(bf16[256,256]{1,0:T(8,128)(2,1)S(1)} %get-tuple-element.20), channel_id=1, source_target_pairs={{0,32},{1,225},{16,48},{17,241},{32,64},{33,1},{48,80},{49,17},{64... | collective-permute-start | bytes 393224 | tf_op jit(solution)/shard_map/ppermute | solution.py:201
